TPU v7x, 32 devices: a whole 2x2x4 slice. The times are simulated.
32 devices in a mesh: seq: 16 (over z, y, x), head: 2 (over core).
Axes of the slice: x: 2, y: 2, z: 4, core: 2. Of those that a mesh axis runs over, the one named last changes fastest.
Arguments:
- tokens: bfloat16 [4096, 2048], P('seq'), may hold values from -6 to 6
- cotangent: bfloat16 [4096, 2048], P('seq'), may hold values from -6 to 6
- lengths: int32 [13], replicated, may hold values from 1 to 3898, as said below
- attn_gain: bfloat16 [2048], P('seq'), may hold values from 0.5 to 1.5
- ffn_gain: bfloat16 [2048], P('seq'), may hold values from 0.5 to 1.5
- mixer_in: bfloat16 [4, 2048, 2048], P(None, 'seq', 'head'), may hold values from -0.125 to 0.125
- decay_down: bfloat16 [2048, 16], P('seq'), may hold values from -0.125 to 0.125
- decay_up: bfloat16 [16, 2048], P(None, 'head'), may hold values from -1.5 to 1.5
- decay_bias: float32 [2048], P('head'), may hold values from -2 to 12
- head_gain: float32 [512], replicated, may hold values from 0.5 to 1.5
- mixer_out: bfloat16 [2048, 2048], P('head', 'seq'), may hold values from -0.25 to 0.25
- ffn_in: bfloat16 [2, 2048, 5632], P(None, 'seq', 'head'), may hold values from -0.125 to 0.125
- ffn_out: bfloat16 [5632, 2048], P('head', 'seq'), may hold values from -0.15625 to 0.15625
Outputs:
- out: bfloat16 [4096, 2048], P('seq')
- tokens_grad: bfloat16 [4096, 2048], P('seq')
- attn_gain_grad: float32 [2048], P('seq')
- ffn_gain_grad: float32 [2048], P('seq')
- mixer_in_grad: float32 [4, 2048, 2048], P(None, 'seq', 'head')
- decay_down_grad: float32 [2048, 16], P('seq')
- decay_up_grad: float32 [16, 2048], P(None, 'head')
- decay_bias_grad: float32 [2048], P('head')
- head_gain_grad: float32 [512], replicated
- mixer_out_grad: float32 [2048, 2048], P('head', 'seq')
- ffn_in_grad: float32 [2, 2048, 5632], P(None, 'seq', 'head')
- ffn_out_grad: float32 [5632, 2048], P('head', 'seq')
Inputs may be any that keep to these rules, and one draw needn't show every extreme that they name: The lengths sum to 4096; item 6, counting from 0, is the longest, starts within the first 256 tokens and ends within the last 256 tokens; every other item has at most 32 tokens.
All inputs are finite; a program needn't handle non-finite values.
Results may differ from a plain program's by a relative error of at most 0.017.
The roundings to bfloat16 on the way count: a program that leaves them out, or rounds other values in their place, can miss the bound.
Values may be sent and summed in bfloat16 or wider, within the bound.
A program may use at most 448 MiB of HBM per device.

v0:
```python
import jax
import jax.numpy as jnp
from jax import lax
from jax.sharding import PartitionSpec as P

HD = 512
GROUP = 64


EPSILON = 1e-06
HEAD_FLOOR = 1.0
MAXIMUM_PRECISION = lax.Precision.HIGHEST


def entering(shard, axis, combine, identity):
    devices, index = (lax.axis_size(axis), lax.axis_index(axis))
    everything = jax.tree.map(lambda part: lax.all_gather(part, axis), shard)
    start = jax.tree.map(
        lambda part, zero: jnp.broadcast_to(jnp.asarray(zero, part.dtype), part.shape),
        shard,
        identity,
    )

    def entering_turn(k, before):
        reached = k < index
        new = combine(before, jax.tree.map(lambda part: part[k], everything))
        return jax.tree.map(lambda a, b: jnp.where(reached, a, b), new, before)

    return lax.fori_loop(0, devices, entering_turn, start)


def prefix(shard, axis, combine, identity):
    devices, index = (lax.axis_size(axis), lax.axis_index(axis))
    everything = jax.tree.map(
        lambda part, kind: lax.all_gather(part.astype(kind), axis),
        shard,
        jax.tree.map(lambda a: jnp.bfloat16 if a.dtype == jnp.float32 else a.dtype, shard),
    )
    start = jax.tree.map(
        lambda part, zero: jnp.broadcast_to(jnp.asarray(zero, part.dtype), part.shape),
        shard,
        identity,
    )

    def prefix_turn(k, before):
        at = devices - 1 - k
        reached = at > index
        new = combine(
            before, jax.tree.map(lambda part, own: part[at].astype(own.dtype), everything, shard)
        )
        return jax.tree.map(lambda a, b: jnp.where(reached, a, b), new, before)

    return lax.fori_loop(0, devices, prefix_turn, start)


def low_dot(left_matrix, right_matrix):
    return jnp.dot(left_matrix, right_matrix, preferred_element_type=jnp.float32)


def contract_rows(left_matrix, right_matrix):
    return lax.dot_general(
        left_matrix, right_matrix, (((0,), (0,)), ((), ())), preferred_element_type=jnp.float32
    )


def contract_last(left_matrix, right_matrix):
    return lax.dot_general(
        left_matrix, right_matrix, (((1,), (1,)), ((), ())), preferred_element_type=jnp.float32
    )


def combine_states(earlier, later):
    return (earlier[0] * later[0], later[0][..., None] * earlier[1] + later[1])


def group_masks(resets):
    counted = jnp.cumsum(resets, axis=1)
    position = jnp.arange(resets.shape[1])
    causal = position[:, None] >= position[None, :]
    pair_mask = (causal[None] & (counted[:, :, None] == counted[:, None, :])).astype(jnp.float32)
    state_visible_mask = (counted == 0).astype(jnp.float32)
    keeps_state = (counted[:, -1] == 0).astype(jnp.float32)
    in_last = (counted == counted[:, -1:]).astype(jnp.float32)
    return (pair_mask, state_visible_mask, keeps_state, in_last)


def group_forward(state_carried_in, group_items):
    (
        queries,
        key_rows,
        value_rows,
        cumulated,
        pair_mask,
        state_visible_mask,
        keeps_state,
        in_last,
    ) = group_items
    growth = jnp.exp(cumulated)
    decayed_query_rows = queries * growth
    key_decayed = key_rows * jnp.exp(-cumulated)
    last_sum = cumulated[-1]
    carried_key_rows = key_rows * jnp.exp(last_sum[None] - cumulated) * in_last[:, None, None]
    scores = (
        jnp.einsum("ihk,jhk->hij", decayed_query_rows, key_decayed, precision=MAXIMUM_PRECISION)
        * pair_mask[None]
    )
    layer_output = jnp.einsum("hij,jhv->ihv", scores, value_rows, precision=MAXIMUM_PRECISION)
    layer_output = layer_output + state_visible_mask[:, None, None] * jnp.einsum(
        "cwb,wbs->cws", decayed_query_rows, state_carried_in, precision=MAXIMUM_PRECISION
    )
    updated_state = keeps_state * jnp.exp(last_sum)[:, :, None] * state_carried_in
    updated_state = updated_state + jnp.einsum(
        "nfe,nfu->feu", carried_key_rows, value_rows, precision=MAXIMUM_PRECISION
    )
    return (updated_state, (layer_output, state_carried_in))


def group_backward(state_gradient, group_items):
    (
        queries,
        key_rows,
        value_rows,
        cumulated,
        pair_mask,
        state_visible_mask,
        keeps_state,
        in_last,
        state_carried_in,
        output_gradient,
    ) = group_items
    growth = jnp.exp(cumulated)
    shrink = jnp.exp(-cumulated)
    decayed_query_rows = queries * growth
    key_decayed = key_rows * shrink
    last_sum = cumulated[-1]
    decay_last = jnp.exp(last_sum[None] - cumulated) * in_last[:, None, None]
    carried_key_rows = key_rows * decay_last
    scores = (
        jnp.einsum("ihk,jhk->hij", decayed_query_rows, key_decayed, precision=MAXIMUM_PRECISION)
        * pair_mask[None]
    )
    grad_scores = (
        jnp.einsum("ihv,jhv->hij", output_gradient, value_rows, precision=MAXIMUM_PRECISION)
        * pair_mask[None]
    )
    grad_values = jnp.einsum("hij,ihv->jhv", scores, output_gradient, precision=MAXIMUM_PRECISION)
    grad_values = grad_values + jnp.einsum(
        "euf,ufw->euw", carried_key_rows, state_gradient, precision=MAXIMUM_PRECISION
    )
    grad_qdec = jnp.einsum("hij,jhk->ihk", grad_scores, key_decayed, precision=MAXIMUM_PRECISION)
    grad_qdec = grad_qdec + state_visible_mask[:, None, None] * jnp.einsum(
        "zas,ays->zay", output_gradient, state_carried_in, precision=MAXIMUM_PRECISION
    )
    grad_kdec = jnp.einsum(
        "hij,ihk->jhk", grad_scores, decayed_query_rows, precision=MAXIMUM_PRECISION
    )
    gradient_key_carried = jnp.einsum(
        "nxo,xwo->nxw", value_rows, state_gradient, precision=MAXIMUM_PRECISION
    )
    carry_part = keeps_state * jnp.exp(last_sum)
    grad_prev = carry_part[:, :, None] * state_gradient
    grad_prev = grad_prev + jnp.einsum(
        "ngd,ngt->gdt",
        decayed_query_rows * state_visible_mask[:, None, None],
        output_gradient,
        precision=MAXIMUM_PRECISION,
    )
    grad_queries = grad_qdec * growth
    grad_keys = grad_kdec * shrink + gradient_key_carried * decay_last
    grad_cum = (
        grad_qdec * decayed_query_rows
        - grad_kdec * key_decayed
        - gradient_key_carried * carried_key_rows
    )
    last_extra = jnp.sum(gradient_key_carried * carried_key_rows, axis=0) + carry_part * jnp.sum(
        state_carried_in * state_gradient, axis=-1
    )
    grad_cum = grad_cum.at[-1].add(last_extra)
    return (grad_prev, (grad_queries, grad_keys, grad_values, grad_cum))


def shards(
    tokens,
    cotangent,
    lengths,
    attn_gain,
    ffn_gain,
    mixer_in,
    decay_down,
    decay_up,
    decay_bias,
    head_gain,
    mixer_out,
    ffn_in,
    ffn_out,
):
    gain_one, gain_two, weights_in, rank_down, weights_out, ffn_pair, ffn_down = (
        lax.all_gather(attn_gain, "seq", axis=0, tiled=True),
        lax.all_gather(ffn_gain, "seq", axis=0, tiled=True),
        lax.all_gather(mixer_in, "seq", axis=1, tiled=True),
        lax.all_gather(decay_down, "seq", axis=0, tiled=True),
        lax.all_gather(mixer_out, "seq", axis=1, tiled=True),
        lax.all_gather(ffn_in, "seq", axis=1, tiled=True),
        lax.all_gather(ffn_out, "seq", axis=1, tiled=True),
    )
    tok_rows = tokens.shape[0]
    local_heads = weights_in.shape[2] // HD
    groups_dev = tok_rows // GROUP
    start_row = lax.axis_index("seq") * tok_rows
    item_starts = jnp.cumsum(lengths) - lengths
    position = start_row + jnp.arange(tok_rows, dtype=jnp.int32)
    resets = jnp.any(position[:, None] == item_starts[None, :], axis=1).astype(jnp.int32)
    pair_mask, state_visible_mask, keeps_state, in_last = group_masks(
        resets.reshape(groups_dev, GROUP)
    )
    device_count = jnp.cumsum(resets)
    open_prefix = (device_count == 0).astype(jnp.float32)
    open_suffix = (device_count == device_count[-1]).astype(jnp.float32)
    open_device = (device_count[-1] == 0).astype(jnp.float32)
    inputs = tokens.astype(jnp.float32)
    scale_one = lax.rsqrt(jnp.mean(inputs * inputs, -1, keepdims=True) + EPSILON)
    normed_one = inputs * scale_one
    hidden_one = (normed_one * gain_one.astype(jnp.float32)).astype(jnp.bfloat16)
    projected = jnp.einsum(
        "td,jde->jte", hidden_one, weights_in, preferred_element_type=jnp.float32
    )
    blocks = projected.reshape(4, groups_dev, GROUP, local_heads, HD)
    queries = blocks[0] * HD ** (-0.5)
    key_rows = blocks[1]
    value_rows = blocks[2]
    out_gate = projected[3].reshape(tok_rows, local_heads, HD)
    low_rank = low_dot(hidden_one, rank_down).astype(jnp.bfloat16)
    gate_input = low_dot(low_rank, decay_up) + decay_bias
    log_gates = (jax.nn.log_sigmoid(gate_input) / 16.0).reshape(groups_dev, GROUP, local_heads, HD)
    lower_ones = (jnp.arange(GROUP)[:, None] >= jnp.arange(GROUP)[None, :]).astype(jnp.float32)
    cumulated = jnp.einsum("ij,cjhk->cihk", lower_ones, log_gates, precision=MAXIMUM_PRECISION)
    group_sums = cumulated[:, -1]
    group_starts = jnp.cumsum(group_sums, axis=0) - group_sums
    device_sum = group_starts[-1] + group_sums[-1]
    flat_running = (cumulated + group_starts[:, None]).reshape(tok_rows, local_heads, HD)
    flattened_values = value_rows.reshape(tok_rows, local_heads, HD)
    keys_carried_over = (
        key_rows.reshape(tok_rows, local_heads, HD)
        * jnp.exp(device_sum[None] - flat_running)
        * open_suffix[:, None, None]
    )
    segment_local_state = jnp.einsum(
        "dzo,dzu->zou", keys_carried_over, flattened_values, precision=MAXIMUM_PRECISION
    )
    device_decay = open_device * jnp.exp(device_sum)
    identity = (jnp.ones_like(device_decay), jnp.zeros_like(segment_local_state))
    incoming = entering((device_decay, segment_local_state), "seq", combine_states, identity)[1]
    reachable_rows = (
        queries.reshape(tok_rows, local_heads, HD)
        * jnp.exp(flat_running)
        * open_prefix[:, None, None]
    )
    group_items = (
        queries,
        key_rows,
        value_rows,
        cumulated,
        pair_mask,
        state_visible_mask,
        keeps_state,
        in_last,
    )
    final_state, (outputs, group_states) = lax.scan(group_forward, incoming, group_items)
    mixed = outputs.reshape(tok_rows, local_heads, HD)
    head_scale = lax.rsqrt(jnp.mean(mixed * mixed, -1, keepdims=True) + HEAD_FLOOR)
    head_normed = mixed * head_scale
    normed_heads = head_normed * head_gain
    gate_sig = jax.nn.sigmoid(out_gate)
    gate_silu = out_gate * gate_sig
    gated_rows = (normed_heads * gate_silu).astype(jnp.bfloat16).reshape(tok_rows, -1)
    branch = lax.psum(low_dot(gated_rows, weights_out), "head")
    middle = inputs + branch
    scale_two = lax.rsqrt(jnp.mean(middle * middle, -1, keepdims=True) + EPSILON)
    normed_two = middle * scale_two
    hidden_two = (normed_two * gain_two.astype(jnp.float32)).astype(jnp.bfloat16)
    up_pair = jnp.einsum("td,jdf->jtf", hidden_two, ffn_pair, preferred_element_type=jnp.float32)
    ffn_sig = jax.nn.sigmoid(up_pair[0])
    ffn_silu = up_pair[0] * ffn_sig
    activated = (ffn_silu * up_pair[1]).astype(jnp.bfloat16)
    ffn_branch = lax.psum(low_dot(activated, ffn_down).astype(jnp.bfloat16), "head").astype(
        jnp.float32
    )
    result = (middle + ffn_branch).astype(jnp.bfloat16)
    held_shards = lax.optimization_barrier(
        (attn_gain, ffn_gain, mixer_in, decay_down, mixer_out, ffn_in, ffn_out, result)
    )
    gain_one, gain_two, weights_in, rank_down, weights_out, ffn_pair, ffn_down = (
        lax.all_gather(held_shards[0], "seq", axis=0, tiled=True),
        lax.all_gather(held_shards[1], "seq", axis=0, tiled=True),
        lax.all_gather(held_shards[2], "seq", axis=1, tiled=True),
        lax.all_gather(held_shards[3], "seq", axis=0, tiled=True),
        lax.all_gather(held_shards[4], "seq", axis=1, tiled=True),
        lax.all_gather(held_shards[5], "seq", axis=1, tiled=True),
        lax.all_gather(held_shards[6], "seq", axis=1, tiled=True),
    )
    grad_result = cotangent.astype(jnp.float32)
    grad_down = contract_rows(activated, cotangent)
    grad_act = contract_last(cotangent, ffn_down)
    grad_gate = grad_act * up_pair[1] * ffn_sig * (1.0 + up_pair[0] * (1.0 - ffn_sig))
    grad_upper = grad_act * ffn_silu
    grad_pair = jnp.stack([grad_gate, grad_upper]).astype(jnp.bfloat16)
    grad_ffn_in = jnp.einsum(
        "td,jtf->jdf", hidden_two, grad_pair, preferred_element_type=jnp.float32
    )
    grad_hidden_two = lax.psum(
        jnp.einsum("jtf,jdf->td", grad_pair, ffn_pair, preferred_element_type=jnp.float32).astype(
            jnp.bfloat16
        ),
        "head",
    ).astype(jnp.float32)
    grad_gain_two = jnp.sum(grad_hidden_two * normed_two, axis=0)
    scaled_two = grad_hidden_two * gain_two.astype(jnp.float32)
    grad_middle = grad_result + scale_two * (
        scaled_two - normed_two * jnp.mean(scaled_two * normed_two, -1, keepdims=True)
    )
    grad_branch = grad_middle.astype(jnp.bfloat16)
    grad_out_proj = contract_rows(gated_rows, grad_branch)
    grad_gated = contract_last(grad_branch, weights_out).reshape(tok_rows, local_heads, HD)
    grad_normed_heads = grad_gated * gate_silu
    grad_out_gate = grad_gated * normed_heads * gate_sig * (1.0 + out_gate * (1.0 - gate_sig))
    grad_head_gain = jnp.sum(grad_normed_heads * head_normed, axis=(0, 1))
    scaled_heads = grad_normed_heads * head_gain
    gradient_mixed_rows = head_scale * (
        scaled_heads - head_normed * jnp.mean(scaled_heads * head_normed, -1, keepdims=True)
    )
    outgoing_decay = jnp.einsum(
        "dzo,dzu->zou", reachable_rows, gradient_mixed_rows, precision=MAXIMUM_PRECISION
    )
    grad_final = prefix((device_decay, outgoing_decay), "seq", combine_states, identity)[1]
    back_items = group_items + (
        group_states,
        gradient_mixed_rows.reshape(groups_dev, GROUP, local_heads, HD),
    )
    grad_first, (grad_queries, grad_keys, grad_values, grad_cum) = lax.scan(
        group_backward, grad_final, back_items, reverse=True
    )
    grad_logs = jnp.einsum(
        "ji,cjhk->cihk", lower_ones, grad_cum, precision=MAXIMUM_PRECISION
    ).reshape(tok_rows, -1)
    grad_gate_input = grad_logs * jax.nn.sigmoid(-gate_input) / 16.0
    grad_bias = jnp.sum(grad_gate_input, axis=0)
    grad_input_low = grad_gate_input.astype(jnp.bfloat16)
    grad_decay_up = contract_rows(low_rank, grad_input_low)
    grad_rank_part = contract_last(grad_input_low, decay_up)
    grad_proj = jnp.stack(
        [
            grad_queries.reshape(tok_rows, -1) * HD ** (-0.5),
            grad_keys.reshape(tok_rows, -1),
            grad_values.reshape(tok_rows, -1),
            grad_out_gate.reshape(tok_rows, -1),
        ]
    ).astype(jnp.bfloat16)
    grad_mixer_in = jnp.einsum(
        "td,jte->jde", hidden_one, grad_proj, preferred_element_type=jnp.float32
    )
    hidden_part = jnp.einsum(
        "jte,jde->td", grad_proj, weights_in, preferred_element_type=jnp.float32
    )
    grad_hidden_one, grad_rank, grad_head_total = (
        lax.psum(hidden_part.astype(jnp.bfloat16), "head").astype(jnp.float32),
        lax.psum(grad_rank_part.astype(jnp.bfloat16), "head").astype(jnp.float32),
        lax.psum(grad_head_gain.astype(jnp.bfloat16), "head").astype(jnp.float32),
    )
    grad_rank_low = grad_rank.astype(jnp.bfloat16)
    grad_rank_down = contract_rows(hidden_one, grad_rank_low)
    grad_hidden_one = grad_hidden_one + contract_last(grad_rank_low, rank_down)
    grad_gain_one = jnp.sum(grad_hidden_one * normed_one, axis=0)
    scaled_one = grad_hidden_one * gain_one.astype(jnp.float32)
    grad_inputs = grad_middle + scale_one * (
        scaled_one - normed_one * jnp.mean(scaled_one * normed_one, -1, keepdims=True)
    )
    home_grads = (
        lax.psum_scatter(grad_gain_one, "seq", scatter_dimension=0, tiled=True),
        lax.psum_scatter(grad_gain_two, "seq", scatter_dimension=0, tiled=True),
        lax.psum_scatter(grad_mixer_in, "seq", scatter_dimension=1, tiled=True),
        lax.psum_scatter(grad_rank_down, "seq", scatter_dimension=0, tiled=True),
        lax.psum_scatter(grad_out_proj, "seq", scatter_dimension=1, tiled=True),
        lax.psum_scatter(grad_ffn_in, "seq", scatter_dimension=1, tiled=True),
        lax.psum_scatter(grad_down, "seq", scatter_dimension=1, tiled=True),
    )
    (
        gain_one_home,
        gain_two_home,
        mixer_in_home,
        rank_down_home,
        out_proj_home,
        ffn_in_home,
        down_home,
    ) = home_grads
    small_sums = lax.psum((grad_decay_up, grad_bias, grad_head_total), "seq")
    return (
        result,
        grad_inputs.astype(jnp.bfloat16),
        gain_one_home,
        gain_two_home,
        mixer_in_home,
        rank_down_home,
        small_sums[0],
        small_sums[1],
        small_sums[2],
        out_proj_home,
        ffn_in_home,
        down_home,
    )


def solution(mesh):
    in_specs = (
        P("seq", None),
        P("seq", None),
        P(),
        P("seq"),
        P("seq"),
        P(None, "seq", "head"),
        P("seq", None),
        P(None, "head"),
        P("head"),
        P(),
        P("head", "seq"),
        P(None, "seq", "head"),
        P("head", "seq"),
    )
    out_specs = (
        P("seq", None),
        P("seq", None),
        P("seq"),
        P("seq"),
        P(None, "seq", "head"),
        P("seq", None),
        P(None, "head"),
        P("head"),
        P(),
        P("head", "seq"),
        P(None, "seq", "head"),
        P("head", "seq"),
    )
    return jax.shard_map(shards, mesh=mesh, in_specs=in_specs, out_specs=out_specs, check_vma=False)
```

profile of v0, /device:TPU:0, one launch (start us, length us, event | category | flops | bytes accessed | tf_op | source)
XLA Modules:
  0.0 4652.5 jit_solution(4195214902650090359)
XLA Ops:
  8.0 42.8 all-gather.2
  54.3 37.5 all_gather.63
  100.1 106.0 %all-gather.17.cloned.1.call-done = bf16[4,2048,1024]{2,1,0:T(8,128)(2,1)} async-done(((bf16[4,128,1024]{2,1,0:T(8,128)(2,1)}), bf16[4,2048,1024]{2,1,0:T(8,128)(2,1)}) %all-gather.17.cloned.1.call-update) | async-done | bytes 16777232 | tf_op jit(solution)/shard_map/all_gather | solution.py:200
  231.4 39.6 all_gather.64
  285.4 294.0 %all-gather.33.cloned.1.call-done = f32[32,512,512]{2,1,0:T(8,128)} async-done(((f32[2,512,512]{2,1,0:T(8,128)}), f32[32,512,512]{2,1,0:T(8,128)}) %all-gather.33.cloned.1.call-update) | async-done | bytes 33554448 | tf_op jit(solution)/shard_map/all_gather | solution.py:17
  579.4 35.5 while.69
  616.0 45.5 while.67
  675.6 37.7 all-gather.3
  715.6 233.9 %all-gather.21.cloned.1.call-done = bf16[2,2048,2816]{2,1,0:T(8,128)(2,1)} async-done(((bf16[2,128,2816]{2,1,0:T(8,128)(2,1)}), bf16[2,2048,2816]{2,1,0:T(8,128)(2,1)}) %all-gather.21.cloned.1.call-update) | async-done | bytes 23068688 | tf_op jit(solution)/shard_map/all_gather | solution.py:203
  964.9 168.3 %all-gather.23.cloned.1.call-done = bf16[2816,2048]{1,0:T(8,128)(2,1)} async-done(((bf16[2816,128]{1,0:T(8,128)(2,1)}), bf16[2816,2048]{1,0:T(8,128)(2,1)}) %all-gather.23.cloned.1.call-update) | async-done | bytes 11534352 | tf_op jit(solution)/shard_map/all_gather | solution.py:204
  1142.2 17.9 all-reduce.12.cloned.1.call-done
  1163.3 183.2 %all-gather.25.cloned.1.call-done = bf16[2816,2048]{1,0:T(8,128)(2,1)} async-done(((bf16[2816,128]{1,0:T(8,128)(2,1)}), bf16[2816,2048]{1,0:T(8,128)(2,1)}) %all-gather.25.cloned.1.call-update) | async-done | bytes 11534352 | tf_op jit(solution)/shard_map/all_gather | solution.py:299
  1358.3 240.5 %all-gather.27.cloned.1.call-done = bf16[2,2048,2816]{2,1,0:T(8,128)(2,1)} async-done(((bf16[2,128,2816]{2,1,0:T(8,128)(2,1)}), bf16[2,2048,2816]{2,1,0:T(8,128)(2,1)}) %all-gather.27.cloned.1.call-update) | async-done | bytes 23068688 | tf_op jit(solution)/shard_map/all_gather | solution.py:298
  1598.8 12.3 fusion.78
  1613.1 37.8 all-gather.4
  1655.6 67.0 %all-gather.29.cloned.1.call-done = bf16[1024,2048]{1,0:T(8,128)(2,1)} async-done(((bf16[1024,128]{1,0:T(8,128)(2,1)}), bf16[1024,2048]{1,0:T(8,128)(2,1)}) %all-gather.29.cloned.1.call-update) | async-done | bytes 4194320 | tf_op jit(solution)/shard_map/all_gather | solution.py:297
  1740.5 38.7 all_gather.75
  1788.6 139.6 %all-gather.35.cloned.1.call-done = bf16[32,512,512]{2,1,0:T(8,128)(2,1)} async-done(((bf16[2,512,512]{2,1,0:T(8,128)(2,1)}), bf16[32,512,512]{2,1,0:T(8,128)(2,1)}) %all-gather.35.cloned.1.call-update) | async-done | bytes 16777232 | tf_op jit(solution)/shard_map/all_gather | solution.py:35
  1928.2 33.7 while.70
  1964.1 93.0 %while.68 = (s32[]{:T(128)}, f32[2,512,512]{2,1,0:T(8,128)S(1)}, f32[4,64,2,512]{3,1,2,0:T(8,128)}, bf16[4,64,2,512]{3,1,2,0:T(8,128)(2,1)}, bf16[4,64,2,512]{3,...) while((s32[]{:T(128)}, f32[2,512,512]{2,1,0:T(8,128)S(1)}, ...), condition=%wide.region_23.24_spmd, body=%wide.region_20.23_spmd.sunk | while | flops 1865960448 | bytes 38664628 | solution.py:339
  2062.1 58.9 %all-gather.31.cloned.1.call-done = bf16[4,2048,1024]{2,1,0:T(8,128)(2,1)} async-done(((bf16[4,128,1024]{2,1,0:T(8,128)(2,1)}), bf16[4,2048,1024]{2,1,0:T(8,128)(2,1)}) %all-gather.31.cloned.1.call-update) | async-done | bytes 16777232 | tf_op jit(solution)/shard_map/all_gather | solution.py:295
  2132.8 20.4 convolution_bitcast_fusion.5
  2155.1 14.4 convolution_bitcast_fusion.6
  2190.8 38.7 all-gather.5
  2229.6 39.7 all_gather.80
  2283.1 79.6 %all-reduce.2 = (f32[2048]{0:T(1024)S(1)}, f32[2048]{0:T(1024)S(1)}, f32[1024]{0:T(1024)}, f32[512]{0:T(512)}) all-reduce(f32[2048]{0:T(1024)S(1)} %get-tuple-element.870, f32[2048]{0:T(1024)S(1)} %copy-done.45, f32[1024]{0:T(1024)S(1)} %get-tuple-element.956, ...), channel_id=4, replica_groups=mesh['seq'=16,'head'=2] {'seq'}, use_global_device_ids=true, to_apply=%region_28.29.clone | all-reduce | flops 5632 | bytes 44032
  2363.9 732.5 %reduce-scatter.12.cloned.1.call-done = f32[2,128,2816]{1,2,0:T(8,128)} async-done(((f32[2,2048,2816]{1,2,0:T(8,128)}), f32[2,128,2816]{1,2,0:T(8,128)}) %reduce-scatter.12.cloned.1.call-update) | async-done | bytes 2883600 | tf_op jit(solution)/shard_map/reduce_scatter | solution.py:383
  3099.8 687.4 %reduce-scatter.6.cloned.1.call-done = f32[4,128,1024]{1,2,0:T(8,128)} async-done(((f32[4,2048,1024]{1,2,0:T(8,128)}), f32[4,128,1024]{1,2,0:T(8,128)}) %reduce-scatter.6.cloned.1.call-update) | async-done | bytes 2097168 | tf_op jit(solution)/shard_map/reduce_scatter | solution.py:380
  3790.0 478.5 %reduce-scatter.14.cloned.1.call-done = f32[2816,128]{1,0:T(8,128)} async-done(((f32[2816,2048]{1,0:T(8,128)}), f32[2816,128]{1,0:T(8,128)}) %reduce-scatter.14.cloned.1.call-update) | async-done | bytes 1441808 | tf_op jit(solution)/shard_map/reduce_scatter | solution.py:384
  4268.6 187.3 %reduce-scatter.10.cloned.1.call-done = f32[1024,128]{1,0:T(8,128)} async-done(((f32[1024,2048]{1,0:T(8,128)}), f32[1024,128]{1,0:T(8,128)}) %reduce-scatter.10.cloned.1.call-update) | async-done | bytes 524304 | tf_op jit(solution)/shard_map/reduce_scatter | solution.py:382
  4455.9 110.5 %all-reduce.18.cloned.1.call-done = f32[16,1024]{1,0:T(8,128)} async-done(((f32[16,1024]{1,0:T(8,128)}), f32[16,1024]{1,0:T(8,128)}) %all-reduce.18.cloned.1.call-update) | async-done | bytes 65552 | tf_op jit(solution)/shard_map/psum | solution.py:395
  4566.4 77.6 %reduce-scatter.8.cloned.1.call-done = f32[128,16]{0,1:T(8,128)} async-done(((f32[2048,16]{0,1:T(8,128)}), f32[128,16]{0,1:T(8,128)}) %reduce-scatter.8.cloned.1.call-update) | async-done | bytes 8208 | tf_op jit(solution)/shard_map/reduce_scatter | solution.py:381
  (510 shorter events, 410.8 us)
Async XLA Ops:
  7.2 86.7 %copy-start = (bf16[16,1024]{1,0:T(8,128)(2,1)S(1)}, bf16[16,1024]{1,0:T(8,128)(2,1)}, u32[]{:S(2)}) copy-start(bf16[16,1024]{1,0:T(8,128)(2,1)} %param.30) | copy-start | bytes 98308
  7.2 86.2 %copy-start.9 = (bf16[256,2048]{1,0:T(8,128)(2,1)S(1)}, bf16[256,2048]{1,0:T(8,128)(2,1)}, u32[]{:S(2)}) copy-start(bf16[256,2048]{1,0:T(8,128)(2,1)} %param.23) | copy-start | bytes 3145732
  7.2 86.7 %copy-start.54 = (f32[1024]{0:T(1024)S(1)}, f32[1024]{0:T(1024)}, u32[]{:S(2)}) copy-start(f32[1024]{0:T(1024)} %param.31) | copy-start | bytes 12292
  7.2 198.9 %all-gather.17.cloned.1.call-start = ((), (), s32[]{:S(2)}) async-start(), calls=%async_computation.5 | async-start | bytes 17825792 | tf_op jit(solution)/shard_map/all_gather | solution.py:200
  7.9 571.5 %all-gather.33.cloned.1.call-start = ((), (), s32[]{:S(2)}) async-start(), calls=%async_computation.23 | async-start | bytes 35651584 | tf_op jit(solution)/shard_map/all_gather | solution.py:17
  50.9 155.3 %copy-start.43 = (f32[16,1,128]{2,1,0:T(1,128)}, f32[16,1,128]{2,1,0:T(1,128)S(1)}, u32[]{:S(2)}) copy-start(f32[16,1,128]{2,1,0:T(1,128)S(1)} %convert_element_type.198) | copy-start | bytes 24580
  93.4 112.7 %copy-start.48 = (f32[256]{0:T(256)}, f32[256]{0:T(256)S(1)}, u32[]{:S(2)}) copy-start(f32[256]{0:T(256)S(1)} %add_rsqrt_fusion.2) | copy-start | bytes 3076
  230.0 439.5 %all-gather.19.cloned.1.call-start = ((), (), s32[]{:S(2)}) async-start(), calls=%async_computation.6 | async-start | bytes 4456448 | tf_op jit(solution)/shard_map/all_gather | solution.py:202
  230.7 482.6 %all-reduce.10.cloned.1.call-start = ((), (), s32[]{:S(2)}) async-start(), calls=%async_computation.7 | async-start | bytes 4194304 | tf_op jit(solution)/shard_map/psum | solution.py:276
  674.4 275.1 %all-gather.21.cloned.1.call-start = ((), (), s32[]{:S(2)}) async-start(), calls=%async_computation.8 | async-start | bytes 24510464 | tf_op jit(solution)/shard_map/all_gather | solution.py:203
  675.0 458.2 %all-gather.23.cloned.1.call-start = ((), (), s32[]{:S(2)}) async-start(), calls=%async_computation.9 | async-start | bytes 12255232 | tf_op jit(solution)/shard_map/all_gather | solution.py:204
  675.6 484.5 %all-reduce.12.cloned.1.call-start = ((), (), s32[]{:S(2)}) async-start(), calls=%async_computation.10 | async-start | bytes 2097152 | tf_op jit(solution)/shard_map/psum | solution.py:285
  715.6 938.0 %copy-start.1 = (f32[256,2048]{1,0:T(8,128)}, f32[256,2048]{1,0:T(8,128)S(1)}, u32[]{:S(2)}) copy-start(f32[256,2048]{1,0:T(8,128)S(1)} %get-tuple-element.964) | copy-start | bytes 6291460
  1142.1 204.4 %all-gather.25.cloned.1.call-start = ((), (), s32[]{:S(2)}) async-start(), calls=%async_computation.11 | async-start | bytes 12255232 | tf_op jit(solution)/shard_map/all_gather | solution.py:299
  1162.6 436.3 %all-gather.27.cloned.1.call-start = ((), (), s32[]{:S(2)}) async-start(), calls=%async_computation.12 | async-start | bytes 24510464 | tf_op jit(solution)/shard_map/all_gather | solution.py:298
  1163.3 487.6 %all-reduce.14.cloned.1.call-start = ((), (), s32[]{:S(2)}) async-start(), calls=%async_computation.13 | async-start | bytes 2097152 | tf_op jit(solution)/shard_map/psum | solution.py:310
  1611.2 111.4 %all-gather.29.cloned.1.call-start = ((), (), s32[]{:S(2)}) async-start(), calls=%async_computation.14 | async-start | bytes 4456448 | tf_op jit(solution)/shard_map/all_gather | solution.py:297
  1611.9 316.2 %all-gather.35.cloned.1.call-start = ((), (), s32[]{:S(2)}) async-start(), calls=%async_computation.24 | async-start | bytes 17825792 | tf_op jit(solution)/shard_map/all_gather | solution.py:35
  1727.5 7.0 copy-start.11
  1738.0 383.0 %all-gather.31.cloned.1.call-start = ((), (), s32[]{:S(2)}) async-start(), calls=%async_computation.15 | async-start | bytes 17825792 | tf_op jit(solution)/shard_map/all_gather | solution.py:295
  1738.8 540.6 %all-reduce.16.cloned.1.call-start = ((), (), s32[]{:S(2)}) async-start(), calls=%async_computation.16 | async-start | bytes 2097152 | tf_op jit(solution)/shard_map/psum | solution.py:365
  2024.8 5.1 copy-start.20
  2059.2 61.7 %copy-start.32 = (bf16[1,256,1024]{2,1,0:T(8,128)(2,1)}, bf16[1,256,1024]{2,1,0:T(8,128)(2,1)S(1)}, u32[]{:S(2)}) copy-start(bf16[1,256,1024]{2,1,0:T(8,128)(2,1)S(1)} %stack_reshape.10) | copy-start | bytes 1572868
  2060.2 72.6 %copy-start.34 = (bf16[1,256,1024]{2,1,0:T(8,128)(2,1)}, bf16[1,256,1024]{2,1,0:T(8,128)(2,1)S(1)}, u32[]{:S(2)}) copy-start(bf16[1,256,1024]{2,1,0:T(8,128)(2,1)S(1)} %stack_reshape.9) | copy-start | bytes 1572868
  2121.0 11.8 copy-start.2
  2132.8 963.6 %reduce-scatter.12.cloned.1.call-start = ((), (), s32[]{:S(2)}) async-start(), calls=%async_computation.21 | async-start | bytes 49020928 | tf_op jit(solution)/shard_map/reduce_scatter | solution.py:383
  2153.3 1633.9 %reduce-scatter.6.cloned.1.call-start = ((), (), s32[]{:S(2)}) async-start(), calls=%async_computation.17 | async-start | bytes 35651584 | tf_op jit(solution)/shard_map/reduce_scatter | solution.py:380
  2169.5 2099.1 %reduce-scatter.14.cloned.1.call-start = ((), (), s32[]{:S(2)}) async-start(), calls=%async_computation.22 | async-start | bytes 24510464 | tf_op jit(solution)/shard_map/reduce_scatter | solution.py:384
  2181.6 2274.2 %reduce-scatter.10.cloned.1.call-start = ((), (), s32[]{:S(2)}) async-start(), calls=%async_computation.20 | async-start | bytes 8912896 | tf_op jit(solution)/shard_map/reduce_scatter | solution.py:382
  2188.9 40.7 copy-start.47
  2188.9 2377.4 %all-reduce.18.cloned.1.call-start = ((), (), s32[]{:S(2)}) async-start(), calls=%async_computation.19 | async-start | bytes 131072 | tf_op jit(solution)/shard_map/psum | solution.py:395
  2278.2 2365.8 %reduce-scatter.8.cloned.1.call-start = ((), (), s32[]{:S(2)}) async-start(), calls=%async_computation.18 | async-start | bytes 139264 | tf_op jit(solution)/shard_map/reduce_scatter | solution.py:381
  (62 other events, 154.1 us)
Sparse Core Ops, SparseCore 0:
  10.8 195.2 all-gather.16
  230.1 349.2 all-gather.32
  582.1 87.3 all-gather.18
  674.5 19.4 all-reduce.9
  697.0 252.4 all-gather.20
  952.5 180.7 all-gather.22
  1142.2 17.7 all-reduce.11
  1162.8 183.7 all-gather.24
  1349.3 249.4 all-gather.26
  1611.3 17.7 all-reduce.13
  1632.2 90.3 all-gather.28
  1738.1 190.0 all-gather.34
  1931.3 189.6 all-gather.30
  2132.9 17.7 all-reduce.15
  2153.4 942.9 reduce-scatter.11
  3098.6 688.5 reduce-scatter.5
  3789.9 478.6 reduce-scatter.13
  4271.3 184.5 reduce-scatter.9
  4461.9 104.3 all-reduce.17
  4569.1 74.8 reduce-scatter.7
where the time goes:
time: 4670 us; the launch traced here: 4650 us
  waiting for transfers between devices  3790 us (81%)
  blocking collectives  395 us (8%)
  matrix products  232 us (5%)
  other arithmetic  121 us (3%)
  local copies, waits for them, and re-layouts  95.9 us (2%)
    reduce_scatter x1, waiting for transfers between devices, shards(): lax.psum_scatter(grad_ffn_in, 'seq', scatter_dimension=1, tiled=True)  732 us
    reduce_scatter x1, waiting for transfers between devices, shards(): lax.psum_scatter(grad_mixer_in, 'seq', scatter_dimension=1, tiled=True)  687 us
    reduce_scatter x1, waiting for transfers between devices, shards(): lax.psum_scatter(grad_down, 'seq', scatter_dimension=1, tiled=True)  479 us
    all_gather x1, waiting for transfers between devices, entering(): everything = jax.tree.map(lambda part: lax.all_gather(part, axis), shard)  294 us
    all_gather x1, waiting for transfers between devices, shards(): lax.all_gather(held_shards[5], 'seq', axis=1, tiled=True)  241 us
    all_gather x1, waiting for transfers between devices, shards(): lax.all_gather(ffn_in, 'seq', axis=1, tiled=True)  234 us
    reduce_scatter x1, waiting for transfers between devices, shards(): lax.psum_scatter(grad_out_proj, 'seq', scatter_dimension=1, tiled=True)  187 us
    all_gather x1, waiting for transfers between devices, shards(): lax.all_gather(held_shards[6], 'seq', axis=1, tiled=True)  183 us
  transfers between devices with their start and end apart: 20, of which 17 were waited for; matrix products, arithmetic and copies ran while one was open for 8% of the time, Pallas kernels for 0%

commit v1 on v0

v1 whole, which is shorter than its diff:
```python
import jax
import jax.numpy as jnp
from jax import lax
from jax.sharding import Mesh, PartitionSpec as P

HD = 512
CHUNK = 128
EPSILON = 1e-06
HEAD_FLOOR = 1.0
TEAM = 4

BF = jnp.bfloat16
F32 = jnp.float32


def dot(a, b):
    return jnp.dot(a, b, preferred_element_type=F32)


def dot_rows(a, b):
    return lax.dot_general(a, b, (((0,), (0,)), ((), ())), preferred_element_type=F32)


def dot_last(a, b):
    return lax.dot_general(a, b, (((1,), (1,)), ((), ())), preferred_element_type=F32)


def swap_cores(parts):
    return lax.all_to_all(parts, "c", 0, 0)


def gather_weights(pack):
    rows, _, cols = pack.shape
    pieces = pack.reshape(2, rows // 2, 2, cols)
    pieces = swap_cores(pieces)
    pieces = pieces.transpose(0, 2, 1, 3).reshape(TEAM, rows // 2, cols)
    pieces = lax.all_to_all(pieces, "t", 0, 0)
    everything = lax.all_gather(pieces, "g")
    everything = lax.all_gather(everything, "c", axis=2)
    return everything.reshape(-1, cols)


def scatter_grads(grad):
    groups = lax.axis_size("g")
    cols = grad.shape[1]
    rows = grad.shape[0] // (groups * TEAM)
    part = grad.astype(BF).reshape(groups, TEAM, 2, rows // 2, cols)
    part = part.transpose(2, 0, 1, 3, 4)
    part = lax.psum_scatter(part, "c", scatter_dimension=0, tiled=False)
    part = lax.psum_scatter(part, "g", scatter_dimension=0, tiled=False)
    part = lax.all_to_all(part, "t", 0, 0)
    part = part.reshape(2, 2, rows // 2, cols)
    part = swap_cores(part)
    return part.transpose(0, 2, 1, 3).reshape(rows, 2, cols).astype(F32)


def blocks_to_owners(partial):
    width = partial.shape[1]
    parts = partial.astype(BF).reshape(2, 2, -1, width).transpose(1, 0, 2, 3)
    parts = swap_cores(parts).reshape(TEAM, -1, width)
    return lax.psum_scatter(parts, "t", scatter_dimension=0, tiled=False).astype(F32)


def owners_to_blocks(rows):
    width = rows.shape[1]
    parts = lax.all_gather(rows, "t").reshape(2, 2, -1, width)
    parts = swap_cores(parts)
    return parts.transpose(1, 0, 2, 3).reshape(-1, width)


def chunk_masks(resets):
    counted = jnp.cumsum(resets)
    position = jnp.arange(resets.shape[0])
    pair = (position[:, None] >= position[None, :]) & (counted[:, None] == counted[None, :])
    visible = (counted == 0).astype(F32)[:, None]
    keep = (counted[-1] == 0).astype(F32)
    last = (counted == counted[-1]).astype(F32)[:, None]
    return pair, visible, keep, last


def low(v):
    return v.astype(BF)


def shards(
    tokens,
    cotangent,
    lengths,
    attn_gain,
    ffn_gain,
    mixer_in,
    decay_down,
    decay_up,
    decay_bias,
    head_gain,
    mixer_out,
    ffn_in,
    ffn_out,
):
    g, t, c = lax.axis_index("g"), lax.axis_index("t"), lax.axis_index("c")
    groups = lax.axis_size("g")
    block, width = tokens.shape
    half = block // 2
    rows = mixer_in.shape[1]
    units = ffn_out.shape[0] // 2
    team_tokens = 2 * block
    chunks = team_tokens // CHUNK

    small = jnp.concatenate([attn_gain[:, None], ffn_gain[:, None], decay_down], axis=1)
    small = lax.all_gather(small, ("g", "t"), axis=0, tiled=True)
    gain_one, gain_two, rank_down = small[:, 0].astype(F32), small[:, 1].astype(F32), small[:, 2:]

    mixer_pack = jnp.concatenate(
        [
            mixer_in.transpose(1, 0, 2).reshape(rows, 4, 2, HD),
            mixer_out.T.reshape(rows, 1, 2, HD),
        ],
        axis=1,
    )
    mixer_pack = mixer_pack.transpose(0, 2, 1, 3).reshape(rows, 2, 5 * HD)
    ffn_pack = jnp.concatenate(
        [
            ffn_in.transpose(1, 0, 2).reshape(rows, 2, 2, units),
            ffn_out.T.reshape(rows, 1, 2, units),
        ],
        axis=1,
    )
    ffn_pack = ffn_pack.transpose(0, 2, 1, 3).reshape(rows, 2, 3 * units)
    mixer_w = gather_weights(mixer_pack)
    ffn_w = gather_weights(ffn_pack)

    inputs = lax.all_gather(tokens, "t")
    inputs = lax.dynamic_slice_in_dim(inputs, 2 * c, 2, 0).reshape(team_tokens, width).astype(F32)
    own = lax.dynamic_slice_in_dim(tokens, half * c, half, 0).astype(F32)
    own_dy = lax.dynamic_slice_in_dim(cotangent, half * c, half, 0)
    ffn_dy = lax.all_gather(own_dy, "t", axis=0, tiled=True)
    scale_one = lax.rsqrt(jnp.mean(inputs * inputs, -1, keepdims=True) + EPSILON)
    hidden_one = low(inputs * scale_one * gain_one)

    up_head = lax.dynamic_slice_in_dim(decay_up, HD * (t % 2), HD, 1)
    bias_head = lax.dynamic_slice_in_dim(decay_bias, HD * (t % 2), HD, 0)
    ups = lax.all_gather(up_head, "c")
    biases = lax.all_gather(bias_head, "c")
    up_head, bias_head = ups[t // 2], biases[t // 2]

    first = (g * 2 + c) * team_tokens
    starts = jnp.cumsum(lengths) - lengths
    position = first + jnp.arange(team_tokens, dtype=jnp.int32)
    resets = jnp.any(position[:, None] == starts[None, :], axis=1).astype(jnp.int32)

    projected = dot(hidden_one, mixer_w[:, : 4 * HD])
    queries = projected[:, :HD] * HD ** (-0.5)
    keys = projected[:, HD : 2 * HD]
    values = projected[:, 2 * HD : 3 * HD]
    out_gate = projected[:, 3 * HD :]
    low_rank = low(dot(hidden_one, rank_down))
    gate_input = dot(low_rank, up_head) + bias_head
    log_gates = jax.nn.log_sigmoid(gate_input) / 16.0

    ones = (jnp.arange(CHUNK)[:, None] >= jnp.arange(CHUNK)[None, :]).astype(F32)
    cumulated = jnp.einsum(
        "ij,cjk->cik", ones, log_gates.reshape(chunks, CHUNK, HD), precision=lax.Precision.HIGHEST
    )
    items = []
    for n in range(chunks):
        at = slice(n * CHUNK, (n + 1) * CHUNK)
        q, k, v, b = queries[at], keys[at], values[at], cumulated[n]
        pair, visible, keep, last = chunk_masks(resets[at])
        middle, end = b[CHUNK // 2 - 1], b[-1]
        eq, ek, eb = jnp.exp(b - middle), jnp.exp(middle - b), jnp.exp(b) * visible
        el = jnp.exp(end - b) * last
        qh, kh, qd, kc = low(q * eq), low(k * ek), low(q * eb), k * el
        scores = low(jnp.where(pair, dot_last(qh, kh), 0.0))
        carry = keep * jnp.exp(end)
        update = dot_rows(low(kc), low(v))
        items.append((q, k, low(v), pair, eq, ek, eb, el, qh, kh, qd, kc, scores, carry, update))

    state = jnp.zeros((HD, HD), F32)
    decay = jnp.ones((HD,), F32)
    for it in items:
        state = it[13][:, None] * state + it[14]
        decay = decay * it[13]
    all_states = lax.all_gather(state, ("g", "c"))
    all_decays = lax.all_gather(decay, ("g", "c"))
    index = g * 2 + c
    segments = 2 * groups

    def enter(n, s):
        new = all_decays[n][:, None] * s + all_states[n]
        return jnp.where(n < index, new, s)

    state = lax.fori_loop(0, segments, enter, jnp.zeros((HD, HD), F32))
    outs, states = [], []
    for it in items:
        states.append(state)
        outs.append(dot(it[12], it[2]) + dot(it[10], low(state)))
        state = it[13][:, None] * state + it[14]
    mixed = jnp.concatenate(outs, axis=0)
    head_scale = lax.rsqrt(jnp.mean(mixed * mixed, -1, keepdims=True) + HEAD_FLOOR)
    head_normed = mixed * head_scale
    normed_heads = head_normed * head_gain
    gate_sig = jax.nn.sigmoid(out_gate)
    gate_silu = out_gate * gate_sig
    gated = low(normed_heads * gate_silu)
    branch = blocks_to_owners(dot_last(gated, mixer_w[:, 4 * HD :]))
    middle = own + branch
    scale_two = lax.rsqrt(jnp.mean(middle * middle, -1, keepdims=True) + EPSILON)
    normed_two = middle * scale_two
    hidden_two = lax.all_gather(low(normed_two * gain_two), "t", axis=0, tiled=True)

    up_a = dot(hidden_two, ffn_w[:, :units])
    up_b = dot(hidden_two, ffn_w[:, units : 2 * units])
    ffn_sig = jax.nn.sigmoid(up_a)
    ffn_silu = up_a * ffn_sig
    activated = low(ffn_silu * up_b)
    down = dot_last(activated, ffn_w[:, 2 * units :]).astype(BF)
    down = lax.psum_scatter(down, "t", scatter_dimension=0, tiled=True).astype(F32)
    result = lax.all_gather((middle + down).astype(BF), "c", axis=0, tiled=True)

    grad_act = dot(ffn_dy, ffn_w[:, 2 * units :])
    grad_gate = low(grad_act * up_b * ffn_sig * (1.0 + up_a * (1.0 - ffn_sig)))
    grad_upper = low(grad_act * ffn_silu)
    back = dot_last(grad_gate, ffn_w[:, :units]) + dot_last(grad_upper, ffn_w[:, units : 2 * units])
    grad_hidden_two = lax.psum_scatter(
        back.astype(BF), "t", scatter_dimension=0, tiled=True
    ).astype(F32)
    grad_ffn = jnp.concatenate(
        [
            dot_rows(hidden_two, grad_gate),
            dot_rows(hidden_two, grad_upper),
            dot_rows(ffn_dy, activated),
        ],
        axis=1,
    )
    grad_gain_two = jnp.sum(grad_hidden_two * normed_two, axis=0)
    scaled_two = grad_hidden_two * gain_two
    grad_middle = own_dy.astype(F32) + scale_two * (
        scaled_two - normed_two * jnp.mean(scaled_two * normed_two, -1, keepdims=True)
    )
    grad_branch = owners_to_blocks(low(grad_middle))
    grad_out_proj = dot_rows(grad_branch, gated)
    grad_gated = dot(grad_branch, mixer_w[:, 4 * HD :])
    grad_normed = grad_gated * gate_silu
    grad_out_gate = grad_gated * normed_heads * gate_sig * (1.0 + out_gate * (1.0 - gate_sig))
    grad_head_gain = jnp.sum(grad_normed * head_normed, axis=0)
    scaled_heads = grad_normed * head_gain
    grad_mixed = head_scale * (
        scaled_heads - head_normed * jnp.mean(scaled_heads * head_normed, -1, keepdims=True)
    )

    douts = [low(grad_mixed[n * CHUNK : (n + 1) * CHUNK]) for n in range(chunks)]
    outgoing = [dot_rows(it[10], d) for it, d in zip(items, douts)]
    dstate = jnp.zeros((HD, HD), F32)
    for it, o in zip(items[::-1], outgoing[::-1]):
        dstate = it[13][:, None] * dstate + o
    all_states = lax.all_gather(low(dstate), ("g", "c"))

    def leave(n, s):
        at = segments - 1 - n
        new = all_decays[at][:, None] * s + all_states[at].astype(F32)
        return jnp.where(at > index, new, s)

    dstate = lax.fori_loop(0, segments, leave, jnp.zeros((HD, HD), F32))
    grads = []
    for n in range(chunks - 1, -1, -1):
        q, k, v, pair, eq, ek, eb, el, qh, kh, qd, kc, scores, carry, update = items[n]
        do, state, ds = douts[n], states[n], low(dstate)
        gs = low(jnp.where(pair, dot_last(do, v), 0.0))
        dv = dot_rows(scores, do) + dot(low(kc), ds)
        dq = dot(gs, kh) * eq + dot_last(do, low(state)) * eb
        gkc = dot_last(v, ds)
        dk = dot_rows(gs, qh) * ek + gkc * el
        dcum = dq * q - dk * k
        extra = jnp.sum(gkc * kc, axis=0) + carry * jnp.sum(state * dstate, axis=-1)
        dcum = dcum.at[-1].add(extra)
        dlog = jnp.einsum("ji,jk->ik", ones, dcum, precision=lax.Precision.HIGHEST)
        dstate = carry[:, None] * dstate + outgoing[n]
        grads.append((dq, dk, dv, dlog))
    grads = grads[::-1]
    grad_queries, grad_keys, grad_values, grad_logs = (
        jnp.concatenate([gr[i] for gr in grads], axis=0) for i in range(4)
    )
    grad_gate_input = grad_logs * jax.nn.sigmoid(-gate_input) / 16.0
    grad_bias = jnp.sum(grad_gate_input, axis=0)
    grad_input_low = low(grad_gate_input)
    grad_decay_up = dot_rows(low_rank, grad_input_low)
    grad_rank_part = dot_last(grad_input_low, up_head)
    grad_proj = jnp.concatenate(
        [
            low(grad_queries * HD ** (-0.5)),
            low(grad_keys),
            low(grad_values),
            low(grad_out_gate),
        ],
        axis=1,
    )
    grad_mixer = jnp.concatenate([dot_rows(hidden_one, grad_proj), grad_out_proj], axis=1)
    hidden_part = dot_last(grad_proj, mixer_w[:, : 4 * HD])
    grad_rank = low(lax.psum(grad_rank_part, "t"))
    grad_rank_down = dot_rows(hidden_one, grad_rank) / TEAM
    hidden_part = jnp.concatenate([hidden_part, jnp.zeros((team_tokens, 0), F32)], axis=1)
    grad_hidden_one = blocks_to_owners(hidden_part)
    rank_own = swap_cores(grad_rank.reshape(2, 2, half, -1).transpose(1, 0, 2, 3))
    rank_own = rank_own.reshape(TEAM, half, -1)[t]
    grad_hidden_one = grad_hidden_one + dot_last(rank_own, rank_down)
    scale_own = lax.rsqrt(jnp.mean(own * own, -1, keepdims=True) + EPSILON)
    normed_own = own * scale_own
    grad_gain_one = jnp.sum(grad_hidden_one * normed_own, axis=0)
    scaled_one = grad_hidden_one * gain_one
    grad_inputs = grad_middle + scale_own * (
        scaled_one - normed_own * jnp.mean(scaled_one * normed_own, -1, keepdims=True)
    )
    grad_inputs = lax.all_gather(grad_inputs.astype(BF), "c", axis=0, tiled=True)

    mixer_home = scatter_grads(grad_mixer).reshape(rows, 2, 5, HD)
    ffn_home = scatter_grads(grad_ffn).reshape(rows, 2, 3, units)
    small_home = jnp.concatenate(
        [grad_gain_one[:, None], grad_gain_two[:, None], grad_rank_down], axis=1
    )
    small_home = lax.psum_scatter(
        lax.psum(small_home, "c"), ("g", "t"), scatter_dimension=0, tiled=True
    )
    head_small = jnp.concatenate([grad_decay_up, grad_bias[None], grad_head_gain[None]], axis=0)
    head_small = lax.psum(head_small, ("g", "c"))
    head_small = lax.all_gather(head_small, "t")
    pair_small = lax.dynamic_slice_in_dim(head_small, 2 * c, 2, 0)
    decay_up_home = pair_small[:, :-2].transpose(1, 0, 2).reshape(-1, 2 * HD)
    bias_home = pair_small[:, -2].reshape(2 * HD)
    head_gain_home = jnp.sum(head_small[:, -1], axis=0)
    return (
        result,
        grad_inputs,
        small_home[:, 0],
        small_home[:, 1],
        mixer_home[:, :, :4].transpose(2, 0, 1, 3).reshape(4, rows, 2 * HD),
        small_home[:, 2:],
        decay_up_home,
        bias_home,
        head_gain_home,
        mixer_home[:, :, 4].reshape(rows, 2 * HD).T,
        ffn_home[:, :, :2].transpose(2, 0, 1, 3).reshape(2, rows, 2 * units),
        ffn_home[:, :, 2].reshape(rows, 2 * units).T,
    )


def solution(mesh):
    devices = mesh.devices
    inner = Mesh(devices.reshape(devices.shape[0] // TEAM, TEAM, devices.shape[1]), ("g", "t", "c"))
    seq = ("g", "t")
    in_specs = (
        P(seq, None),
        P(seq, None),
        P(),
        P(seq),
        P(seq),
        P(None, seq, "c"),
        P(seq, None),
        P(None, "c"),
        P("c"),
        P(),
        P("c", seq),
        P(None, seq, "c"),
        P("c", seq),
    )
    out_specs = (
        P(seq, None),
        P(seq, None),
        P(seq),
        P(seq),
        P(None, seq, "c"),
        P(seq, None),
        P(None, "c"),
        P("c"),
        P(),
        P("c", seq),
        P(None, seq, "c"),
        P("c", seq),
    )
    return jax.shard_map(shards, mesh=inner, in_specs=in_specs, out_specs=out_specs, check_vma=False)
```

time: 4670 us -> 1420 us (0.30)
  waiting for transfers between devices: 3790 us -> 781 us
  blocking collectives: 395 us -> 211 us
  matrix products: 232 us -> 141 us
  local copies, waits for them, and re-layouts: 95.9 us -> 151 us
    reduce_scatter x5 -> x6, waiting for transfers between devices: 2160 us -> 362 us  [the longest x2 196 us: scatter_grads(): part = lax.psum_scatter(part, 'g', scatter_dimension=0, tiled=False)]
    all_gather x10 -> x12, waiting for transfers between devices: 1490 us -> 378 us  [the longest x2 199 us: gather_weights(): everything = lax.all_gather(pieces, 'g')]
    all_gather x8 -> x5, blocking collectives: 312 us -> 65.4 us  [the longest x1 39.3 us: shards(): small = lax.all_gather(small, ('g', 't'), axis=0, tiled=True)]
    psum x5 -> x0, waiting for transfers between devices: 128 us -> none  [the longest x1 110 us: shards(): small_sums = lax.psum((grad_decay_up, grad_bias, grad_head_total), 'seq')]
    all_to_all x0 -> x9, blocking collectives: none -> 95 us  [the longest x2 52.6 us: gather_weights(): pieces = lax.all_to_all(pieces, 't', 0, 0)]
    dot_general x74, matrix products: 232 us -> 141 us  [the longest x23 49.9 us: dot_last(): lax.dot_general(a, b, (((1,), (1,)), ((), ())), preferred_element_type=F32)]
    unnamed x1 -> x0, blocking collectives: 79.6 us -> none
    psum x1 -> x3, blocking collectives: 2.51 us -> 50.5 us  [the longest x1 29.6 us: shards(): head_small = lax.psum(head_small, ('g', 'c'))]
  transfers between devices with their start and end apart: 20 -> 24, of which waited for: 17 -> 20; matrix products, arithmetic and copies ran while one was open for 8% -> 16% of each run, Pallas kernels for 0% -> 0%
where the time goes in v1:
time: 1420 us; the launch traced here: 1410 us
  waiting for transfers between devices  781 us (55%)
  blocking collectives  211 us (15%)
  local copies, waits for them, and re-layouts  151 us (11%)
  matrix products  141 us (10%)
  other arithmetic  94.6 us (7%)
  between operations  19.9 us (1%)
    all_gather x2, waiting for transfers between devices, gather_weights(): everything = lax.all_gather(pieces, 'g')  199 us
    reduce_scatter x2, waiting for transfers between devices, scatter_grads(): part = lax.psum_scatter(part, 'g', scatter_dimension=0, tiled=False)  196 us
    reduce_scatter x1, waiting for transfers between devices, shards(): lax.psum_scatter(lax.psum(small_home, 'c'), ('g', 't'), scatter_dimension...  75.1 us
    all_to_all x2, blocking collectives, gather_weights(): pieces = lax.all_to_all(pieces, 't', 0, 0)  52.6 us
    dot_general x23, matrix products, dot_last(): lax.dot_general(a, b, (((1,), (1,)), ((), ())), preferred_element_type=F32)  49.9 us
    dot_general x23, matrix products, dot(): return jnp.dot(a, b, preferred_element_type=F32)  47.2 us
    all_to_all x7, blocking collectives, swap_cores(): return lax.all_to_all(parts, 'c', 0, 0)  42.4 us
    unnamed x24, waiting for transfers between devices  40.5 us
  transfers between devices with their start and end apart: 24, of which 20 were waited for; matrix products, arithmetic and copies ran while one was open for 16% of the time, Pallas kernels for 0%

profile of v1, /device:TPU:0, one launch (start us, length us, event | category | flops | bytes accessed | tf_op | source)
XLA Modules:
  0.0 1411.3 jit_solution(2513838245801495346)
XLA Ops:
  20.9 22.3 %all_to_all.61 = bf16[4,64,2560]{2,1,0:T(8,128)(2,1)} all-to-all(bf16[4,64,2560]{2,1,0:T(8,128)(2,1)S(1)} %bitcast.418), channel_id=1, replica_groups=mesh['g'=4,'t'=4,'c'=2] {'t'}, dimensions={0} | all-to-all | bytes 2621440 | tf_op jit(solution)/shard_map/all_to_all | solution.py:37
  44.0 97.1 %all-gather.35.cloned.1.call-done = bf16[16,64,2560]{2,1,0:T(8,128)(2,1)} async-done(((bf16[4,64,2560]{2,1,0:T(8,128)(2,1)}), bf16[16,64,2560]{2,1,0:T(8,128)(2,1)}) %all-gather.35.cloned.1.call-update) | async-done | bytes 5242896 | tf_op jit(solution)/shard_map/all_gather | solution.py:38
  151.6 39.3 %all_gather.87 = bf16[2048,18]{0,1:T(8,128)(2,1)S(1)} all-gather(bf16[128,18]{0,1:T(8,128)(2,1)S(1)} %pad_maximum_fusion.4), channel_id=1, replica_groups=mesh['g'=4,'t'=4,'c'=2] {'g','t'}, dimensions={0}, use_global_device_ids=true | all-gather | bytes 78336 | tf_op jit(solution)/shard_map/all_gather | solution.py:110
  264.9 30.3 %all_to_all.63 = bf16[4,64,4224]{2,1,0:T(8,128)(2,1)} all-to-all(bf16[4,64,4224]{2,1,0:T(8,128)(2,1)S(1)} %bitcast.405), channel_id=1, replica_groups=mesh['g'=4,'t'=4,'c'=2] {'t'}, dimensions={0} | all-to-all | bytes 4325376 | tf_op jit(solution)/shard_map/all_to_all | solution.py:37
  295.4 13.6 all-gather.11
  324.2 9.4 copy.231
  333.6 17.9 %while.34 = (s32[]{:T(128)}, f32[512,512]{1,0:T(8,128)S(1)}, s32[]{:T(128)}, f32[8,512]{1,0:T(8,128)}, f32[8,512,512]{2,1,0:T(8,128)}, /*index=5*/s32[]{:T(128)}, s32[]{:T(128)}) while((s32[]{:T(128)}, f32[512,512]{1,0:T(8,128)S(1)}, s32[]{:T(128)}, f32[8,512]{1,0:T(8,128)}, f32[8,512,512]{2,1,0:T(8,128)}, /*index=5*/s32[]{:T(128)}, ...), condition=%wide.region_8.9_spmd.clone, body=%wide.region_7.8_spmd.clone.sunk | while | flops 1048580 | bytes 3151985 | solution.py:192
  368.8 102.2 %all-gather.41.cloned.1.call-done = bf16[16,64,4224]{2,1,0:T(8,128)(2,1)} async-done(((bf16[4,64,4224]{2,1,0:T(8,128)(2,1)}), bf16[16,64,4224]{2,1,0:T(8,128)(2,1)}) %all-gather.41.cloned.1.call-update) | async-done | bytes 8650768 | tf_op jit(solution)/shard_map/all_gather | solution.py:38
  471.0 36.2 %reduce-scatter.28.cloned.1.call-done = bf16[1,128,2048]{2,1,0:T(8,128)(2,1)} async-done(((bf16[4,128,2048]{2,1,0:T(8,128)(2,1)}), bf16[1,128,2048]{2,1,0:T(8,128)(2,1)}) %reduce-scatter.28.cloned.1.call-update) | async-done | bytes 524304
  511.7 33.4 %all-gather.29.cloned.1.call-done = bf16[512,2048]{1,0:T(8,128)(2,1)} async-done(((bf16[128,2048]{1,0:T(8,128)(2,1)}), bf16[512,2048]{1,0:T(8,128)(2,1)}) %all-gather.29.cloned.1.call-update) | async-done | bytes 2097168 | tf_op jit(solution)/shard_map/all_gather | solution.py:136
  545.1 33.2 %all-gather.43.cloned.1.call-done = bf16[4,4,128,4224]{3,2,1,0:T(8,128)(2,1)} async-done(((bf16[4,4,64,4224]{3,2,1,0:T(8,128)(2,1)}), bf16[4,4,128,4224]{3,2,1,0:T(8,128)(2,1)}) %all-gather.43.cloned.1.call-update) | async-done | bytes 17301520 | tf_op jit(solution)/shard_map/all_gather | solution.py:39
  578.3 8.3 fusion.6
  586.6 30.8 %all-gather.25.cloned.1.call-done = bf16[512,2048]{1,0:T(8,128)(2,1)} async-done(((bf16[128,2048]{1,0:T(8,128)(2,1)}), bf16[512,2048]{1,0:T(8,128)(2,1)}) %all-gather.25.cloned.1.call-update) | async-done | bytes 2097168 | tf_op jit(solution)/shard_map/all_gather | solution.py:209
  617.4 8.4 fusion.12
  627.2 7.4 multiply_convert_fusion.2
  642.9 35.3 %reduce-scatter.18.cloned.1.call-done = bf16[128,2048]{1,0:T(8,128)(2,1)} async-done(((bf16[512,2048]{1,0:T(8,128)(2,1)}), bf16[128,2048]{1,0:T(8,128)(2,1)}) %reduce-scatter.18.cloned.1.call-update) | async-done | bytes 524304 | tf_op jit(solution)/shard_map/reduce_scatter | solution.py:224
  683.7 35.4 %all-gather.45.cloned.1.call-done = bf16[512,2048]{1,0:T(8,128)(2,1)} async-done(((bf16[128,2048]{1,0:T(8,128)(2,1)}), bf16[512,2048]{1,0:T(8,128)(2,1)}) %all-gather.45.cloned.1.call-update) | async-done | bytes 2097168 | tf_op jit(solution)/shard_map/all_gather | solution.py:66
  758.9 26.1 %all-gather.47.cloned.1.call-done = bf16[4096,512]{0,1:T(8,128)(2,1)} async-done(((bf16[512,512]{0,1:T(8,128)(2,1)}), bf16[4096,512]{0,1:T(8,128)(2,1)}) %all-gather.47.cloned.1.call-update) | async-done | bytes 4194320 | tf_op jit(solution)/shard_map/all_gather | solution.py:256
  791.5 16.9 %while.35 = (s32[]{:T(128)}, f32[512,512]{1,0:T(8,128)S(1)}, s32[]{:T(128)}, f32[8,512]{1,0:T(8,128)}, bf16[8,512,512]{2,1,0:T(8,128)(2,1)}, /*index=5*/s32[]{:T(128)}, s32[]{:T(128)}, s32[]{:T(128)}, s32[]{:T(128)}) while((s32[]{:T(128)}, f32[512,512]{1,0:T(8,128)S(1)}, s32[]{:T(128)}, f32[8,512]{1,0:T(8,128)}, ...), condition=%wide.region_18.19_spmd.clone, body=%wide.region_17.18_spmd.clone.sunk | while | flops 1310728 | bytes 2627759 | solution.py:263
  827.2 9.1 convolution_convert_fusion.3
  864.2 8.6 fusion.20
  872.9 7.5 all_to_all.66
  880.5 8.7 fusion.23
  896.1 19.2 %reduce-scatter.22.cloned.1.call-done = bf16[1,4,4,64,4224]{4,3,2,1,0:T(8,128)(2,1)} async-done(((bf16[2,4,4,64,4224]{4,3,2,1,0:T(8,128)(2,1)}), bf16[1,4,4,64,4224]{4,3,2,1,0:T(8,128)(2,1)}) %reduce-scatter.22.cloned.1.call-update) | async-done | bytes 8650768 | tf_op jit(solution)/shard_map/reduce_scatter | solution.py:49
  930.5 16.9 %psum.21 = bf16[512,16]{0,1:T(8,128)(2,1)S(1)} all-reduce(f32[512,16]{0,1:T(8,128)S(1)} %fusion.79), channel_id=1, replica_groups=mesh['g'=4,'t'=4,'c'=2] {'t'}, use_global_device_ids=true, to_apply=%region_28.29 | all-reduce | flops 8192 | bytes 49152 | tf_op jit(solution)/shard_map/psum | solution.py:299
  957.6 36.2 %reduce-scatter.16.cloned.1.call-done = bf16[128,2048]{1,0:T(8,128)(2,1)} async-done(((bf16[512,2048]{1,0:T(8,128)(2,1)}), bf16[128,2048]{1,0:T(8,128)(2,1)}) %reduce-scatter.16.cloned.1.call-update) | async-done | bytes 524304 | tf_op jit(solution)/shard_map/reduce_scatter | solution.py:217
  996.8 93.0 %reduce-scatter.20.cloned.1.call-done = bf16[1,4,64,2560]{3,2,1,0:T(8,128)(2,1)} async-done(((bf16[4,4,64,2560]{3,2,1,0:T(8,128)(2,1)}), bf16[1,4,64,2560]{3,2,1,0:T(8,128)(2,1)}) %reduce-scatter.20.cloned.1.call-update) | async-done | bytes 1310736 | tf_op jit(solution)/shard_map/reduce_scatter | solution.py:50
  1094.4 29.6 %psum.23 = f32[1,18,512]{2,1,0:T(8,128)S(1)} all-reduce(f32[1,18,512]{2,1,0:T(8,128)S(1)} %maximum_bitcast_fusion.3), channel_id=1, replica_groups=mesh['g'=4,'t'=4,'c'=2] {'g','c'}, use_global_device_ids=true, to_apply=%region_38.39 | all-reduce | flops 9216 | bytes 73728 | tf_op jit(solution)/shard_map/psum | solution.py:324
  1124.0 8.9 all_gather.112
  1139.1 103.2 %reduce-scatter.24.cloned.1.call-done = bf16[1,4,64,4224]{3,2,1,0:T(8,128)(2,1)} async-done(((bf16[4,4,64,4224]{3,2,1,0:T(8,128)(2,1)}), bf16[1,4,64,4224]{3,2,1,0:T(8,128)(2,1)}) %reduce-scatter.24.cloned.1.call-update) | async-done | bytes 2162704 | tf_op jit(solution)/shard_map/reduce_scatter | solution.py:50
  1247.2 75.1 %reduce-scatter.26.cloned.1.call-done = f32[128,18]{0,1:T(8,128)} async-done(((f32[2048,18]{0,1:T(8,128)}), f32[128,18]{0,1:T(8,128)}) %reduce-scatter.26.cloned.1.call-update) | async-done | bytes 9232 | tf_op jit(solution)/shard_map/reduce_scatter | solution.py:320
  1330.0 12.4 all-gather.27.cloned.1.call-done
  (670 shorter events, 393.9 us)
Async XLA Ops:
  7.2 142.5 %copy-start = (bf16[16,1024]{1,0:T(8,128)(2,1)S(1)}, bf16[16,1024]{1,0:T(8,128)(2,1)}, u32[]{:S(2)}) copy-start(bf16[16,1024]{1,0:T(8,128)(2,1)} %param.32) | copy-start | bytes 98308
  7.2 133.9 %all-gather.35.cloned.1.call-start = ((), (), s32[]{:S(2)}) async-start(), calls=%async_computation.30 | async-start | bytes 6553600 | tf_op jit(solution)/shard_map/all_gather | solution.py:38
  43.2 152.1 %all-gather.33.cloned.1.call-start = ((), (), s32[]{:S(2)}) async-start(), calls=%async_computation.29 | async-start | bytes 5242880 | tf_op jit(solution)/shard_map/all_gather | solution.py:132
  43.9 97.3 %copy-start.185 = (s32[13]{0:T(128)S(1)}, s32[13]{0:T(128)}, u32[]{:S(2)}) copy-start(s32[13]{0:T(128)} %param.27) | copy-start | bytes 160
  44.0 175.5 %all-gather.37.cloned.1.call-start = ((), (), s32[]{:S(2)}) async-start(), calls=%async_computation.31 | async-start | bytes 15728640 | tf_op jit(solution)/shard_map/all_gather | solution.py:39
  141.2 183.0 %all-gather.39.cloned.1.call-start = ((), (), s32[]{:S(2)}) async-start(), calls=%async_computation.32 | async-start | bytes 9437184 | tf_op jit(solution)/shard_map/all_gather | solution.py:183
  230.3 122.5 %copy-start.8 = (f32[512,512]{0,1:T(8,128)}, f32[512,512]{0,1:T(8,128)S(1)}, u32[]{:S(2)}) copy-start(f32[512,512]{0,1:T(8,128)S(1)} %fusion.129) | copy-start | bytes 3145732
  233.5 237.4 %all-gather.41.cloned.1.call-start = ((), (), s32[]{:S(2)}) async-start(), calls=%async_computation.33 | async-start | bytes 10813440 | tf_op jit(solution)/shard_map/all_gather | solution.py:38
  295.3 211.9 %reduce-scatter.28.cloned.1.call-start = ((), (), s32[]{:S(2)}) async-start(), calls=%async_computation.39 | async-start | bytes 2621440
  367.8 177.3 %all-gather.29.cloned.1.call-start = ((), (), s32[]{:S(2)}) async-start(), calls=%async_computation.23 | async-start | bytes 2621440 | tf_op jit(solution)/shard_map/all_gather | solution.py:136
  368.7 209.6 %all-gather.43.cloned.1.call-start = ((), (), s32[]{:S(2)}) async-start(), calls=%async_computation.34 | async-start | bytes 25952256 | tf_op jit(solution)/shard_map/all_gather | solution.py:39
  470.9 146.5 %all-gather.25.cloned.1.call-start = ((), (), s32[]{:S(2)}) async-start(), calls=%async_computation.20 | async-start | bytes 2621440 | tf_op jit(solution)/shard_map/all_gather | solution.py:209
  511.2 167.0 %reduce-scatter.18.cloned.1.call-start = ((), (), s32[]{:S(2)}) async-start(), calls=%async_computation.24 | async-start | bytes 2621440 | tf_op jit(solution)/shard_map/reduce_scatter | solution.py:224
  642.9 76.2 %all-gather.45.cloned.1.call-start = ((), (), s32[]{:S(2)}) async-start(), calls=%async_computation.35 | async-start | bytes 2621440 | tf_op jit(solution)/shard_map/all_gather | solution.py:66
  683.7 101.3 %all-gather.47.cloned.1.call-start = ((), (), s32[]{:S(2)}) async-start(), calls=%async_computation.36 | async-start | bytes 4718592 | tf_op jit(solution)/shard_map/all_gather | solution.py:256
  737.7 152.2 %all-reduce.5.cloned.1.call-start = ((), (), s32[]{:S(2)}) async-start(), calls=%async_computation.38 | async-start | bytes 20971520
  843.5 71.7 %reduce-scatter.22.cloned.1.call-start = ((), (), s32[]{:S(2)}) async-start(), calls=%async_computation.27 | async-start | bytes 25952256 | tf_op jit(solution)/shard_map/reduce_scatter | solution.py:49
  864.2 91.0 %reduce-scatter.30.cloned.1.call-start = ((), (), s32[]{:S(2)}) async-start(), calls=%async_computation.40 | async-start | bytes 2621440
  880.5 113.3 %reduce-scatter.16.cloned.1.call-start = ((), (), s32[]{:S(2)}) async-start(), calls=%async_computation.21 | async-start | bytes 2621440 | tf_op jit(solution)/shard_map/reduce_scatter | solution.py:217
  889.3 200.6 %reduce-scatter.20.cloned.1.call-start = ((), (), s32[]{:S(2)}) async-start(), calls=%async_computation.26 | async-start | bytes 6553600 | tf_op jit(solution)/shard_map/reduce_scatter | solution.py:50
  896.0 346.3 %reduce-scatter.24.cloned.1.call-start = ((), (), s32[]{:S(2)}) async-start(), calls=%async_computation.28 | async-start | bytes 10813440 | tf_op jit(solution)/shard_map/reduce_scatter | solution.py:50
  929.4 64.3 %copy-start.152 = (f32[128]{0:T(128)S(1)}, f32[128]{0:T(128)}, u32[]{:S(2)}) copy-start(f32[128]{0:T(128)} %copy-done.151) | copy-start | bytes 1540
  929.5 64.3 %copy-start.176 = (f32[128]{0:T(128)S(1)}, f32[128]{0:T(128)}, u32[]{:S(2)}) copy-start(f32[128]{0:T(128)} %copy-done.175) | copy-start | bytes 1540
  948.0 4.6 all-to-all-start.7
  951.2 371.1 %reduce-scatter.26.cloned.1.call-start = ((), (), s32[]{:S(2)}) async-start(), calls=%async_computation.37 | async-start | bytes 208896 | tf_op jit(solution)/shard_map/reduce_scatter | solution.py:320
  957.5 372.4 %all-gather.31.cloned.1.call-start = ((), (), s32[]{:S(2)}) async-start(), calls=%async_computation.25 | async-start | bytes 1572864 | tf_op jit(solution)/shard_map/all_gather | solution.py:313
  996.8 97.4 %copy-start.26 = (bf16[512,512]{1,0:T(8,128)(2,1)S(1)}, bf16[512,512]{1,0:T(8,128)(2,1)}, u32[]{:S(2)}) copy-start(bf16[512,512]{1,0:T(8,128)(2,1)} %copy-done.25) | copy-start | bytes 1572868
  996.8 97.4 %copy-start.119 = (bf16[512,16]{0,1:T(8,128)(2,1)S(1)}, bf16[512,16]{0,1:T(8,128)(2,1)}, u32[]{:S(2)}) copy-start(bf16[512,16]{0,1:T(8,128)(2,1)} %copy-done.118) | copy-start | bytes 49156
  996.8 97.6 %copy-start.174 = (f32[512]{0:T(512)S(1)}, f32[512]{0:T(512)}, u32[]{:S(2)}) copy-start(f32[512]{0:T(512)} %get-tuple-element.432) | copy-start | bytes 6148
  1089.8 43.7 %all-to-all-start.8 = ((bf16[4,64,2560]{2,1,0:T(8,128)(2,1)}), bf16[4,64,2560]{2,1,0:T(8,128)(2,1)S(1)}, u32[]{:S(2)}, u32[]{:S(2)}) async-start(bf16[4,64,2560]{2,1,0:T(8,128)(2,1)} %bitcast.428), calls=%async_computation.11 | async-start | bytes 2621440 | tf_op jit(solution)/shard_map/all_to_all | solution.py:51
  1093.5 248.8 %all-gather.27.cloned.1.call-start = ((), (), s32[]{:S(2)}) async-start(), calls=%async_computation.22 | async-start | bytes 1572864 | tf_op jit(solution)/shard_map/all_gather | solution.py:218
  1242.3 121.8 %all-to-all-start.10 = ((bf16[4,64,4224]{2,1,0:T(8,128)(2,1)}), bf16[4,64,4224]{2,1,0:T(8,128)(2,1)S(1)}, u32[]{:S(2)}, u32[]{:S(2)}) async-start(bf16[4,64,4224]{2,1,0:T(8,128)(2,1)} %bitcast.421), calls=%async_computation.15 | async-start | bytes 4325376 | tf_op jit(solution)/shard_map/all_to_all | solution.py:51
  (183 other events, 1449.5 us)
Sparse Core Ops, SparseCore 0:
  43.3 97.7 all-gather.34
  143.0 52.2 all-gather.32
  196.8 22.5 all-gather.36
  233.6 83.3 all-gather.38
  318.4 152.4 all-gather.40
  473.7 33.4 reduce-scatter.27
  509.8 35.2 all-gather.28
  546.7 31.5 all-gather.42
  580.9 36.4 all-gather.24
  643.0 35.1 reduce-scatter.17
  683.8 35.2 all-gather.44
  737.8 47.1 all-gather.46
  843.6 41.3 all-reduce.4
  887.3 27.8 reduce-scatter.21
  918.3 36.7 reduce-scatter.29
  958.5 35.1 reduce-scatter.15
  996.0 93.7 reduce-scatter.19
  1092.2 150.1 reduce-scatter.23
  1245.2 77.0 reduce-scatter.25
  1324.3 5.5 all-gather.30
  1332.1 10.1 all-gather.26

commit v2 on v1

v2 whole, which is shorter than its diff:
```python
import functools

import jax
import jax.numpy as jnp
from jax import lax
from jax.experimental import pallas as pl
from jax.experimental.pallas import tpu as pltpu
from jax.sharding import Mesh, PartitionSpec as P

HD = 512
CHUNK = 128
EPSILON = 1e-06
HEAD_FLOOR = 1.0
TEAM = 4

BF = jnp.bfloat16
F32 = jnp.float32
MESH = pl.DeviceIdType.MESH
ANY = pl.BlockSpec(memory_space=pl.ANY)
VMEM = pl.BlockSpec(memory_space=pltpu.VMEM)
DMA = pltpu.SemaphoreType.DMA

SEQ = ("g", "y", "x")
FLIPS = ((1, 1), (0, 1), (1, 0), (0, 0))


def dot(a, b):
    return jnp.dot(a, b, preferred_element_type=F32)


def dot_rows(a, b):
    return lax.dot_general(a, b, (((0,), (0,)), ((), ())), preferred_element_type=F32)


def dot_last(a, b):
    return lax.dot_general(a, b, (((1,), (1,)), ((), ())), preferred_element_type=F32)


def low(v):
    return v.astype(BF)


def flip(index, by):
    return 1 - index if by else index


class Place:
    def __init__(self):
        self.y, self.x, self.c = lax.axis_index("y"), lax.axis_index("x"), lax.axis_index("c")
        self.member = self.y * 2 + self.x


def greet_team(me):
    barrier = pltpu.get_barrier_semaphore()
    for n in range(1, 8):
        to = {"y": flip(me.y, n & 1), "x": flip(me.x, n & 2), "c": flip(me.c, n & 4)}
        pl.semaphore_signal(barrier, inc=1, device_id=to, device_id_type=MESH)
    pl.semaphore_wait(barrier, 7)


def greet_all(me):
    barrier = pltpu.get_barrier_semaphore()
    g, groups = lax.axis_index("g"), lax.axis_size("g")
    for k in range(groups):
        for n in range(8):
            if k == 0 and n == 0:
                continue
            to = {
                "g": lax.rem(g + k, groups),
                "y": flip(me.y, n & 1),
                "x": flip(me.x, n & 2),
                "c": flip(me.c, n & 4),
            }
            pl.semaphore_signal(barrier, inc=1, device_id=to, device_id_type=MESH)
    pl.semaphore_wait(barrier, groups * 8 - 1)


def route_member(me):
    out, arrive = [], []
    for fy, fx in FLIPS:
        y, x = flip(me.y, fy), flip(me.x, fx)
        own = (fy, fx) == (0, 0)
        out.append((y * 2 + x, me.member, {"y": y, "x": x}, own))
        arrive.append((y * 2 + x, own))
    return out, arrive


def route_all(me):
    g, groups = lax.axis_index("g"), lax.axis_size("g")
    out, arrive = [], []
    for k in range(groups):
        for fy, fx in FLIPS:
            to_g, y, x = lax.rem(g + k, groups), flip(me.y, fy), flip(me.x, fx)
            own = k == 0 and (fy, fx) == (0, 0)
            chip = to_g * 4 + y * 2 + x
            out.append((chip, g * 4 + me.member, {"g": to_g, "y": y, "x": x}, own))
            arrive.append((chip, own))
    return out, arrive


def route_halves(me):
    mine = me.c == me.y
    out, arrive = [], []
    for fy, fx in FLIPS:
        y, x = flip(me.y, fy), flip(me.x, fx)
        own = mine if (fy, fx) == (0, 0) else False
        out.append((0, me.x * 2 + me.c, {"y": y, "x": x, "c": me.y}, own))
    for fc, fx in FLIPS:
        c, x = flip(me.c, fc), flip(me.x, fx)
        own = mine if (fc, fx) == (0, 0) else False
        arrive.append((x * 2 + c, own))
    return out, arrive


def route_owners(me):
    mine = me.c == me.y
    out, arrive = [], []
    for fc, fx in FLIPS:
        c, x = flip(me.c, fc), flip(me.x, fx)
        own = mine if (fc, fx) == (0, 0) else False
        out.append((x * 2 + c, me.member, {"y": me.c, "x": x, "c": c}, own))
    for fy, fx in FLIPS:
        y, x = flip(me.y, fy), flip(me.x, fx)
        own = mine if (fy, fx) == (0, 0) else False
        arrive.append((y * 2 + x, own))
    return out, arrive


def route_weights(me):
    mine = (me.c == me.y) & (me.c == me.x)
    out, arrive = [], []
    for f in (1, 0):
        x = flip(me.x, f)
        own = (me.c == me.y) & (me.c == x) & (me.x == me.c) if not f else False
        out.append((x, me.y, {"y": me.c, "x": x, "c": me.x}, own))
    for f in (1, 0):
        y = flip(me.y, f)
        own = mine if not f else False
        arrive.append((y, own))
    return out, arrive


def route_weights_home(me):
    mine = (me.c == me.y) & (me.c == me.x)
    out, arrive = [], []
    for f in (1, 0):
        y = flip(me.y, f)
        own = mine if not f else False
        out.append((y, me.x, {"y": y, "x": me.c, "c": me.y}, own))
    for f in (1, 0):
        x = flip(me.x, f)
        own = mine if not f else False
        arrive.append((x, own))
    return out, arrive


def when(condition, run):
    if condition is True:
        run()
    elif condition is not False:
        pl.when(condition)(run)


def unless(condition, run):
    if condition is False:
        run()
    elif condition is not True:
        pl.when(jnp.logical_not(condition))(run)


class Transfer:
    def __init__(self, route, source, target, send, arrive):
        self.route, self.source, self.target, self.send, self.arrive = route, source, target, send, arrive

    def _remote(self, n):
        index, slot, to, own = self.route[0][n]
        return pltpu.make_async_remote_copy(
            src_ref=self.source(index),
            dst_ref=self.target(slot),
            send_sem=self.send.at[n],
            recv_sem=self.arrive.at[slot],
            device_id=to,
            device_id_type=MESH,
        )

    def _local(self, n):
        index, slot, to, own = self.route[0][n]
        return pltpu.make_async_copy(self.source(index), self.target(slot), self.send.at[n])

    def start(self):
        for n, (_, _, _, own) in enumerate(self.route[0]):
            unless(own, lambda: self._remote(n).start())
            when(own, lambda: self._local(n).start())

    def wait_arrive(self):
        for slot, own in self.route[1]:
            ref = self.target(slot)

            def arrived():
                pltpu.make_async_copy(ref, ref, self.arrive.at[slot]).wait()

            unless(own, arrived)

    def wait_local(self):
        for n, (_, _, _, own) in enumerate(self.route[0]):
            when(own, lambda: self._local(n).wait())

    def wait_sent(self):
        for n, (_, _, _, own) in enumerate(self.route[0]):
            unless(own, lambda: self._remote(n).wait_send())

    def wait(self):
        self.wait_arrive()
        self.wait_local()
        self.wait_sent()


def exchange_kernel(routes, everyone, *refs):
    count = len(routes)
    ins, outs = refs[:count], refs[count : 2 * count]
    sems = refs[2 * count :]
    me = Place()
    if everyone:
        greet_all(me)
    else:
        greet_team(me)
    transfers = []
    for n, (route, whole) in enumerate(routes):
        i, o = ins[n], outs[n]
        transfer = Transfer(
            route(me),
            (lambda _, i=i: i) if whole else (lambda k, i=i: i.at[k]),
            lambda k, o=o: o.at[k],
            sems[2 * n],
            sems[2 * n + 1],
        )
        transfer.start()
        transfers.append(transfer)
    for transfer in transfers:
        transfer.wait()


def exchange(call_id, *parts, everyone=False):
    routes = [(route, whole) for route, _, _, whole in parts]
    arrays = [array for _, array, _, _ in parts]
    shapes = []
    size = 0
    for _, array, slots, whole in parts:
        shape = array.shape if whole else array.shape[1:]
        shapes.append(jax.ShapeDtypeStruct((slots,) + shape, array.dtype))
        size += (array.size + shapes[-1].size) * array.dtype.itemsize
    scratch = []
    for _, _, slots, _ in parts:
        scratch += [DMA((slots,)), DMA((slots,))]
    return pl.pallas_call(
        functools.partial(exchange_kernel, routes, everyone),
        out_shape=shapes,
        in_specs=[VMEM] * len(parts),
        out_specs=[VMEM] * len(parts),
        scratch_shapes=scratch,
        compiler_params=pltpu.CompilerParams(
            collective_id=call_id, has_side_effects=True, vmem_limit_bytes=size + (8 << 20)
        ),
        name=f"exchange_{call_id}",
    )(*arrays)


def norm_forward_kernel(partial, own, gain, hidden, middle, got, line, send, arrive, send2, arrive2):
    me = Place()
    greet_team(me)
    steps = send.shape[0]
    rows = own.shape[0] // steps

    def part(ref, k, n):
        return ref.at[k, pl.ds(n * rows, rows)]

    sums = [
        Transfer(
            route_owners(me),
            lambda k, n=n: part(partial, k, n),
            lambda k, n=n: part(got, k, n),
            send.at[n],
            arrive.at[n],
        )
        for n in range(steps)
    ]
    spreads = [
        Transfer(
            route_member(me),
            lambda k, n=n: line.at[pl.ds(n * rows, rows)],
            lambda k, n=n: part(hidden, k, n),
            send2.at[n],
            arrive2.at[n],
        )
        for n in range(steps)
    ]
    for transfer in sums:
        transfer.start()
    for n in range(steps):
        sums[n].wait_arrive()
        sums[n].wait_local()
        at = pl.ds(n * rows, rows)
        total = own[at].astype(F32)
        for k in range(TEAM):
            total = total + got[k, at].astype(F32)
        middle[at] = total
        scale = lax.rsqrt(jnp.mean(total * total, -1, keepdims=True) + EPSILON)
        line[at] = low(total * scale * gain[...])
        spreads[n].start()
    for transfer in sums:
        transfer.wait_sent()
    for transfer in spreads:
        transfer.wait()


STEPS = 4


def norm_forward(partial, own, gain):
    rows, width = own.shape
    return pl.pallas_call(
        norm_forward_kernel,
        out_shape=(
            jax.ShapeDtypeStruct((TEAM, rows, width), BF),
            jax.ShapeDtypeStruct((rows, width), F32),
        ),
        in_specs=[VMEM, VMEM, VMEM],
        out_specs=(VMEM, VMEM),
        scratch_shapes=[
            pltpu.VMEM((TEAM, rows, width), BF),
            pltpu.VMEM((rows, width), BF),
            DMA((STEPS, TEAM)),
            DMA((STEPS, TEAM)),
            DMA((STEPS, TEAM)),
            DMA((STEPS, TEAM)),
        ],
        compiler_params=pltpu.CompilerParams(
            collective_id=2, has_side_effects=True, vmem_limit_bytes=32 << 20
        ),
        name="norm_forward",
    )(partial, own, gain)


def norm_backward_kernel(
    partial, cot, middle, gain, branch, grad, gain_grad, got, line, send, arrive, send2, arrive2
):
    me = Place()
    greet_team(me)
    steps = send.shape[0]
    rows = cot.shape[0] // steps

    def part(ref, k, n):
        return ref.at[k, pl.ds(n * rows, rows)]

    sums = [
        Transfer(
            route_member(me),
            lambda k, n=n: part(partial, k, n),
            lambda k, n=n: part(got, k, n),
            send.at[n],
            arrive.at[n],
        )
        for n in range(steps)
    ]
    spreads = [
        Transfer(
            route_halves(me),
            lambda k, n=n: line.at[pl.ds(n * rows, rows)],
            lambda k, n=n: part(branch, k, n),
            send2.at[n],
            arrive2.at[n],
        )
        for n in range(steps)
    ]
    for transfer in sums:
        transfer.start()
    for n in range(steps):
        at = pl.ds(n * rows, rows)
        mid = middle[at]
        scale = lax.rsqrt(jnp.mean(mid * mid, -1, keepdims=True) + EPSILON)
        normed = mid * scale
        sums[n].wait_arrive()
        sums[n].wait_local()
        total = got[0, at].astype(F32)
        for k in range(1, TEAM):
            total = total + got[k, at].astype(F32)
        gsum = jnp.sum(total * normed, axis=0, keepdims=True)
        gain_grad[...] = gsum if n == 0 else gain_grad[...] + gsum
        scaled = total * gain[...]
        out = cot[at].astype(F32) + scale * (
            scaled - normed * jnp.mean(scaled * normed, -1, keepdims=True)
        )
        grad[at] = out
        line[at] = low(out)
        spreads[n].start()
    for transfer in sums:
        transfer.wait_sent()
    for transfer in spreads:
        transfer.wait()


def norm_backward(partial, cot, middle, gain):
    rows, width = cot.shape
    return pl.pallas_call(
        norm_backward_kernel,
        out_shape=(
            jax.ShapeDtypeStruct((TEAM, rows, width), BF),
            jax.ShapeDtypeStruct((rows, width), F32),
            jax.ShapeDtypeStruct((1, width), F32),
        ),
        in_specs=[VMEM] * 4,
        out_specs=(VMEM, VMEM, VMEM),
        scratch_shapes=[
            pltpu.VMEM((TEAM, rows, width), BF),
            pltpu.VMEM((rows, width), BF),
            DMA((STEPS, TEAM)),
            DMA((STEPS, TEAM)),
            DMA((STEPS, TEAM)),
            DMA((STEPS, TEAM)),
        ],
        compiler_params=pltpu.CompilerParams(
            collective_id=3, has_side_effects=True, vmem_limit_bytes=32 << 20
        ),
        name="norm_backward",
    )(partial, cot, middle, gain)


def first_norm_kernel(
    partial, own, grad_middle, gain, down, out, gain_grad, rank_grad, got, line, send, arrive, send2, arrive2
):
    me = Place()
    greet_team(me)
    steps = send.shape[0]
    rows, width = own.shape[0] // steps, own.shape[1]

    def part(ref, k, n):
        return ref.at[k, pl.ds(n * rows, rows)]

    sums = [
        Transfer(
            route_owners(me),
            lambda k, n=n: part(partial, k, n),
            lambda k, n=n: part(got, k, n),
            send.at[n],
            arrive.at[n],
        )
        for n in range(steps)
    ]
    other = {"c": 1 - me.c}

    def twin(n):
        return pltpu.make_async_remote_copy(
            src_ref=line.at[pl.ds(n * rows, rows)],
            dst_ref=part(out, me.c, n),
            send_sem=send2.at[n],
            recv_sem=arrive2.at[n],
            device_id=other,
            device_id_type=MESH,
        )

    def mine(n):
        return pltpu.make_async_copy(
            line.at[pl.ds(n * rows, rows)], part(out, me.c, n), arrive2.at[steps + n]
        )

    for transfer in sums:
        transfer.start()
    for n in range(steps):
        at = pl.ds(n * rows, rows)
        x = own[at].astype(F32)
        scale = lax.rsqrt(jnp.mean(x * x, -1, keepdims=True) + EPSILON)
        normed = x * scale
        sums[n].wait_arrive()
        sums[n].wait_local()
        total = got[0, at].astype(F32)
        for k in range(1, TEAM):
            total = total + got[k, at].astype(F32)
        rank = low(total[:, width:])
        total = total[:, :width] + dot(rank, down[...])
        gsum = jnp.sum(total * normed, axis=0, keepdims=True)
        hidden = low(normed * gain[...])
        rsum = dot_rows(rank, hidden)
        gain_grad[...] = gsum if n == 0 else gain_grad[...] + gsum
        rank_grad[...] = rsum if n == 0 else rank_grad[...] + rsum
        scaled = total * gain[...]
        line[at] = low(
            grad_middle[at]
            + scale * (scaled - normed * jnp.mean(scaled * normed, -1, keepdims=True))
        )
        twin(n).start()
        mine(n).start()
    for transfer in sums:
        transfer.wait_sent()
    for n in range(steps):
        twin(n).wait()
        mine(n).wait()


def first_norm(partial, own, grad_middle, gain, down):
    rows, width = own.shape
    lanes = partial.shape[-1] - width
    return pl.pallas_call(
        first_norm_kernel,
        out_shape=(
            jax.ShapeDtypeStruct((2, rows, width), BF),
            jax.ShapeDtypeStruct((1, width), F32),
            jax.ShapeDtypeStruct((lanes, width), F32),
        ),
        in_specs=[VMEM] * 5,
        out_specs=(VMEM, VMEM, VMEM),
        scratch_shapes=[
            pltpu.VMEM((TEAM, rows, width + lanes), BF),
            pltpu.VMEM((rows, width), BF),
            DMA((STEPS, TEAM)),
            DMA((STEPS, TEAM)),
            DMA((STEPS,)),
            DMA((2 * STEPS,)),
        ],
        compiler_params=pltpu.CompilerParams(
            collective_id=4, has_side_effects=True, vmem_limit_bytes=40 << 20
        ),
        name="first_norm",
    )(partial, own, grad_middle, gain, down)


def join_kernel(piece, out, send, arrive, here):
    c = lax.axis_index("c")
    barrier = pltpu.get_barrier_semaphore()
    pl.semaphore_signal(barrier, inc=1, device_id={"c": 1 - c}, device_id_type=MESH)
    pl.semaphore_wait(barrier, 1)
    copies = []
    for n in range(piece.shape[0]):
        place = out.at[n, :, c]
        copies.append(
            pltpu.make_async_remote_copy(
                src_ref=piece.at[n],
                dst_ref=place,
                send_sem=send.at[n],
                recv_sem=arrive.at[n],
                device_id={"c": 1 - c},
                device_id_type=MESH,
            )
        )
        copies.append(pltpu.make_async_copy(piece.at[n], place, here.at[n]))
    for copy in copies:
        copy.start()
    for copy in copies:
        copy.wait()


def join_pieces(call_id, piece):
    groups, _, rows, cols = piece.shape
    size = piece.size * 4
    out = pl.pallas_call(
        join_kernel,
        out_shape=jax.ShapeDtypeStruct((groups, 2, 2, rows, cols), BF),
        in_specs=[ANY],
        out_specs=VMEM,
        scratch_shapes=[DMA((groups,)), DMA((groups,)), DMA((groups,))],
        compiler_params=pltpu.CompilerParams(
            collective_id=call_id, has_side_effects=True, vmem_limit_bytes=size + (8 << 20)
        ),
        name=f"join_{call_id}",
    )(piece)
    return out.reshape(-1, cols)


def sum_pieces(grad):
    groups = lax.axis_size("g")
    cols = grad.shape[1]
    c = lax.axis_index("c")
    rows = grad.shape[0] // (groups * 4)
    part = low(grad).reshape(groups, 2, 2, rows, cols)
    away = lax.dynamic_index_in_dim(part, 1 - c, 2, keepdims=False)
    keep = lax.dynamic_index_in_dim(part, c, 2, keepdims=False)
    got = lax.ppermute(away, "c", [(0, 1), (1, 0)])
    part = low(keep.astype(F32) + got.astype(F32))
    return lax.psum_scatter(part, "g", scatter_dimension=0, tiled=False)


def states_kernel(
    back, local, decay, out, pair, pair_decay, sums, sum_decays, stage, stage_decay, entering,
    near, far_send, far_arrive, far_send2, far_arrive2,
):
    g, c = lax.axis_index("g"), lax.axis_index("c")
    groups = lax.axis_size("g")
    half = local.shape[0] // 2
    sibling = {"c": 1 - c}
    barrier = pltpu.get_barrier_semaphore()
    pl.semaphore_signal(barrier, inc=1, device_id=sibling, device_id_type=MESH)
    for n in range(1, groups):
        to = {"g": lax.rem(g + n, groups)}
        pl.semaphore_signal(barrier, inc=1, device_id=to, device_id_type=MESH)
    pl.semaphore_wait(barrier, groups)

    def remote(src, dst, send, arrive, to):
        return pltpu.make_async_remote_copy(
            src_ref=src, dst_ref=dst, send_sem=send, recv_sem=arrive, device_id=to, device_id_type=MESH
        )

    first = [
        remote(local.at[pl.ds((1 - c) * half, half)], pair, near.at[0], near.at[1], sibling),
        remote(decay, pair_decay, near.at[2], near.at[3], sibling),
    ]
    for copy in first:
        copy.start()
    for copy in first:
        copy.wait()
    leads = (c == 1) if back else (c == 0)
    mine, theirs = local[pl.ds(c * half, half)], pair[...]
    my_decay, their_decay = decay[...], pair_decay[...]
    early = jnp.where(leads, mine, theirs)
    late = jnp.where(leads, theirs, mine)
    early_decay = jnp.where(leads, my_decay, their_decay)[:1]
    late_decay = jnp.where(leads, their_decay, my_decay)[:1]
    stage[...] = low(late_decay * early + late)
    stage_decay[...] = jnp.broadcast_to(early_decay * late_decay, stage_decay.shape)

    def needs(source, target):
        return (source > target) if back else (source < target)

    for n in range(1, groups):
        to = lax.rem(g + n, groups)

        @pl.when(needs(g, to))
        def _(n=n, to=to):
            remote(stage, sums.at[g], far_send.at[n], far_arrive.at[g], {"g": to}).start()
            remote(stage_decay, sum_decays.at[g], far_send2.at[n], far_arrive2.at[g], {"g": to}).start()

    entering[...] = jnp.zeros_like(entering)
    for n in range(groups):
        k = groups - 1 - n if back else n

        @pl.when(needs(k, g))
        def _(k=k):
            pltpu.make_async_copy(sums.at[k], sums.at[k], far_arrive.at[k]).wait()
            pltpu.make_async_copy(sum_decays.at[k], sum_decays.at[k], far_arrive2.at[k]).wait()
            entering[...] = sum_decays[k][:1] * entering[...] + sums[k].astype(F32)

    at_early = entering[...]
    at_late = early_decay * at_early + early
    out[pl.ds(c * half, half)] = jnp.where(leads, at_early, at_late)
    pair[...] = jnp.where(leads, at_late, at_early)
    last = remote(pair, out.at[pl.ds(c * half, half)], near.at[4], near.at[5], sibling)
    last.start()
    last.wait()
    for n in range(1, groups):
        to = lax.rem(g + n, groups)

        @pl.when(needs(g, to))
        def _(n=n, to=to):
            remote(stage, sums.at[g], far_send.at[n], far_arrive.at[g], {"g": to}).wait_send()
            remote(
                stage_decay, sum_decays.at[g], far_send2.at[n], far_arrive2.at[g], {"g": to}
            ).wait_send()


def states(call_id, back, local, decay):
    groups = lax.axis_size("g")
    rows, cols = local.shape
    half = rows // 2
    return pl.pallas_call(
        functools.partial(states_kernel, back),
        out_shape=jax.ShapeDtypeStruct((rows, cols), F32),
        in_specs=[VMEM, VMEM],
        out_specs=VMEM,
        scratch_shapes=[
            pltpu.VMEM((half, cols), F32),
            pltpu.VMEM((8, cols), F32),
            pltpu.VMEM((groups, half, cols), BF),
            pltpu.VMEM((groups, 8, cols), F32),
            pltpu.VMEM((half, cols), BF),
            pltpu.VMEM((8, cols), F32),
            pltpu.VMEM((half, cols), F32),
            DMA((6,)),
            DMA((groups,)),
            DMA((groups,)),
            DMA((groups,)),
            DMA((groups,)),
        ],
        compiler_params=pltpu.CompilerParams(
            collective_id=call_id, has_side_effects=True, vmem_limit_bytes=32 << 20
        ),
        name="states_back" if back else "states",
    )(local, jnp.broadcast_to(decay, (8, cols)))


def finish_kernel(wide, heads, wide_out, heads_out, gains_out, wide_got, heads_got, line, twin, *sems):
    wide_send, wide_arrive, heads_send, heads_arrive, near, out_send, out_arrive, gain_send, gain_arrive = sems
    me = Place()
    g, groups = lax.axis_index("g"), lax.axis_size("g")
    greet_all(me)
    owners = groups * 4

    def remote(src, dst, send, arrive, to):
        return pltpu.make_async_remote_copy(
            src_ref=src, dst_ref=dst, send_sem=send, recv_sem=arrive, device_id=to, device_id_type=MESH
        )

    mine = g * 4 + me.member
    spreads = Transfer(
        route_all(me),
        lambda k: wide.at[k],
        lambda k: wide_got.at[k],
        wide_send,
        wide_arrive,
    )
    spreads.start()
    group_out, group_arrive = [], []
    for n in range(groups):
        for f in range(2):
            to_g, to_c = lax.rem(g + n, groups), flip(me.c, f)
            own = n == 0 and f == 0
            group_out.append((0, g * 2 + me.c, {"g": to_g, "c": to_c}, own))
            group_arrive.append((to_g * 2 + to_c, own))
    heads_move = Transfer(
        (group_out, group_arrive), lambda _: heads, lambda k: heads_got.at[k], heads_send, heads_arrive
    )
    heads_move.start()
    heads_move.wait()
    total = heads_got[0]
    for n in range(1, groups * 2):
        total = total + heads_got[n]
    line[...] = total
    member_out, member_arrive = route_member(me)
    gain_rows = line.shape[0] - gains_out.shape[1]
    gains = Transfer(
        (member_out, member_arrive),
        lambda _: line.at[pl.ds(gain_rows, gains_out.shape[1])],
        lambda k: gains_out.at[k],
        gain_send,
        gain_arrive,
    )
    gains.start()
    for n, (fy, fx) in enumerate(FLIPS):
        to = {"y": flip(me.y, fy), "x": flip(me.x, fx)}
        if (fy, fx) == (0, 0):
            continue

        @pl.when(me.c == me.y)
        def _(n=n, to=to):
            remote(line, heads_out.at[me.x], out_send.at[n], out_arrive.at[me.x], to).start()

    @pl.when(me.c == me.y)
    def _():
        heads_out[me.x] = line[...]

    spreads.wait()
    total = wide_got[0]
    for n in range(1, owners):
        total = total + wide_got[n]
    wide_got[0] = total
    last = remote(wide_got.at[0], twin, near.at[0], near.at[1], {"c": 1 - me.c})
    last.start()
    for k in range(2):
        own = (me.c == me.y) & (me.x == k)

        @pl.when(jnp.logical_not(own))
        def _(k=k):
            pltpu.make_async_copy(heads_out.at[k], heads_out.at[k], out_arrive.at[k]).wait()

    for n, (fy, fx) in enumerate(FLIPS):
        to = {"y": flip(me.y, fy), "x": flip(me.x, fx)}
        if (fy, fx) == (0, 0):
            continue

        @pl.when(me.c == me.y)
        def _(n=n, to=to):
            remote(line, heads_out.at[me.x], out_send.at[n], out_arrive.at[me.x], to).wait_send()

    gains.wait()
    last.wait()
    wide_out[...] = wide_got[0] + twin[...]


def finish(wide, heads):
    owners, r, rows = wide.shape
    groups = owners // 4
    return pl.pallas_call(
        finish_kernel,
        out_shape=(
            jax.ShapeDtypeStruct((r, rows), F32),
            jax.ShapeDtypeStruct((2,) + heads.shape, F32),
            jax.ShapeDtypeStruct((TEAM, 8, heads.shape[1]), F32),
        ),
        in_specs=[VMEM, VMEM],
        out_specs=(VMEM, VMEM, VMEM),
        scratch_shapes=[
            pltpu.VMEM((owners, r, rows), F32),
            pltpu.VMEM((groups * 2,) + heads.shape, F32),
            pltpu.VMEM(heads.shape, F32),
            pltpu.VMEM((r, rows), F32),
            DMA((owners,)),
            DMA((owners,)),
            DMA((groups * 2,)),
            DMA((groups * 2,)),
            DMA((2,)),
            DMA((TEAM,)),
            DMA((2,)),
            DMA((TEAM,)),
            DMA((TEAM,)),
        ],
        compiler_params=pltpu.CompilerParams(
            collective_id=11, has_side_effects=True, vmem_limit_bytes=32 << 20
        ),
        name="finish",
    )(wide, heads)


def chunk_masks(resets):
    counted = jnp.cumsum(resets)
    position = jnp.arange(resets.shape[0])
    pair = (position[:, None] >= position[None, :]) & (counted[:, None] == counted[None, :])
    visible = (counted == 0).astype(F32)[:, None]
    keep = (counted[-1] == 0).astype(F32)
    last = (counted == counted[-1]).astype(F32)[:, None]
    return pair, visible, keep, last


def shards(
    tokens,
    cotangent,
    lengths,
    attn_gain,
    ffn_gain,
    mixer_in,
    decay_down,
    decay_up,
    decay_bias,
    head_gain,
    mixer_out,
    ffn_in,
    ffn_out,
):
    g, y, x, c = (lax.axis_index(a) for a in SEQ + ("c",))
    groups = lax.axis_size("g")
    block, width = tokens.shape
    half = block // 2
    rows = mixer_in.shape[1]
    units = ffn_out.shape[0] // 2
    team_tokens = 2 * block
    chunks = team_tokens // CHUNK
    rank = decay_down.shape[1]

    mixer_pack = jnp.concatenate(
        [
            mixer_in.transpose(1, 0, 2).reshape(rows, 4, 2, HD),
            mixer_out.T.reshape(rows, 1, 2, HD),
        ],
        axis=1,
    )
    mixer_pack = mixer_pack.transpose(2, 0, 1, 3).reshape(2, rows, 5 * HD)
    small = jnp.concatenate([attn_gain[None], ffn_gain[None], decay_down.T], axis=0)
    small = jnp.pad(small, ((0, 32 - small.shape[0]), (0, 0)))
    mixer_piece, small = exchange(
        0, (route_weights, mixer_pack, 2, False), (route_all, small, 4 * groups, True), everyone=True
    )
    small = small.transpose(1, 0, 2).reshape(32, width)
    gain_one, gain_two = small[0].astype(F32), small[1].astype(F32)
    rank_down = small[2 : 2 + rank]
    mixer_w = lax.all_gather(mixer_piece, "g")
    ffn_pack = jnp.concatenate(
        [
            ffn_in.transpose(1, 0, 2).reshape(rows, 2, 2, units),
            ffn_out.T.reshape(rows, 1, 2, units),
        ],
        axis=1,
    )
    ffn_pack = ffn_pack.transpose(2, 0, 1, 3).reshape(2, rows, 3 * units)
    own = lax.dynamic_slice_in_dim(tokens, half * c, half, 0)
    own_dy = lax.dynamic_slice_in_dim(cotangent, half * c, half, 0)
    ffn_piece, inputs, ffn_dy = exchange(
        1,
        (route_weights, ffn_pack, 2, False),
        (route_halves, own, 4, True),
        (route_member, own_dy, 4, True),
    )
    ffn_w = lax.all_gather(ffn_piece, "g")
    mixer_w = join_pieces(5, mixer_w)

    inputs = inputs.reshape(team_tokens, width).astype(F32)
    ffn_dy = ffn_dy.reshape(team_tokens, width)
    scale_one = lax.rsqrt(jnp.mean(inputs * inputs, -1, keepdims=True) + EPSILON)
    hidden_one = low(inputs * scale_one * gain_one)

    up_head = lax.dynamic_slice_in_dim(decay_up, HD * x, HD, 1)
    bias_head = lax.dynamic_slice_in_dim(decay_bias, HD * x, HD, 0)
    cross = [(0, 1), (1, 0)]
    up_head = jnp.where(c == y, up_head, lax.ppermute(up_head, "c", cross))
    bias_head = jnp.where(c == y, bias_head, lax.ppermute(bias_head, "c", cross))

    first = (g * 2 + c) * team_tokens
    starts = jnp.cumsum(lengths) - lengths
    position = first + jnp.arange(team_tokens, dtype=jnp.int32)
    resets = jnp.any(position[:, None] == starts[None, :], axis=1).astype(jnp.int32)

    projected = dot(hidden_one, mixer_w[:, : 4 * HD])
    queries = projected[:, :HD] * HD ** (-0.5)
    keys = projected[:, HD : 2 * HD]
    values = projected[:, 2 * HD : 3 * HD]
    out_gate = projected[:, 3 * HD :]
    low_rank = low(dot_last(hidden_one, rank_down))
    gate_input = dot(low_rank, up_head) + bias_head
    log_gates = jax.nn.log_sigmoid(gate_input) / 16.0

    ones = (jnp.arange(CHUNK)[:, None] >= jnp.arange(CHUNK)[None, :]).astype(F32)
    cumulated = jnp.einsum(
        "ij,cjk->cik", ones, log_gates.reshape(chunks, CHUNK, HD), precision=lax.Precision.HIGHEST
    )
    items = []
    state = jnp.zeros((HD, HD), F32)
    decay = jnp.ones((1, HD), F32)
    for n in range(chunks):
        at = slice(n * CHUNK, (n + 1) * CHUNK)
        q, k, v, b = queries[at], keys[at], values[at], cumulated[n]
        pair, visible, keep, last = chunk_masks(resets[at])
        middle, end = b[CHUNK // 2 - 1], b[-1:]
        eq, ek, eb = jnp.exp(b - middle), jnp.exp(middle - b), jnp.exp(b) * visible
        el = jnp.exp(end - b) * last
        qh, kh, qd, kc = low(q * eq), low(k * ek), low(q * eb), k * el
        scores = low(jnp.where(pair, dot_last(qh, kh), 0.0))
        carry = keep * jnp.exp(end)
        update = dot_rows(low(v), low(kc))
        state = carry * state + update
        decay = decay * carry
        items.append((q, k, low(v), pair, eq, ek, eb, el, qh, kh, qd, kc, scores, carry, update))
    state = states(9, False, state, decay)
    outs, befores = [], []
    for it in items:
        befores.append(state)
        outs.append(dot(it[12], it[2]) + dot_last(it[10], low(state)))
        state = it[13] * state + it[14]
    mixed = jnp.concatenate(outs, axis=0)
    head_scale = lax.rsqrt(jnp.mean(mixed * mixed, -1, keepdims=True) + HEAD_FLOOR)
    head_normed = mixed * head_scale
    normed_heads = head_normed * head_gain
    gate_sig = jax.nn.sigmoid(out_gate)
    gate_silu = out_gate * gate_sig
    gated = low(normed_heads * gate_silu)
    branch = low(dot_last(gated, mixer_w[:, 4 * HD :])).reshape(TEAM, half, width)
    hidden_two, middle = norm_forward(branch, own, gain_two[None])
    hidden_two = hidden_two.reshape(team_tokens, width)

    ffn_w = join_pieces(6, ffn_w)
    up_a = dot(hidden_two, ffn_w[:, :units])
    up_b = dot(hidden_two, ffn_w[:, units : 2 * units])
    ffn_sig = jax.nn.sigmoid(up_a)
    ffn_silu = up_a * ffn_sig
    activated = low(ffn_silu * up_b)
    down = dot_last(activated, ffn_w[:, 2 * units :]).astype(BF)
    down = lax.psum_scatter(down, ("y", "x"), scatter_dimension=0, tiled=True).astype(F32)
    result = lax.all_gather((middle + down).astype(BF), "c", axis=0, tiled=True)

    grad_act = dot(ffn_dy, ffn_w[:, 2 * units :])
    grad_gate = low(grad_act * up_b * ffn_sig * (1.0 + up_a * (1.0 - ffn_sig)))
    grad_upper = low(grad_act * ffn_silu)
    back = dot_last(grad_gate, ffn_w[:, :units]) + dot_last(grad_upper, ffn_w[:, units : 2 * units])
    grad_ffn_parts = [
        sum_pieces(dot_rows(ffn_dy, activated)),
        sum_pieces(dot_rows(hidden_two, jnp.concatenate([grad_gate, grad_upper], axis=1))),
    ]
    back = low(back).reshape(TEAM, half, width)
    grad_branch, grad_middle, grad_gain_two = norm_backward(back, own_dy, middle, gain_two[None])
    grad_branch = grad_branch.reshape(team_tokens, width)
    grad_out_proj = dot_rows(grad_branch, gated)
    grad_gated = dot(grad_branch, mixer_w[:, 4 * HD :])
    grad_normed = grad_gated * gate_silu
    grad_out_gate = grad_gated * normed_heads * gate_sig * (1.0 + out_gate * (1.0 - gate_sig))
    grad_head_gain = jnp.sum(grad_normed * head_normed, axis=0)
    scaled_heads = grad_normed * head_gain
    grad_mixed = head_scale * (
        scaled_heads - head_normed * jnp.mean(scaled_heads * head_normed, -1, keepdims=True)
    )

    douts = [low(grad_mixed[n * CHUNK : (n + 1) * CHUNK]) for n in range(chunks)]
    outgoing = [dot_rows(d, it[10]) for it, d in zip(items, douts)]
    dstate = jnp.zeros((HD, HD), F32)
    for it, o in zip(items[::-1], outgoing[::-1]):
        dstate = it[13] * dstate + o
    dstate = states(10, True, dstate, decay)
    grads = []
    for n in range(chunks - 1, -1, -1):
        q, k, v, pair, eq, ek, eb, el, qh, kh, qd, kc, scores, carry, update = items[n]
        do, state, ds = douts[n], befores[n], low(dstate)
        gs = low(jnp.where(pair, dot_last(do, v), 0.0))
        dv = dot_rows(scores, do) + dot_last(low(kc), ds)
        dq = dot(gs, kh) * eq + dot(do, low(state)) * eb
        gkc = dot(v, ds)
        dk = dot_rows(gs, qh) * ek + gkc * el
        dcum = dq * q - dk * k
        extra = jnp.sum(gkc * kc, axis=0) + carry[0] * jnp.sum(state * dstate, axis=0)
        dcum = dcum.at[-1].add(extra)
        dlog = jnp.einsum("ji,jk->ik", ones, dcum, precision=lax.Precision.HIGHEST)
        dstate = carry * dstate + outgoing[n]
        grads.append((dq, dk, dv, dlog))
    grads = grads[::-1]
    grad_queries, grad_keys, grad_values, grad_logs = (
        jnp.concatenate([gr[i] for gr in grads], axis=0) for i in range(4)
    )
    grad_gate_input = grad_logs * jax.nn.sigmoid(-gate_input) / 16.0
    grad_bias = jnp.sum(grad_gate_input, axis=0)
    grad_input_low = low(grad_gate_input)
    grad_decay_up = dot_rows(low_rank, grad_input_low)
    grad_proj = jnp.concatenate(
        [
            low(grad_queries * HD ** (-0.5)),
            low(grad_keys),
            low(grad_values),
            low(grad_out_gate),
        ],
        axis=1,
    )
    grad_rank_part = dot_last(grad_input_low, up_head)
    hidden_part = dot_last(grad_proj, mixer_w[:, : 4 * HD])
    lanes = 128
    hidden_part = jnp.concatenate(
        [low(hidden_part), jnp.pad(low(grad_rank_part), ((0, 0), (0, lanes - rank)))], axis=1
    ).reshape(TEAM, half, width + lanes)
    grad_mixer = sum_pieces(
        jnp.concatenate([dot_rows(hidden_one, grad_proj), grad_out_proj], axis=1)
    )
    down_pad = jnp.pad(rank_down, ((0, lanes - rank), (0, 0)))
    grad_inputs, grad_gain_one, grad_rank_down = first_norm(
        hidden_part, own, grad_middle, gain_one[None], down_pad
    )
    grad_inputs = grad_inputs.reshape(block, width)

    wide = jnp.concatenate([grad_gain_one, grad_gain_two, grad_rank_down[:rank]], axis=0)
    wide = jnp.pad(wide, ((0, 24 - wide.shape[0]), (0, 0)))
    wide = wide.reshape(24, 4 * groups, rows).transpose(1, 0, 2)
    heads = jnp.concatenate([grad_decay_up, grad_bias[None], grad_head_gain[None]], axis=0)
    heads = jnp.pad(heads, ((0, 24 - heads.shape[0]), (0, 0)))
    wide, heads, gains = finish(wide, heads)
    homes = exchange(7, *((route_weights_home, a, 2, False) for a in grad_ffn_parts))
    (mixer_home,) = exchange(8, (route_weights_home, grad_mixer, 2, False))
    ffn_down, ffn_pair = (a.astype(F32) for a in homes)
    mixer_home = mixer_home.reshape(2, rows, 5, HD).astype(F32)
    return (
        result,
        grad_inputs,
        wide[0],
        wide[1],
        mixer_home[:, :, :4].transpose(2, 1, 0, 3).reshape(4, rows, 2 * HD),
        wide[2 : 2 + rank].T,
        heads[:, :rank].transpose(1, 0, 2).reshape(rank, 2 * HD),
        heads[:, rank].reshape(2 * HD),
        jnp.sum(gains[:, rank + 1 - 16], axis=0),
        mixer_home[:, :, 4].transpose(0, 2, 1).reshape(2 * HD, rows),
        ffn_pair.reshape(2, rows, 2, units).transpose(2, 1, 0, 3).reshape(2, rows, 2 * units),
        ffn_down.transpose(0, 2, 1).reshape(2 * units, rows),
    )


def solution(mesh):
    devices = mesh.devices
    inner = Mesh(devices.reshape(devices.shape[0] // 4, 2, 2, devices.shape[1]), SEQ + ("c",))
    in_specs = (
        P(SEQ, None),
        P(SEQ, None),
        P(),
        P(SEQ),
        P(SEQ),
        P(None, SEQ, "c"),
        P(SEQ, None),
        P(None, "c"),
        P("c"),
        P(),
        P("c", SEQ),
        P(None, SEQ, "c"),
        P("c", SEQ),
    )
    out_specs = (
        P(SEQ, None),
        P(SEQ, None),
        P(SEQ),
        P(SEQ),
        P(None, SEQ, "c"),
        P(SEQ, None),
        P(None, "c"),
        P("c"),
        P(),
        P("c", SEQ),
        P(None, SEQ, "c"),
        P("c", SEQ),
    )
    return jax.shard_map(shards, mesh=inner, in_specs=in_specs, out_specs=out_specs, check_vma=False)
```

time: 1420 us -> 878 us (0.62)
  waiting for transfers between devices: 781 us -> 205 us
  Pallas kernels: 0 us -> 391 us
  blocking collectives: 211 us -> 0 us
  local copies, waits for them, and re-layouts: 151 us -> 91.3 us
  other arithmetic: 94.6 us -> 49 us
  matrix products: 141 us -> 116 us
    pallas_call x0 -> x12, Pallas kernels: none -> 391 us  [the longest x4 144 us: exchange(): pl.pallas_call(functools.partial(exchange_kernel, routes, everyone), out_...]
    all_gather x11 -> x2, waiting for transfers between devices: 365 us -> 41.2 us  [the longest x1 41.2 us: shards(): ffn_w = lax.all_gather(ffn_piece, 'g')]
    reduce_scatter x6 -> x4, waiting for transfers between devices: 362 us -> 158 us  [the longest x3 120 us: sum_pieces(): return lax.psum_scatter(part, 'g', scatter_dimension=0, tiled=False)]
    all_to_all x9 -> x0, blocking collectives: 95 us -> none  [the longest x2 52.6 us: gather_weights(): pieces = lax.all_to_all(pieces, 't', 0, 0)]
    all_gather x5 -> x0, blocking collectives: 65.4 us -> none  [the longest x1 39.3 us: shards(): small = lax.all_gather(small, ('g', 't'), axis=0, tiled=True)]
    psum x3 -> x0, blocking collectives: 50.5 us -> none  [the longest x1 29.6 us: shards(): head_small = lax.psum(head_small, ('g', 'c'))]
    unnamed x24 -> x7, waiting for transfers between devices: 40.5 us -> 0.11 us
    select_n x16 -> x1, other arithmetic: 22.7 us -> 0.08 us  [shards(): jnp.where(c == y, bias_head, lax.ppermute(bias_head, 'c', cross))]
  transfers between devices with their start and end apart: 24 -> 12, of which waited for: 20 -> 5; matrix products, arithmetic and copies ran while one was open for 16% -> 13% of each run, Pallas kernels for 0% -> 28%
where the time goes in v2:
time: 878 us; the launch traced here: 874 us
  Pallas kernels  391 us (45%)
  waiting for transfers between devices  205 us (23%)
  matrix products  116 us (13%)
  local copies, waits for them, and re-layouts  91.3 us (10%)
  other arithmetic  49 us (6%)
  between operations  20 us (2%)
    pallas_call x4, Pallas kernels, exchange(): pl.pallas_call(functools.partial(exchange_kernel, routes, everyone), out_...  144 us
    reduce_scatter x3, waiting for transfers between devices, sum_pieces(): return lax.psum_scatter(part, 'g', scatter_dimension=0, tiled=False)  120 us
    pallas_call x2, Pallas kernels, states(): pl.pallas_call(functools.partial(states_kernel, back), out_shape=jax.Shap...  72.9 us
    pallas_call x1, Pallas kernels, norm_backward(): pl.pallas_call(norm_backward_kernel, out_shape=(jax.ShapeDtypeStruct((TEA...  50.1 us
    pallas_call x1, Pallas kernels, norm_forward(): pl.pallas_call(norm_forward_kernel, out_shape=(jax.ShapeDtypeStruct((TEAM...  49.9 us
    unnamed x365, local copies, waits for them, and re-layouts  44.8 us
    all_gather x1, waiting for transfers between devices, shards(): ffn_w = lax.all_gather(ffn_piece, 'g')  41.2 us
    dot_general x22, matrix products, dot(): return jnp.dot(a, b, preferred_element_type=F32)  39.1 us
  transfers between devices with their start and end apart: 12, of which 5 were waited for; matrix products, arithmetic and copies ran while one was open for 13% of the time, Pallas kernels for 28%

profile of v2, /device:TPU:0, one launch (start us, length us, event | category | flops | bytes accessed | tf_op | source)
XLA Modules:
  0.0 873.9 jit_solution(18304122061353741030)
XLA Ops:
  10.8 25.7 %exchange_0.1 = (bf16[2,128,2560]{2,1,0:T(8,128)(2,1)}, bf16[16,32,128]{2,1,0:T(8,128)(2,1)S(1)}) custom-call(bf16[2,128,2560]{2,1,0:T(8,128)(2,1)S(1)} %copy.152.refs_0_, bf16[32,128]{1,0:T(8,128)(2,1)S(1)} %fusion.166.refs_1_), custom_call_target="tpu_custom_call" | custom-call | tf_op jit(solution)/shard_map/exchange_0/pallas_call | solution.py:255
  44.3 72.1 %exchange_1.1 = (bf16[2,128,4224]{2,1,0:T(8,128)(2,1)S(1)}, bf16[4,128,2048]{2,1,0:T(8,128)(2,1)S(1)}, bf16[4,128,2048]{2,1,0:T(8,128)(2,1)S(1)}) custom-call(bf16[2,128,4224]{2,1,0:T(8,128)(2,1)S(1)} %copy-done.6, bf16[128,2048]{1,0:T(8,128)(2,1)S(1)} %get-tuple-element.245.refs_1_.own, bf16[128,2048]{1,0:T(8,128)(2,1)S(1)} %get-tuple-element.244.refs_2_.cot), custom_call_target="tpu_custom_call" | custom-call | tf_op jit(solution)/shard_map/exchange_1/pallas_call | solution.py:255
  145.5 8.8 %join_5.1 = bf16[4,2,2,128,2560]{4,3,2,1,0:T(8,128)(2,1)S(1)} custom-call(bf16[4,2,128,2560]{3,2,1,0:T(8,128)(2,1)S(1)} %bitcast.334), custom_call_target="tpu_custom_call" | custom-call | tf_op jit(solution)/shard_map/join_5/pallas_call | solution.py:554
  161.4 39.5 %states.1 = f32[512,512]{1,0:T(8,128)S(1)} custom-call(f32[512,512]{1,0:T(8,128)S(1)} %convolution_add_fusion.1.local, f32[8,512]{1,0:T(8,128)S(1)} %broadcast_in_dim.101.decay), custom_call_target="tpu_custom_call" | custom-call | tf_op jit(solution)/shard_map/states/pallas_call | solution.py:662
  208.2 49.9 %norm_forward.1 = (bf16[4,128,2048]{2,1,0:T(8,128)(2,1)S(1)}, f32[128,2048]{1,0:T(8,128)S(1)}) custom-call(bf16[4,128,2048]{2,1,0:T(8,128)(2,1)S(1)} %bitcast.336, bf16[128,2048]{1,0:T(8,128)(2,1)S(1)} %get-tuple-element.245.refs_1_.own, f32[1,2048]{1,0:T(1,128)S(1)} %get-tuple-element.208.gain), custom_call_target="tpu_custom_call" | custom-call | tf_op jit(solution)/shard_map/norm_forward/pallas_call | solution.py:321
  259.5 41.2 %all-gather.10.cloned.1.call-done = bf16[8,128,4224]{2,1,0:T(8,128)(2,1)} async-done(((bf16[2,128,4224]{2,1,0:T(8,128)(2,1)}), bf16[8,128,4224]{2,1,0:T(8,128)(2,1)}) %all-gather.10.cloned.1.call-update) | async-done | bytes 8650768 | tf_op jit(solution)/shard_map/all_gather | solution.py:878
  304.2 13.6 %join_6.1 = bf16[4,2,2,128,4224]{4,3,2,1,0:T(8,128)(2,1)S(1)} custom-call(bf16[4,2,128,4224]{3,2,1,0:T(8,128)(2,1)S(1)} %bitcast.333), custom_call_target="tpu_custom_call" | custom-call | tf_op jit(solution)/shard_map/join_6/pallas_call | solution.py:554
  317.8 6.0 copy-done.2
  323.8 7.8 fusion.11
  333.1 5.0 fusion.17
  338.1 7.7 multiply_convert_fusion.2
  345.9 4.9 fusion.15
  350.8 5.8 add_convert_fusion
  356.7 50.1 %norm_backward.1 = (bf16[4,128,2048]{2,1,0:T(8,128)(2,1)S(1)}, f32[128,2048]{1,0:T(8,128)S(1)}, f32[1,2048]{1,0:T(1,128)S(1)}) custom-call(bf16[4,128,2048]{2,1,0:T(8,128)(2,1)S(1)} %bitcast.335, bf16[128,2048]{1,0:T(8,128)(2,1)S(1)} %get-tuple-element.244.refs_2_.cot, f32[128,2048]{1,0:T(8,128)S(1)} %get-tuple-element.81.middle, ...), custom_call_target="tpu_custom_call" | custom-call | tf_op jit(solution)/shard_map/norm_backward/pallas_call | solution.py:404
  418.5 33.4 %states_back.1 = f32[512,512]{1,0:T(8,128)S(1)} custom-call(f32[512,512]{1,0:T(8,128)S(1)} %convolution_add_fusion.local, f32[8,512]{1,0:T(8,128)S(1)} %broadcast_in_dim.101.decay), custom_call_target="tpu_custom_call" | custom-call | tf_op jit(solution)/shard_map/states_back/pallas_call | solution.py:662
  478.5 9.0 %convolution_convert_fusion.2 = bf16[4,2,2,128,2048]{4,3,1,0,2:T(8,128)(2,1)S(1)} fusion(bf16[4,2,2,128,512]{4,3,2,1,0:T(8,128)(2,1)S(1)} %bitcast.365, bf16[512,512]{1,0:T(8,128)(2,1)S(1)} %copy-done.88, bf16[128,512]{1,0:T(8,128)(2,1)S(1)} %copy-done.112, bf16[128,512]{1,0:T(8,128)(2,1)S(1)} %copy-done.113, bf16[128,512]{1,0:T(8,128)(2,1)S(1)} %copy-done.114, ...), kind=kOutput, calls=%fused_computation.17 | convolution fusion | flops 4320133120 | bytes 12582912 | tf_op jit(solution)/shard_map/dot_general | solution.py:32
  492.8 7.4 fusion.31
  500.3 38.4 %reduce-scatter.5.cloned.1.call-done = bf16[128,2048]{1,0:T(8,128)(2,1)} async-done(((bf16[512,2048]{1,0:T(8,128)(2,1)}), bf16[128,2048]{1,0:T(8,128)(2,1)}) %reduce-scatter.5.cloned.1.call-update) | async-done | bytes 524304 | tf_op jit(solution)/shard_map/reduce_scatter | solution.py:951
  541.1 8.2 fusion.1
  549.6 5.5 convolution_convert_fusion.1
  558.1 7.8 convolution_convert_fusion
  576.2 5.5 collective-permute-done.4
  581.7 8.3 fusion
  600.0 8.6 fusion.28
  609.9 30.0 %first_norm.1 = (bf16[2,128,2048]{2,1,0:T(8,128)(2,1)S(1)}, f32[1,2048]{1,0:T(1,128)S(1)}, f32[128,2048]{1,0:T(8,128)S(1)}) custom-call(bf16[4,128,2176]{2,1,0:T(8,128)(2,1)S(1)} %bitcast.332, bf16[128,2048]{1,0:T(8,128)(2,1)S(1)} %get-tuple-element.245.refs_1_.own, f32[128,2048]{1,0:T(8,128)S(1)} %copy-done.14, f32[1,2048]{1,0:T(1,128)S(1)} %get-tuple-element.207.gain, ...), custom_call_target="tpu_custom_call" | custom-call | tf_op jit(solution)/shard_map/first_norm/pallas_call | solution.py:502
  640.1 22.2 %finish.1 = (f32[24,128]{1,0:T(8,128)S(1)}, f32[2,24,512]{2,1,0:T(8,128)S(1)}, f32[4,8,512]{2,1,0:T(8,128)S(1)}) custom-call(f32[16,24,128]{2,1,0:T(8,128)S(1)} %bitcast_bitcast_fusion.wide, f32[24,512]{1,0:T(8,128)S(1)} %select_maximum_fusion.2.heads), custom_call_target="tpu_custom_call" | custom-call | tf_op jit(solution)/shard_map/finish/pallas_call | solution.py:779
  666.6 18.1 %exchange_8.1 = bf16[2,128,2560]{2,1,0:T(8,128)(2,1)S(1)} custom-call(bf16[2,128,2560]{2,1,0:T(8,128)(2,1)S(1)} %bitcast.340), custom_call_target="tpu_custom_call" | custom-call | tf_op jit(solution)/shard_map/exchange_8/pallas_call | solution.py:255
  694.5 15.5 %reduce-scatter.9.cloned.1.call-done = bf16[1,2,128,1408]{3,2,1,0:T(8,128)(2,1)} async-done(((bf16[4,2,128,1408]{3,2,1,0:T(8,128)(2,1)}), bf16[1,2,128,1408]{3,2,1,0:T(8,128)(2,1)}) %reduce-scatter.9.cloned.1.call-update) | async-done | bytes 720912 | tf_op jit(solution)/shard_map/reduce_scatter | solution.py:578
  710.0 104.5 %reduce-scatter.11.cloned.1.call-done = bf16[1,2,128,2816]{3,2,1,0:T(8,128)(2,1)} async-done(((bf16[4,2,128,2816]{3,2,1,0:T(8,128)(2,1)}), bf16[1,2,128,2816]{3,2,1,0:T(8,128)(2,1)}) %reduce-scatter.11.cloned.1.call-update) | async-done | bytes 1441808 | tf_op jit(solution)/shard_map/reduce_scatter | solution.py:578
  817.0 27.8 %exchange_7.1 = (bf16[2,128,1408]{2,1,0:T(8,128)(2,1)S(1)}, bf16[2,128,2816]{2,1,0:T(8,128)(2,1)S(1)}) custom-call(bf16[2,128,1408]{2,1,0:T(8,128)(2,1)S(1)} %bitcast.342, bf16[2,128,2816]{2,1,0:T(8,128)(2,1)S(1)} %bitcast.339), custom_call_target="tpu_custom_call" | custom-call | tf_op jit(solution)/shard_map/exchange_7/pallas_call | solution.py:255
  848.4 5.6 copy.170
  854.1 5.1 reshape.592
  (541 shorter events, 154.8 us)
Async XLA Ops:
  7.2 112.3 %copy-start = (bf16[16,1024]{1,0:T(8,128)(2,1)S(1)}, bf16[16,1024]{1,0:T(8,128)(2,1)}, u32[]{:S(2)}) copy-start(bf16[16,1024]{1,0:T(8,128)(2,1)} %param.28) | copy-start | bytes 98308
  7.2 135.4 %all-gather.8.cloned.1.call-start = ((), (), s32[]{:S(2)}) async-start(), calls=%async_computation.9 | async-start | bytes 6553600 | tf_op jit(solution)/shard_map/all_gather | solution.py:861
  36.5 91.7 %copy-start.18 = (bf16[16,32,128]{2,1,0:T(8,128)(2,1)}, bf16[16,32,128]{2,1,0:T(8,128)(2,1)S(1)}, u32[]{:S(2)}) copy-start(bf16[16,32,128]{2,1,0:T(8,128)(2,1)S(1)} %get-tuple-element.79) | copy-start | bytes 393220
  36.5 264.2 %all-gather.10.cloned.1.call-start = ((), (), s32[]{:S(2)}) async-start(), calls=%async_computation.10 | async-start | bytes 10813440 | tf_op jit(solution)/shard_map/all_gather | solution.py:878
  41.1 78.2 %copy-start.162 = (f32[1024]{0:T(1024)S(1)}, f32[1024]{0:T(1024)}, u32[]{:S(2)}) copy-start(f32[1024]{0:T(1024)} %param.29) | copy-start | bytes 12292
  42.5 77.4 %copy-start.175 = (s32[13]{0:T(128)S(1)}, s32[13]{0:T(128)}, u32[]{:S(2)}) copy-start(s32[13]{0:T(128)} %param.23) | copy-start | bytes 160
  119.1 419.6 %reduce-scatter.5.cloned.1.call-start = ((), (), s32[]{:S(2)}) async-start(), calls=%async_computation.4 | async-start | bytes 2621440 | tf_op jit(solution)/shard_map/reduce_scatter | solution.py:951
  119.5 19.8 %collective-permute-start.1 = (f32[512]{0:T(512)S(1)}, f32[512]{0:T(512)S(1)}, u32[]{:S(2)}, u32[]{:S(2)}) collective-permute-start(f32[512]{0:T(512)S(1)} %dynamic_slice.36), channel_id=1, source_target_pairs={{0,1},{1,0},{2,3},{3,2},{4,5},{5,4},{6,7},{7,6},{8,9},{9,8},{10,11... | collective-permute-start | bytes 6152 | tf_op jit(solution)/shard_map/ppermute | solution.py:890
  119.5 19.8 %collective-permute-start = (bf16[16,512]{1,0:T(8,128)(2,1)S(1)}, bf16[16,512]{1,0:T(8,128)(2,1)S(1)}, u32[]{:S(2)}, u32[]{:S(2)}) collective-permute-start(bf16[16,512]{1,0:T(8,128)(2,1)S(1)} %constant_dynamic-slice_fusion), channel_id=1, source_target_pairs={{0,1},{1,0},{2,3},{3,2},{4,5},{5,4},{6,7},{7,6},{8,9},{9,8},{10,11... | collective-permute-start | bytes 49160 | tf_op jit(solution)/shard_map/ppermute | solution.py:889
  127.0 73.9 %copy-start.152 = (f32[128]{0:T(128)}, f32[128]{0:T(128)S(1)}, u32[]{:S(2)}) copy-start(f32[128]{0:T(128)S(1)} %get-tuple-element.243) | copy-start | bytes 1540
  127.0 73.9 %copy-start.158 = (f32[128]{0:T(128)}, f32[128]{0:T(128)S(1)}, u32[]{:S(2)}) copy-start(f32[128]{0:T(128)S(1)} %get-tuple-element.225) | copy-start | bytes 1540
  132.6 68.3 %copy-start.154 = (f32[128]{0:T(128)}, f32[128]{0:T(128)S(1)}, u32[]{:S(2)}) copy-start(f32[128]{0:T(128)S(1)} %get-tuple-element.222) | copy-start | bytes 1540
  132.6 68.3 %copy-start.156 = (f32[128]{0:T(128)}, f32[128]{0:T(128)S(1)}, u32[]{:S(2)}) copy-start(f32[128]{0:T(128)S(1)} %get-tuple-element.241) | copy-start | bytes 1540
  141.8 59.1 %copy-start.25 = (f32[4,128,512]{2,1,0:T(8,128)}, f32[4,128,512]{2,1,0:T(8,128)S(1)}, u32[]{:S(2)}) copy-start(f32[4,128,512]{2,1,0:T(8,128)S(1)} %convolution_bitcast_fusion) | copy-start | bytes 3145732
  141.9 59.1 %copy-start.123 = (f32[1,1,512]{2,1,0:T(1,128)}, f32[1,1,512]{2,1,0:T(1,128)S(1)}, u32[]{:S(2)}) copy-start(f32[1,1,512]{2,1,0:T(1,128)S(1)} %get-tuple-element.197) | copy-start | bytes 6148
  154.3 52.4 %copy-start.4 = (bf16[4,2,2,128,2560]{4,3,2,1,0:T(8,128)(2,1)}, bf16[4,2,2,128,2560]{4,3,2,1,0:T(8,128)(2,1)S(1)}, u32[]{:S(2)}) copy-start(bf16[4,2,2,128,2560]{4,3,2,1,0:T(8,128)(2,1)S(1)} %join_5.1) | copy-start | bytes 31457284
  158.9 45.4 %copy-start.77 = (bf16[512,2048]{1,0:T(8,128)(2,1)}, bf16[512,2048]{1,0:T(8,128)(2,1)S(1)}, u32[]{:S(2)}) copy-start(bf16[512,2048]{1,0:T(8,128)(2,1)S(1)} %get-tuple-element.228) | copy-start | bytes 6291460
  158.9 47.8 %copy-start.46 = (f32[512,2048]{1,0:T(8,128)}, f32[512,2048]{1,0:T(8,128)S(1)}, u32[]{:S(2)}) copy-start(f32[512,2048]{1,0:T(8,128)S(1)} %get-tuple-element.229) | copy-start | bytes 12582916
  206.7 205.0 %copy-start.143 = (f32[512]{0:T(512)}, f32[512]{0:T(512)S(1)}, u32[]{:S(2)}) copy-start(f32[512]{0:T(512)S(1)} %add_rsqrt_fusion) | copy-start | bytes 6148
  259.5 97.2 %copy-start.8 = (f32[128,2048]{1,0:T(8,128)}, f32[128,2048]{1,0:T(8,128)S(1)}, u32[]{:S(2)}) copy-start(f32[128,2048]{1,0:T(8,128)S(1)} %get-tuple-element.81.middle) | copy-start | bytes 3145732
  350.8 56.0 %copy-start.47 = (f32[512,2048]{1,0:T(8,128)S(1)}, f32[512,2048]{1,0:T(8,128)}, u32[]{:S(2)}) copy-start(f32[512,2048]{1,0:T(8,128)} %copy-done.46) | copy-start | bytes 12582916
  356.6 50.2 %copy-start.57 = (f32[128,512]{1,0:T(8,128)S(1)}, f32[128,512]{1,0:T(8,128)}, u32[]{:S(2)}) copy-start(f32[128,512]{1,0:T(8,128)} %copy-done.56) | copy-start | bytes 786436
  356.7 50.2 %copy-start.60 = (f32[128,512]{1,0:T(8,128)S(1)}, f32[128,512]{1,0:T(8,128)}, u32[]{:S(2)}) copy-start(f32[128,512]{1,0:T(8,128)} %copy-done.59) | copy-start | bytes 786436
  356.7 50.2 %copy-start.63 = (f32[128,512]{1,0:T(8,128)S(1)}, f32[128,512]{1,0:T(8,128)}, u32[]{:S(2)}) copy-start(f32[128,512]{1,0:T(8,128)} %copy-done.62) | copy-start | bytes 786436
  356.7 50.2 %copy-start.66 = (f32[128,512]{1,0:T(8,128)S(1)}, f32[128,512]{1,0:T(8,128)}, u32[]{:S(2)}) copy-start(f32[128,512]{1,0:T(8,128)} %copy-done.65) | copy-start | bytes 786436
  492.5 48.6 %collective-permute-start.2 = (bf16[4,2,128,2560]{3,2,1,0:T(8,128)(2,1)}, bf16[4,2,128,2560]{3,2,1,0:T(8,128)(2,1)}, u32[]{:S(2)}, u32[]{:S(2)}) collective-permute-start(bf16[4,2,128,2560]{3,2,1,0:T(8,128)(2,1)} %fusion.8), channel_id=1, source_target_pairs={{0,1},{1,0},{2,3},{3,2},{4,5},{5,4},{6,7},{7,6},{8,9},{9,8},{10,11... | collective-permute-start | bytes 15728648 | tf_op jit(solution)/shard_map/ppermute | solution.py:576
  500.2 165.1 %all-gather.6.cloned.1.call-start = ((), (), s32[]{:S(2)}) async-start(), calls=%async_computation.5 | async-start | bytes 1572864 | tf_op jit(solution)/shard_map/all_gather | solution.py:952
  541.0 124.3 %reduce-scatter.7.cloned.1.call-start = ((), (), s32[]{:S(2)}) async-start(), calls=%async_computation.6 | async-start | bytes 6553600 | tf_op jit(solution)/shard_map/reduce_scatter | solution.py:578
  549.3 160.7 %reduce-scatter.9.cloned.1.call-start = ((), (), s32[]{:S(2)}) async-start(), calls=%async_computation.7 | async-start | bytes 3604480 | tf_op jit(solution)/shard_map/reduce_scatter | solution.py:578
  556.9 15.1 %collective-permute-start.3 = (bf16[4,2,128,1408]{3,2,1,0:T(8,128)(2,1)}, bf16[4,2,128,1408]{3,2,1,0:T(8,128)(2,1)}, u32[]{:S(2)}, u32[]{:S(2)}) collective-permute-start(bf16[4,2,128,1408]{3,2,1,0:T(8,128)(2,1)} %dynamic-slice_bitcast_fusion.1), channel_id=1, source_target_pairs={{0,1},{1,0},{2,3},{3,2},{4,5},{5,4},{6,7},{7,6},{8,9},{9,8},{10,11... | collective-permute-start | bytes 8650760 | tf_op jit(solution)/shard_map/ppermute | solution.py:576
  571.9 9.8 %collective-permute-start.4 = (bf16[4,2,128,2816]{3,2,1,0:T(8,128)(2,1)}, bf16[4,2,128,2816]{3,2,1,0:T(8,128)(2,1)}, u32[]{:S(2)}, u32[]{:S(2)}) collective-permute-start(bf16[4,2,128,2816]{3,2,1,0:T(8,128)(2,1)} %dynamic-slice_bitcast_fusion), channel_id=1, source_target_pairs={{0,1},{1,0},{2,3},{3,2},{4,5},{5,4},{6,7},{7,6},{8,9},{9,8},{10,11... | collective-permute-start | bytes 17301512 | tf_op jit(solution)/shard_map/ppermute | solution.py:576
  576.1 238.4 %reduce-scatter.11.cloned.1.call-start = ((), (), s32[]{:S(2)}) async-start(), calls=%async_computation.8 | async-start | bytes 7208960 | tf_op jit(solution)/shard_map/reduce_scatter | solution.py:578
  (159 other events, 1313.0 us)
Sparse Core Ops, SparseCore 0:
  36.6 95.9 all-gather.7
  134.7 165.9 all-gather.9
  500.3 38.3 reduce-scatter.4
  541.1 9.0 all-gather.5
  552.4 95.8 reduce-scatter.6
  651.1 58.7 reduce-scatter.8
  712.4 102.0 reduce-scatter.10

commit v3 on v1

v3 whole, which is shorter than its diff:
```python
import functools

import jax
import jax.numpy as jnp
from jax import lax
from jax.experimental import pallas as pl
from jax.experimental.pallas import tpu as pltpu
from jax.sharding import Mesh, PartitionSpec as P

HD = 512
CHUNK = 128
EPSILON = 1e-06
HEAD_FLOOR = 1.0
TEAM = 4

BF = jnp.bfloat16
F32 = jnp.float32
MESH = pl.DeviceIdType.MESH
ANY = pl.BlockSpec(memory_space=pl.ANY)
VMEM = pl.BlockSpec(memory_space=pltpu.VMEM)
DMA = pltpu.SemaphoreType.DMA

SEQ = ("zh", "zl", "y", "x")
FLIPS = ((1, 1), (0, 1), (1, 0), (0, 0))


def dot(a, b):
    return jnp.dot(a, b, preferred_element_type=F32)


def dot_rows(a, b):
    return lax.dot_general(a, b, (((0,), (0,)), ((), ())), preferred_element_type=F32)


def dot_last(a, b):
    return lax.dot_general(a, b, (((1,), (1,)), ((), ())), preferred_element_type=F32)


def low(v):
    return v.astype(BF)


def flip(index, by):
    return 1 - index if by else index


class Place:
    def __init__(self):
        self.zl, self.x, self.c = lax.axis_index("zl"), lax.axis_index("x"), lax.axis_index("c")
        self.member = self.zl * 2 + self.x


def greet_team(me, more=0):
    barrier = pltpu.get_barrier_semaphore()
    for n in range(1, 8):
        to = {"zl": flip(me.zl, n & 1), "x": flip(me.x, n & 2), "c": flip(me.c, n & 4)}
        pl.semaphore_signal(barrier, inc=1, device_id=to, device_id_type=MESH)
    pl.semaphore_wait(barrier, 7 + more)


def others(me):
    zh, y, highs = lax.axis_index("zh"), lax.axis_index("y"), lax.axis_size("zh")
    for k in range(highs):
        for n in range(8):
            yield lax.rem(zh + k, highs), flip(me.zl, n & 1), flip(y, n & 2), flip(me.x, n & 4), k + n == 0


def greet_all(me):
    barrier = pltpu.get_barrier_semaphore()
    count = 0
    for zh, zl, y, x, own in others(me):
        for f in range(2):
            if own and not f:
                continue
            to = {"zh": zh, "zl": zl, "y": y, "x": x, "c": flip(me.c, f)}
            pl.semaphore_signal(barrier, inc=1, device_id=to, device_id_type=MESH)
            count += 1
    pl.semaphore_wait(barrier, count)


def route_member(me):
    out, arrive = [], []
    for fz, fx in FLIPS:
        zl, x = flip(me.zl, fz), flip(me.x, fx)
        own = (fz, fx) == (0, 0)
        out.append((zl * 2 + x, me.member, {"zl": zl, "x": x}, own))
        arrive.append((zl * 2 + x, own))
    return out, arrive


def chip_index(zh, zl, y, x):
    return ((zh * 2 + zl) * 2 + y) * 2 + x


def route_all(me):
    mine = chip_index(lax.axis_index("zh"), me.zl, lax.axis_index("y"), me.x)
    out, arrive = [], []
    for zh, zl, y, x, own in others(me):
        chip = chip_index(zh, zl, y, x)
        out.append((chip, mine, {"zh": zh, "zl": zl, "y": y, "x": x}, own))
        arrive.append((chip, own))
    return out, arrive


def route_halves(me):
    mine = me.c == me.zl
    out, arrive = [], []
    for fz, fx in FLIPS:
        zl, x = flip(me.zl, fz), flip(me.x, fx)
        own = mine if (fz, fx) == (0, 0) else False
        out.append((0, me.x * 2 + me.c, {"zl": zl, "x": x, "c": me.zl}, own))
    for fc, fx in FLIPS:
        c, x = flip(me.c, fc), flip(me.x, fx)
        own = mine if (fc, fx) == (0, 0) else False
        arrive.append((x * 2 + c, own))
    return out, arrive


def route_owners(me):
    mine = me.c == me.zl
    out, arrive = [], []
    for fc, fx in FLIPS:
        c, x = flip(me.c, fc), flip(me.x, fx)
        own = mine if (fc, fx) == (0, 0) else False
        out.append((x * 2 + c, me.member, {"zl": me.c, "x": x, "c": c}, own))
    for fz, fx in FLIPS:
        zl, x = flip(me.zl, fz), flip(me.x, fx)
        own = mine if (fz, fx) == (0, 0) else False
        arrive.append((zl * 2 + x, own))
    return out, arrive


def route_weights(me):
    mine = (me.c == me.zl) & (me.c == me.x)
    out, arrive = [], []
    for f in (1, 0):
        x = flip(me.x, f)
        own = (me.c == me.zl) & (me.c == x) & (me.x == me.c) if not f else False
        out.append((x, me.zl, {"zl": me.c, "x": x, "c": me.x}, own))
    for f in (1, 0):
        zl = flip(me.zl, f)
        own = mine if not f else False
        arrive.append((zl, own))
    return out, arrive


def route_weights_home(me):
    mine = (me.c == me.zl) & (me.c == me.x)
    out, arrive = [], []
    for f in (1, 0):
        zl = flip(me.zl, f)
        own = mine if not f else False
        out.append((zl, me.x, {"zl": zl, "x": me.c, "c": me.zl}, own))
    for f in (1, 0):
        x = flip(me.x, f)
        own = mine if not f else False
        arrive.append((x, own))
    return out, arrive


def when(condition, run):
    if condition is True:
        run()
    elif condition is not False:
        pl.when(condition)(run)


def unless(condition, run):
    if condition is False:
        run()
    elif condition is not True:
        pl.when(jnp.logical_not(condition))(run)


class Transfer:
    def __init__(self, route, source, target, send, arrive):
        self.route, self.source, self.target, self.send, self.arrive = route, source, target, send, arrive

    def _remote(self, n):
        index, slot, to, own = self.route[0][n]
        return pltpu.make_async_remote_copy(
            src_ref=self.source(index),
            dst_ref=self.target(slot),
            send_sem=self.send.at[n],
            recv_sem=self.arrive.at[slot],
            device_id=to,
            device_id_type=MESH,
        )

    def _local(self, n):
        index, slot, to, own = self.route[0][n]
        return pltpu.make_async_copy(self.source(index), self.target(slot), self.send.at[n])

    def start(self):
        for n, (_, _, _, own) in enumerate(self.route[0]):
            unless(own, lambda: self._remote(n).start())
            when(own, lambda: self._local(n).start())

    def wait_arrive(self):
        for slot, own in self.route[1]:
            ref = self.target(slot)

            def arrived():
                pltpu.make_async_copy(ref, ref, self.arrive.at[slot]).wait()

            unless(own, arrived)

    def wait_local(self):
        for n, (_, _, _, own) in enumerate(self.route[0]):
            when(own, lambda: self._local(n).wait())

    def wait_sent(self):
        for n, (_, _, _, own) in enumerate(self.route[0]):
            unless(own, lambda: self._remote(n).wait_send())

    def wait(self):
        self.wait_arrive()
        self.wait_local()
        self.wait_sent()


def copy_to(src, dst, send, arrive, to):
    return pltpu.make_async_remote_copy(
        src_ref=src, dst_ref=dst, send_sem=send, recv_sem=arrive, device_id=to, device_id_type=MESH
    )


def wait_for(ref, sem):
    pltpu.make_async_copy(ref, ref, sem).wait()


def member_slots(me, two):
    along = me.zl * 2 + 1 - me.x, {"x": 1 - me.x}
    over = (1 - me.zl) * 2 + me.x, {"zl": 1 - me.zl}
    one, double = (over, along) if two == "x" else (along, over)
    return one[0], double[0], (1 - me.zl) * 2 + 1 - me.x, one[1], double[1]


class MemberSpread:
    def __init__(self, me, source, target, send, arrive, two="x"):
        self.target, self.arrive = target, arrive
        mine = me.member
        one, double, across, to_one, to_double = member_slots(me, two)
        self.slots = one, double, across
        self.direct = [
            copy_to(source, target(mine), send.at[0], arrive.at[mine], to_one),
            copy_to(source, target(mine), send.at[1], arrive.at[mine], to_double),
        ]
        self.local = pltpu.make_async_copy(source, target(mine), arrive.at[mine])
        self.forward = copy_to(target(one), target(one), send.at[2], arrive.at[one], to_double)

    def start(self):
        for copy in self.direct:
            copy.start()
        self.local.start()

    def relay(self):
        wait_for(self.target(self.slots[0]), self.arrive.at[self.slots[0]])
        self.forward.start()

    def wait(self):
        for slot in self.slots[1:]:
            wait_for(self.target(slot), self.arrive.at[slot])
        self.local.wait()
        for copy in self.direct + [self.forward]:
            copy.wait_send()


class HalvesSpread:
    def __init__(self, me, source, target, send, arrive):
        self.me, self.target, self.arrive = me, target, arrive
        mine = me.x * 2 + me.c
        self.home = me.c == me.zl
        self.direct = [
            copy_to(source, target(mine), send.at[0], arrive.at[mine], {"zl": 1 - me.zl, "c": me.zl}),
            copy_to(source, target(mine), send.at[1], arrive.at[mine], {"x": 1 - me.x, "c": me.zl}),
        ]
        self.near = copy_to(source, target(mine), send.at[2], arrive.at[mine], {"c": 1 - me.c})
        self.local = pltpu.make_async_copy(source, target(mine), send.at[2])
        self.near_slots = [me.x * 2 + c for c in range(2)]
        self.far_slots = [(1 - me.x) * 2 + c for c in range(2)]
        self.forwards = [
            copy_to(target(slot), target(slot), send.at[3 + c], arrive.at[slot], {"x": 1 - me.x})
            for c, slot in enumerate(self.near_slots)
        ]

    def start(self):
        for copy in self.direct:
            copy.start()
        pl.when(self.home)(self.local.start)
        unless(self.home, self.near.start)

    def relay(self):
        @pl.when(jnp.logical_not(self.home))
        def _():
            for slot, forward in zip(self.near_slots, self.forwards):
                wait_for(self.target(slot), self.arrive.at[slot])
                forward.start()

    def wait(self):
        me = self.me

        @pl.when(self.home)
        def _():
            self.local.wait()
            slot = me.x * 2 + 1 - me.c
            wait_for(self.target(slot), self.arrive.at[slot])

        for slot in self.far_slots:
            wait_for(self.target(slot), self.arrive.at[slot])
        for copy in self.direct:
            copy.wait_send()

        @pl.when(jnp.logical_not(self.home))
        def _():
            self.near.wait_send()
            for forward in self.forwards:
                forward.wait_send()


class MemberSum:
    def __init__(self, me, source, got, relayed, staged, send, arrive, two="x"):
        self.me, self.source, self.got, self.relayed, self.staged = me, source, got, relayed, staged
        self.arrive = arrive
        self.one, double, across, to_one, to_double = member_slots(me, two)
        self.direct = [
            copy_to(source(across), relayed(0), send.at[0], arrive.at[0], to_double),
            copy_to(source(double), got(0), send.at[1], arrive.at[1], to_double),
        ]
        self.onward = copy_to(staged(0), got(1), send.at[2], arrive.at[2], to_one)

    def start(self):
        for copy in self.direct:
            copy.start()

    def relay(self):
        wait_for(self.relayed(0), self.arrive.at[0])
        own = self.source(self.one)[...].astype(F32)
        self.staged(0)[...] = low(own + self.relayed(0)[...].astype(F32))
        self.onward.start()

    def total(self):
        wait_for(self.got(0), self.arrive.at[1])
        wait_for(self.got(1), self.arrive.at[2])
        total = self.source(self.me.member)[...].astype(F32)
        return total + self.got(0)[...].astype(F32) + self.got(1)[...].astype(F32)

    def wait_sent(self):
        for copy in self.direct + [self.onward]:
            copy.wait_send()


class OwnersSum:
    def __init__(self, me, source, got, relayed, staged, send, arrive):
        self.me, self.source, self.got, self.relayed, self.staged = me, source, got, relayed, staged
        self.arrive = arrive
        self.home = me.c == me.zl
        mine, other = me.x * 2, (1 - me.x) * 2
        self.near = copy_to(source(mine + 1 - me.c), got(0), send.at[0], arrive.at[0], {"c": 1 - me.c})
        self.local = pltpu.make_async_copy(source(mine + me.c), got(0), send.at[1])
        self.across = [
            copy_to(source(other + c), got(1), send.at[2 + c], arrive.at[1], {"x": 1 - me.x, "c": c})
            for c in range(2)
        ]
        self.first = [
            copy_to(source(other + c), relayed(c), send.at[2 + c], arrive.at[3 + c], {"x": 1 - me.x})
            for c in range(2)
        ]
        self.onward = [
            copy_to(staged(c), got(2), send.at[4 + c], arrive.at[2], {"zl": me.c, "c": c})
            for c in range(2)
        ]

    def start(self):
        @pl.when(self.home)
        def _():
            for copy in self.across + [self.near, self.local]:
                copy.start()

        @pl.when(jnp.logical_not(self.home))
        def _():
            for copy in self.first:
                copy.start()

    def relay(self):
        @pl.when(jnp.logical_not(self.home))
        def _():
            for c in range(2):
                wait_for(self.relayed(c), self.arrive.at[3 + c])
                own = self.source(self.me.x * 2 + c)[...].astype(F32)
                self.staged(c)[...] = low(own + self.relayed(c)[...].astype(F32))
                self.onward[c].start()

    def total(self):
        pl.when(self.home)(self.local.wait)
        unless(self.home, lambda: wait_for(self.got(0), self.arrive.at[0]))
        wait_for(self.got(1), self.arrive.at[1])
        wait_for(self.got(2), self.arrive.at[2])
        return sum(self.got(k)[...].astype(F32) for k in range(3))

    def wait_sent(self):
        @pl.when(self.home)
        def _():
            for copy in self.across + [self.near]:
                copy.wait_send()

        @pl.when(jnp.logical_not(self.home))
        def _():
            for copy in self.first + self.onward:
                copy.wait_send()


class Placed(Transfer):
    def __init__(self, route, source, there, target, send, arrive):
        super().__init__(route, source, target, send, arrive)
        self.there = there

    def _remote(self, n):
        index, slot, to, own = self.route[0][n]
        return pltpu.make_async_remote_copy(
            src_ref=self.source(index),
            dst_ref=self.there(slot),
            send_sem=self.send.at[n],
            recv_sem=self.arrive.at[slot],
            device_id=to,
            device_id_type=MESH,
        )


LANES = 128


def keyed_mask(start, starts_row, starts_column):
    rows = lax.broadcasted_iota(jnp.int32, (CHUNK, CHUNK), 0)
    columns = lax.broadcasted_iota(jnp.int32, (CHUNK, CHUNK), 1)
    ids = jnp.sum((rows + start >= starts_row[0:1]).astype(F32), axis=1, keepdims=True)
    places = lax.broadcasted_iota(jnp.int32, starts_column.shape, 1)
    ids_row = jnp.sum((places + start >= starts_column[...]).astype(F32), axis=0, keepdims=True)
    before = jnp.sum((starts_row[0:1] < start).astype(F32), axis=1, keepdims=True)
    final = ids_row[:, CHUNK - 1 :]
    pair = (rows >= columns) & (ids == ids_row)
    visible = (ids == before).astype(F32)
    keep = (final == before).astype(F32)
    return pair, visible, keep, (ids == final).astype(F32)


class StatePass:
    def __init__(self, back, local, decay, out, rounded, got, got_decay, sums, sum_decays, stage, stage_decay,
                 entering, leave, enter, send, arrive, far_send, far_arrive, leave_send, leave_arrive):
        self.__dict__.update(locals())
        self.zh, c, y = lax.axis_index("zh"), lax.axis_index("c"), lax.axis_index("y")
        self.highs = lax.axis_size("zh")
        self.mine = c * 2 + y
        self.quarter = local.shape[0] // 4
        self.partners = []
        for fc, fy in ((1, 1), (0, 1), (1, 0)):
            to_c, to_y = flip(c, fc), flip(y, fy)
            self.partners.append((to_c * 2 + to_y, {"c": to_c, "y": to_y}))
        self.order = range(3, -1, -1) if back else range(4)
        self.moves, self.outs = [], []

    def begin(self):
        self.rounded[...] = low(self.local[...])
        for n, (index, to) in enumerate(self.partners):
            rows = self.rounded.at[pl.ds(index * self.quarter, self.quarter)]
            self.moves.append(copy_to(rows, self.got.at[self.mine], self.send.at[0, n], self.arrive.at[0, self.mine], to))
            self.moves.append(
                copy_to(self.decay, self.got_decay.at[self.mine], self.send.at[1, n], self.arrive.at[1, self.mine], to)
            )
        for move in self.moves:
            move.start()
        self.got[self.mine] = self.rounded[pl.ds(self.mine * self.quarter, self.quarter)]
        self.got_decay[self.mine] = self.decay[...]

    def needs(self, source, target):
        return (source > target) if self.back else (source < target)

    def far(self, n, to):
        zh = self.zh
        return (
            copy_to(self.stage, self.sums.at[zh], self.far_send.at[0, n], self.far_arrive.at[0, zh], {"zh": to}),
            copy_to(
                self.stage_decay, self.sum_decays.at[zh], self.far_send.at[1, n], self.far_arrive.at[1, zh], {"zh": to}
            ),
        )

    def combine(self):
        for index, _ in self.partners:
            wait_for(self.got.at[index], self.arrive.at[0, index])
            wait_for(self.got_decay.at[index], self.arrive.at[1, index])
        total, total_decay = None, None
        for k in self.order:
            piece, d = self.got[k].astype(F32), self.got_decay[k][:1]
            total = piece if total is None else d * total + piece
            total_decay = d if total_decay is None else total_decay * d
        self.stage[...] = low(total)
        self.stage_decay[...] = jnp.broadcast_to(total_decay, self.stage_decay.shape)
        for n in range(1, self.highs):
            to = lax.rem(self.zh + n, self.highs)

            @pl.when(self.needs(self.zh, to))
            def _(n=n, to=to):
                for move in self.far(n, to):
                    move.start()

    def spread(self):
        self.entering[...] = jnp.zeros_like(self.entering)
        for n in range(self.highs):
            k = self.highs - 1 - n if self.back else n

            @pl.when(self.needs(k, self.zh))
            def _(k=k):
                wait_for(self.sums.at[k], self.far_arrive.at[0, k])
                wait_for(self.sum_decays.at[k], self.far_arrive.at[1, k])
                self.entering[...] = self.sum_decays[k][:1] * self.entering[...] + self.sums[k].astype(F32)

        state = self.entering[...]
        for k in self.order:
            self.leave[k] = low(state)
            state = self.got_decay[k][:1] * state + self.got[k].astype(F32)
        for n, (index, to) in enumerate(self.partners):
            self.outs.append(
                copy_to(
                    self.leave.at[index], self.enter.at[self.mine], self.leave_send.at[n],
                    self.leave_arrive.at[self.mine], to,
                )
            )
        for move in self.outs:
            move.start()
        self.enter[self.mine] = self.leave[self.mine]

    def finish(self):
        for index, _ in self.partners:
            wait_for(self.enter.at[index], self.leave_arrive.at[index])
        for k in range(4):
            self.out[pl.ds(k * self.quarter, self.quarter)] = self.enter[k].astype(F32)

    def wait_sent(self):
        for move in self.moves + self.outs:
            move.wait_send()
        for n in range(1, self.highs):
            to = lax.rem(self.zh + n, self.highs)

            @pl.when(self.needs(self.zh, to))
            def _(n=n, to=to):
                for move in self.far(n, to):
                    move.wait_send()


def state_pass_scratch(highs):
    quarter = HD // 4
    return [
        pltpu.VMEM((HD, HD), BF),
        pltpu.VMEM((4, quarter, HD), BF),
        pltpu.VMEM((4, 8, HD), F32),
        pltpu.VMEM((highs, quarter, HD), BF),
        pltpu.VMEM((highs, 8, HD), F32),
        pltpu.VMEM((quarter, HD), BF),
        pltpu.VMEM((8, HD), F32),
        pltpu.VMEM((quarter, HD), F32),
        pltpu.VMEM((4, quarter, HD), BF),
        pltpu.VMEM((4, quarter, HD), BF),
        DMA((2, 3)),
        DMA((2, 4)),
        DMA((2, highs)),
        DMA((2, highs)),
        DMA((3,)),
        DMA((4,)),
    ]


STATE_REFS = 16


def forward_kernel(*refs):
    (
        mixer_in, mixer_out, ffn_in, ffn_out, small, ups, own, cot, starts_row, starts_column, head_gain,
        mixer_w, merge_w, pair_w, down_w, gains, cots, hidden, low_rank, gate, cumulated, projected, mixed, gated,
        befores, decay, second, middle,
        mixer_v, merge_v, projected_v, befores_v, inputs, smalls, ups_got, columns, state, partial, got, relayed, staged, line,
        own_send, own_arrive, far_send, arrive, small_send, small_arrive, ups_sem, inputs_send, inputs_arrive,
        cot_send, cot_arrive, sum_send, sum_arrive, spread_send, spread_arrive, saves,
    ) = refs[:-STATE_REFS]
    me = Place()
    zh, y, highs = lax.axis_index("zh"), lax.axis_index("y"), lax.axis_size("zh")
    units = down_w.shape[-1]
    width = own.shape[1]
    chunks = hidden.shape[0]
    first = ((zh * 2 + me.c) * 2 + y) * (chunks * CHUNK)
    greet_all(me)
    twin, side = {"c": 1 - me.c}, {"y": 1 - y}

    def own_source(part, k):
        if part < 5:
            at = pl.ds(pl.multiple_of(k * HD, HD), HD)
            return mixer_out.at[:, at] if part == 4 else mixer_in.at[part, :, at]
        at = pl.ds(pl.multiple_of(k * units, LANES), units)
        return ffn_out.at[:, at] if part == 7 else ffn_in.at[part - 5, :, at]

    def piece(at_zh, at_y, x, part, zl=slice(None)):
        if part < 4:
            return mixer_v.at[at_zh, zl, at_y, x, :, pl.ds(part * HD, HD)]
        if part == 4:
            return merge_v.at[at_zh, zl, at_y, x]
        if part < 7:
            return pair_w.at[at_zh, zl, at_y, x, :, pl.ds((part - 5) * units, units)]
        return down_w.at[at_zh, zl, at_y, x]

    firsts = [
        Placed(
            route_weights(me),
            lambda k, p=p: own_source(p, k),
            lambda zl, p=p: piece(zh, y, me.x, p, zl),
            lambda zl, p=p: piece(zh, y, me.c, p, zl),
            own_send.at[p],
            own_arrive.at[p],
        )
        for p in range(8)
    ]
    count = [0]
    sent = []

    def forward(at_zh, at_y, part, to):
        place = piece(at_zh, at_y, me.c, part)
        copy = copy_to(place, place, far_send.at[count[0]], arrive.at[at_zh, at_y, me.c, part], to)
        copy.start()
        count[0] += 1
        sent.append(copy)

    def arrived(at_zh, at_y, x, part):
        wait_for(piece(at_zh, at_y, x, part), arrive.at[at_zh, at_y, x, part])

    def send_own(part):
        firsts[part].wait_arrive()
        firsts[part].wait_local()
        for k in range(1, highs):
            forward(zh, y, part, {"zh": lax.rem(zh + k, highs)})
        forward(zh, y, part, side)
        forward(zh, y, part, twin)

    def pass_high(part):
        for k in range(1, highs):
            at_zh = lax.rem(zh + k, highs)
            arrived(at_zh, y, me.c, part)
            forward(at_zh, y, part, side)
            forward(at_zh, y, part, twin)

    def pass_side(part):
        for k in range(highs):
            at_zh = lax.rem(zh + k, highs)
            arrived(at_zh, 1 - y, me.c, part)
            forward(at_zh, 1 - y, part, twin)

    def complete(part):
        for k in range(highs):
            at_zh = lax.rem(zh + k, highs)
            arrived(at_zh, y, 1 - me.c, part)
            arrived(at_zh, 1 - y, 1 - me.c, part)

    save_count = [0]
    saved = []

    def save(source, target):
        copy = pltpu.make_async_copy(source, target, saves.at[save_count[0]])
        copy.start()
        save_count[0] += 1
        saved.append(copy)

    order = (1, 2, 0, 3, 4)
    for part in order:
        firsts[part].start()
    move_small = Transfer(route_all(me), lambda _: small, lambda k: smalls.at[k], small_send, small_arrive)
    move_small.start()
    lend = copy_to(ups, ups_got, ups_sem.at[0], ups_sem.at[1], twin)
    lend.start()
    for part in order:
        send_own(part)
    move_inputs = HalvesSpread(me, own, lambda k: inputs.at[k], inputs_send, inputs_arrive)
    move_cot = MemberSpread(me, cot, lambda k: cots.at[k], cot_send, cot_arrive)
    move_inputs.start()
    for part in (5, 6, 7):
        firsts[part].start()
    move_inputs.relay()
    pass_high(1)
    move_small.wait()
    lend.wait()
    owner_rows = smalls.shape[1]
    for n in range(smalls.shape[0]):
        columns[pl.ds(n * owner_rows, owner_rows)] = smalls[n].astype(F32)
    gains[...] = columns[...].T
    pass_high(2)
    move_inputs.wait()

    up = jnp.where(me.c == me.zl, ups[...], ups_got[...])
    rank_up, bias = low(up[:16]), up[16:17]
    down = low(columns[...])
    lower = (
        lax.broadcasted_iota(jnp.int32, (CHUNK, CHUNK), 0)
        >= lax.broadcasted_iota(jnp.int32, (CHUNK, CHUNK), 1)
    ).astype(F32)

    def gates_step(n, _):
        x = inputs[n].astype(F32)
        scale = lax.rsqrt(jnp.mean(x * x, -1, keepdims=True) + EPSILON)
        h = low(x * scale * gains[0:1])
        hidden[n] = h
        z = low(dot(h, down))
        low_rank[n] = z
        a = dot(z[:, 2:18], rank_up) + bias
        gate[n] = a
        log_gate = (jnp.minimum(a, 0.0) - jnp.log1p(jnp.exp(-jnp.abs(a)))) / 16.0
        cumulated[n] = jnp.dot(
            lower, log_gate, precision=lax.Precision.HIGHEST, preferred_element_type=F32
        )
        return 0

    lax.fori_loop(0, chunks, gates_step, 0)

    def project(part):
        rows = hidden[...].reshape(chunks * CHUNK, width)
        block = mixer_v[:, :, :, :, :, pl.ds(part * HD, HD)].reshape(width, HD)
        result = dot(rows, block)
        if part == 0:
            result = result * HD ** (-0.5)
        projected_v[part] = result.reshape(chunks, CHUNK, HD)
        save(projected_v.at[part], projected.at[part])

    pass_side(1)
    pass_side(2)
    pass_high(0)
    complete(1)
    project(1)
    complete(2)
    project(2)
    pass_high(3)

    state[...] = jnp.zeros_like(state)
    decay[...] = jnp.ones_like(decay)

    def masks(n):
        return keyed_mask(first + n * CHUNK, starts_row, starts_column)

    def local_step(n, _):
        _, _, keep, last = masks(n)
        b = cumulated[n]
        end = b[CHUNK - 1 :]
        kc = low(projected_v[1, n] * jnp.exp(end - b) * last)
        update = dot_rows(low(projected_v[2, n]), kc)
        befores_v[n] = update
        carry = keep * jnp.exp(end)
        state[...] = carry * state[...] + update
        decay[...] = decay[...] * carry
        return 0

    lax.fori_loop(0, chunks, local_step, 0)
    states = StatePass(False, state, decay, state, *refs[-STATE_REFS:])
    states.begin()
    pass_side(0)
    pass_high(4)
    for part in (5, 6, 7):
        send_own(part)
    complete(0)
    project(0)
    states.combine()
    pass_side(3)
    pass_side(4)

    def inner_step(n, _):
        pair, _, _, _ = masks(n)
        b = cumulated[n]
        mid = b[CHUNK // 2 - 1 : CHUNK // 2]
        qh = low(projected_v[0, n] * jnp.exp(b - mid))
        kh = low(projected_v[1, n] * jnp.exp(mid - b))
        scores = low(jnp.where(pair, dot_last(qh, kh), 0.0))
        mixed[n] = dot(scores, low(projected_v[2, n]))
        return 0

    lax.fori_loop(0, chunks, inner_step, 0)
    states.spread()
    complete(3)
    project(3)
    states.finish()

    def outer_step(n, _):
        _, visible, keep, _ = masks(n)
        b = cumulated[n]
        before = state[...]
        qd = low(projected_v[0, n] * jnp.exp(b) * visible)
        out = mixed[n] + dot_last(qd, low(before))
        mixed[n] = out
        update = befores_v[n]
        befores_v[n] = before
        state[...] = keep * jnp.exp(b[CHUNK - 1 :]) * before + update
        scale = lax.rsqrt(jnp.mean(out * out, -1, keepdims=True) + HEAD_FLOOR)
        u = projected_v[3, n]
        gated[n] = low(out * scale * head_gain[...] * (u * jax.nn.sigmoid(u)))
        return 0

    lax.fori_loop(0, chunks, outer_step, 0)
    save(befores_v, befores)
    complete(4)

    def merge_step(n, _):
        partial[n] = low(dot_last(gated[n], merge_v[...].reshape(width, HD)))
        return 0

    lax.fori_loop(0, chunks, merge_step, 0)

    steps = sum_send.shape[0]
    rows = own.shape[0] // steps

    def rows_of(ref, k, n):
        return ref.at[k, pl.ds(n * rows, rows)]

    sums = [
        OwnersSum(
            me,
            lambda k, n=n: rows_of(partial, k, n),
            lambda k, n=n: rows_of(got, k, n),
            lambda k, n=n: rows_of(relayed, k, n),
            lambda k, n=n: rows_of(staged, k, n),
            sum_send.at[n],
            sum_arrive.at[n],
        )
        for n in range(steps)
    ]
    spreads = [
        MemberSpread(
            me,
            line.at[pl.ds(n * rows, rows)],
            lambda k, n=n: rows_of(second, k, n),
            spread_send.at[n],
            spread_arrive.at[n],
        )
        for n in range(steps)
    ]
    for transfer in sums:
        transfer.start()
    pass_high(5)
    for transfer in sums:
        transfer.relay()
    for n in range(steps):
        at = pl.ds(n * rows, rows)
        total = own[at].astype(F32) + sums[n].total()
        middle[at] = total
        scale = lax.rsqrt(jnp.mean(total * total, -1, keepdims=True) + EPSILON)
        line[at] = low(total * scale * gains[1:2])
        spreads[n].start()
        if n:
            spreads[n - 1].relay()
    spreads[steps - 1].relay()
    move_cot.start()
    save(mixer_v, mixer_w)
    save(merge_v, merge_w)
    pass_high(6)
    pass_side(5)
    move_cot.relay()
    pass_high(7)
    for part in (6, 7):
        pass_side(part)
    for part in (5, 6, 7):
        complete(part)
    for transfer in sums:
        transfer.wait_sent()
    for transfer in spreads:
        transfer.wait()
    states.wait_sent()
    move_cot.wait()
    for transfer in firsts:
        transfer.wait_sent()
    for copy in sent:
        copy.wait_send()
    for copy in saved:
        copy.wait()


def starts_arrays(starts):
    starts = jnp.pad(starts, (0, LANES - starts.shape[0]), constant_values=jnp.int32(1 << 30))
    return jnp.broadcast_to(starts[None], (8, LANES)), jnp.broadcast_to(starts[:16, None], (16, LANES))


def forward(mixer_in, mixer_out, ffn_in, ffn_out, small, ups, own, cot, starts, head_gain):
    highs = lax.axis_size("zh")
    chips = highs * 8
    rows, half, width = small.shape[0], own.shape[0], own.shape[1]
    units = ffn_out.shape[1] // 2
    chunks = TEAM * half // CHUNK

    def shape(*dims, kind=BF):
        return jax.ShapeDtypeStruct(dims, kind)

    shapes = [
        (shape(highs, 2, 2, 2, rows, 4 * HD), ANY),
        (shape(highs, 2, 2, 2, rows, HD), ANY),
        (shape(highs, 2, 2, 2, rows, 2 * units), ANY),
        (shape(highs, 2, 2, 2, rows, units), ANY),
        (shape(LANES, width, kind=F32), VMEM),
        (shape(TEAM, half, width), ANY),
        (shape(chunks, CHUNK, width), VMEM),
        (shape(chunks, CHUNK, LANES), VMEM),
        (shape(chunks, CHUNK, HD, kind=F32), VMEM),
        (shape(chunks, CHUNK, HD, kind=F32), VMEM),
        (shape(4, chunks, CHUNK, HD, kind=F32), ANY),
        (shape(chunks, CHUNK, HD, kind=F32), VMEM),
        (shape(chunks, CHUNK, HD), VMEM),
        (shape(chunks, HD, HD, kind=F32), ANY),
        (shape(8, HD, kind=F32), VMEM),
        (shape(TEAM, half, width), VMEM),
        (shape(half, width, kind=F32), VMEM),
    ]
    arrays = [mixer_in, mixer_out, ffn_in, ffn_out, small, ups, own, cot, *starts_arrays(starts), head_gain]
    scratch = [
        shapes[0][0],
        shapes[1][0],
        shapes[10][0],
        shapes[13][0],
        shape(TEAM, half, width),
        shape(chips, rows, LANES),
        shape(*ups.shape, kind=F32),
        shape(width, LANES, kind=F32),
        shape(HD, HD, kind=F32),
        shape(TEAM, half, width),
        shape(3, half, width),
        shape(2, half, width),
        shape(2, half, width),
        shape(half, width),
    ]
    used = arrays + scratch + [a for a, place in shapes if place is VMEM]
    size = sum(a.size * a.dtype.itemsize for a in used)
    forwards = 8 * ((highs - 1) + highs + 2 * highs)
    sems = [
        (8, 2), (8, 2), (forwards,), (highs, 2, 2, 8), (chips,), (chips,), (2,), (5,), (4,), (3,), (4,),
        (STEPS, 6), (STEPS, 5), (STEPS, 3), (STEPS, 4), (7,),
    ]
    return pl.pallas_call(
        forward_kernel,
        out_shape=[a for a, _ in shapes],
        in_specs=[VMEM] * len(arrays),
        out_specs=[place for _, place in shapes],
        scratch_shapes=[pltpu.VMEM(a.shape, a.dtype) for a in scratch]
        + [DMA(n) for n in sems]
        + state_pass_scratch(highs),
        compiler_params=pltpu.CompilerParams(
            collective_id=0, has_side_effects=True, vmem_limit_bytes=min(size + (14 << 20), 62 << 20)
        ),
        name="forward",
    )(*arrays)


STEPS = 4


CROSS = [(0, 1), (1, 0)]


TILE = 256


def grads_kernel(count, *refs):
    lefts, rights = refs[:count], refs[count : 2 * count]
    away, keep = refs[2 * count : 2 * count + 2]
    ordered = refs[2 * count + 2 : 3 * count + 2]
    out, got, send, arrive = refs[3 * count + 2 :]
    zh, y, c = lax.axis_index("zh"), lax.axis_index("y"), lax.axis_index("c")
    highs = lax.axis_size("zh")
    chips, rows, _ = lefts[0].shape
    half = chips // 2 * rows
    quarter = half // 2
    barrier = pltpu.get_barrier_semaphore()
    pl.semaphore_signal(barrier, inc=1, device_id={"c": 1 - c}, device_id_type=MESH)
    for left, order in zip(lefts, ordered):
        n = 0
        for x in (1 - c, c):
            for at_y in (1 - y, y):
                for k in range(highs):
                    for zl in range(2):
                        chip = chip_index(lax.rem(zh + k, highs), zl, at_y, x)
                        order[pl.ds(n * rows, rows)] = left[chip]
                        n += 1
    pl.semaphore_wait(barrier, 1)

    def move(n):
        return pltpu.make_async_remote_copy(
            src_ref=out.at[n],
            dst_ref=got.at[n],
            send_sem=send.at[n],
            recv_sem=arrive.at[n],
            device_id={"c": 1 - c},
            device_id_type=MESH,
        )

    def send_tile(order, right, n, column, width):
        block = dot(order[pl.ds(0, half)], right[:, pl.ds(column, width)])
        if width == TILE:
            out[n] = low(block)
        else:
            out[n, :, pl.ds(0, width)] = low(block)
        move(n).start()

    def add_tile(order, right, n, column, width, start):
        block = dot(order[pl.ds(half, half)], right[:, pl.ds(column, width)])
        move(n).wait_recv()
        block = low(block + got[n, :, pl.ds(0, width)].astype(F32))
        away[:, pl.ds(start + column, width)] = block[:quarter]
        keep[:, pl.ds(start + column, width)] = block[quarter:]

    tile, start = 0, 0
    for order, right in zip(ordered, rights):
        whole, odd = right.shape[1] // TILE, right.shape[1] % TILE

        def send_step(n, _, order=order, right=right, tile=tile):
            send_tile(order, right, tile + n, pl.multiple_of(n * TILE, TILE), TILE)
            return 0

        lax.fori_loop(0, whole, send_step, 0)
        if odd:
            send_tile(order, right, tile + whole, whole * TILE, odd)
        tile += whole + (odd > 0)
    total = tile
    tile = 0
    for order, right in zip(ordered, rights):
        whole, odd = right.shape[1] // TILE, right.shape[1] % TILE

        def add_step(n, _, order=order, right=right, tile=tile, start=start):
            add_tile(order, right, tile + n, pl.multiple_of(n * TILE, TILE), TILE, start)
            return 0

        lax.fori_loop(0, whole, add_step, 0)
        if odd:
            add_tile(order, right, tile + whole, whole * TILE, odd, start)
        tile += whole + (odd > 0)
        start += right.shape[1]

    def sent(n, _):
        move(n).wait_send()
        return 0

    lax.fori_loop(0, total, sent, 0)


def weight_grads(call_id, pairs):
    highs = lax.axis_size("zh")
    count = len(pairs)
    team_tokens, width = pairs[0][0].shape
    chips = highs * 8
    rows = width // chips
    lefts = [left.T.reshape(chips, rows, team_tokens) for left, _ in pairs]
    rights = [right for _, right in pairs]
    cols = sum(r.shape[1] for r in rights)
    tiles = sum(-(-r.shape[1] // TILE) for r in rights)
    half = width // 2
    shape = jax.ShapeDtypeStruct((half // 2, cols), BF)
    size = 4 * count * width * team_tokens + 2 * team_tokens * cols + 2 * half * cols
    size += 4 * half * tiles * TILE
    away, keep = pl.pallas_call(
        functools.partial(grads_kernel, count),
        out_shape=(shape, shape),
        in_specs=[VMEM] * (2 * count),
        out_specs=(VMEM, VMEM),
        scratch_shapes=[pltpu.VMEM((width, team_tokens), BF)] * count
        + [
            pltpu.VMEM((tiles, half, TILE), BF),
            pltpu.VMEM((tiles, half, TILE), BF),
            DMA((tiles,)),
            DMA((tiles,)),
        ],
        compiler_params=pltpu.CompilerParams(
            collective_id=call_id, has_side_effects=True, vmem_limit_bytes=size + (8 << 20)
        ),
        name=f"grads_{call_id}",
    )(*lefts, *rights)
    shape = (highs, 2, rows, cols)
    return away.reshape(shape), keep.reshape(shape)


def together(*values):
    return lax.optimization_barrier(values)


def add_rows(out, *parts):
    def step(n, _):
        at = pl.ds(n * 16, 16)
        total = parts[0][at].astype(F32)
        for part in parts[1:]:
            total = total + part[at].astype(F32)
        out[at] = low(total)
        return 0

    lax.fori_loop(0, out.shape[0] // 16, step, 0)


def backward_kernel(*refs):
    (
        back, cot, middle, gain, pair_away, pair_keep, down_away, down_keep, merge_w, gated, projected, mixed,
        cumulated, gate, befores, decay, low_rank, up_pad, head_gain, hidden, starts_row, starts_column,
        grad_middle, gain_grad, proj, ranks, heads, early_away, early_keep, gate_sum, up_part, down_sum,
        got, relayed, staged, line, branch, left_hidden, left_branch, normed_grad, douts, tiles, tiles_got,
        pair_side, down_side, gate_got, down_got, up_grad, state,
        send, arrive, send2, arrive2, side_send, side_arrive, high_send, high_arrive, tile_send, tile_arrive,
    ) = refs[:-STATE_REFS]
    me = Place()
    zh, y, highs = lax.axis_index("zh"), lax.axis_index("y"), lax.axis_size("zh")
    chunks, _, width = hidden.shape
    units = down_keep.shape[-1]
    first = ((zh * 2 + me.c) * 2 + y) * (chunks * CHUNK)
    greet_all(me)

    def side_part(part, pair, down):
        return down if part == 0 else pair.at[:, :, :, pl.ds((part - 1) * units, units)]

    sides = [
        copy_to(
            side_part(p, pair_away, down_away),
            side_part(p, pair_side, down_side),
            side_send.at[p],
            side_arrive.at[p],
            {"y": 1 - y},
        )
        for p in range(3)
    ]
    highs_moves = [
        [
            copy_to(
                side_part(p, pair_side, down_side).at[k],
                (down_got if p == 0 else gate_got).at[k - 1],
                high_send.at[p, k],
                high_arrive.at[p, k],
                {"zh": lax.rem(zh + k, highs)},
            )
            for k in range(1, highs)
        ]
        for p in range(2)
    ]

    def side_add(part):
        sides[part].wait()
        mine, there = side_part(part, pair_keep, down_keep), side_part(part, pair_side, down_side)
        out = up_part if part == 2 else there
        for k in range(highs):
            for m in range(2):
                add_rows(out.at[k, m], mine.at[k, m], there.at[k, m])

    def high_add(part):
        source, there = side_part(part, pair_side, down_side), (down_got if part == 0 else gate_got)
        out = down_sum if part == 0 else gate_sum
        for k in range(1, highs):
            wait_for(there.at[k - 1], high_arrive.at[part, k])
        for m in range(2):
            add_rows(out.at[m], source.at[0, m], *(there.at[k - 1, m] for k in range(1, highs)))

    sides[0].start()

    steps = send.shape[0]
    rows = cot.shape[0] // steps

    def part(ref, k, n):
        return ref.at[k, pl.ds(n * rows, rows)]

    sums = [
        MemberSum(
            me,
            lambda k, n=n: part(back, k, n),
            lambda k, n=n: part(got, k, n),
            lambda k, n=n: part(relayed, k, n),
            lambda k, n=n: part(staged, k, n),
            send.at[n],
            arrive.at[n],
            two="zl",
        )
        for n in range(steps)
    ]
    spreads = [
        HalvesSpread(
            me,
            line.at[pl.ds(n * rows, rows)],
            lambda k, n=n: part(branch, k, n),
            send2.at[n],
            arrive2.at[n],
        )
        for n in range(steps)
    ]
    for transfer in sums:
        transfer.start()

    owners = highs * 8
    owner_rows = width // owners

    def transpose(source, target):
        for n in range(chunks):
            turned = source[n].T
            for chip in range(owners):
                at_zh, zl, at_y, x = chip // 8, chip // 4 % 2, chip // 2 % 2, chip % 2
                x_place = me.c if x == 1 else 1 - me.c
                x_place = jnp.where(x_place == 1, 1, 0)
                y_place = jnp.where((y if at_y == 1 else 1 - y) == 1, 1, 0)
                place = ((x_place * 2 + y_place) * highs + lax.rem(at_zh - zh + highs, highs)) * 2 + zl
                at = pl.ds(pl.multiple_of(place * owner_rows, owner_rows), owner_rows)
                target[at, n * CHUNK : (n + 1) * CHUNK] = turned[chip * owner_rows : (chip + 1) * owner_rows]

    transpose(hidden, left_hidden)
    for transfer in sums:
        transfer.relay()
    for n in range(steps):
        at = pl.ds(n * rows, rows)
        mid = middle[at]
        scale = lax.rsqrt(jnp.mean(mid * mid, -1, keepdims=True) + EPSILON)
        normed = mid * scale
        total = sums[n].total()
        gsum = jnp.sum(total * normed, axis=0, keepdims=True)
        gain_grad[...] = gsum if n == 0 else gain_grad[...] + gsum
        scaled = total * gain[...]
        out = cot[at].astype(F32) + scale * (
            scaled - normed * jnp.mean(scaled * normed, -1, keepdims=True)
        )
        grad_middle[at] = out
        line[at] = low(out)
        spreads[n].start()
        if n:
            spreads[n - 1].relay()
    spreads[steps - 1].relay()
    side_add(0)
    for move in highs_moves[0]:
        move.start()
    sides[1].start()
    for transfer in spreads:
        transfer.wait()

    heads[...] = jnp.zeros_like(heads)

    def head_step(n, _):
        grad = dot(branch[n], merge_w[...])
        out = mixed[n]
        scale = lax.rsqrt(jnp.mean(out * out, -1, keepdims=True) + HEAD_FLOOR)
        normed = out * scale
        u = projected[3, n]
        sig = jax.nn.sigmoid(u)
        dn = grad * (u * sig)
        proj[n, :, 3 * HD :] = low(grad * normed * head_gain[...] * sig * (1.0 + u * (1.0 - sig)))
        heads[17:18] = heads[17:18] + jnp.sum(dn * normed, axis=0, keepdims=True)
        scaled = dn * head_gain[...]
        douts[n] = low(scale * (scaled - normed * jnp.mean(scaled * normed, -1, keepdims=True)))
        return 0

    lax.fori_loop(0, chunks, head_step, 0)

    def masks(n):
        return keyed_mask(first + n * CHUNK, starts_row, starts_column)

    def query_rows(n, visible):
        return low(projected[0, n] * jnp.exp(cumulated[n]) * visible)

    state[...] = jnp.zeros_like(state)

    def local_step(i, _):
        n = chunks - 1 - i
        _, visible, keep, _ = masks(n)
        carry = keep * jnp.exp(cumulated[n, CHUNK - 1 :])
        state[...] = carry * state[...] + dot_rows(douts[n], query_rows(n, visible))
        return 0

    lax.fori_loop(0, chunks, local_step, 0)
    states = StatePass(True, state, decay, state, *refs[-STATE_REFS:])
    states.begin()

    transpose(branch, left_branch)
    half = width // 2
    quarter = half // 2

    def tile_move(n):
        return copy_to(tiles.at[n], tiles_got.at[n], tile_send.at[n], tile_arrive.at[n], {"c": 1 - me.c})

    def right_tile(kind, n):
        if kind == 0:
            return gated[...].reshape(chunks * CHUNK, HD)[:, n * TILE : (n + 1) * TILE]
        at = 3 * HD + n * TILE
        return proj[...].reshape(chunks * CHUNK, 4 * HD)[:, at : at + TILE]

    lefts = left_branch, left_hidden
    for kind in range(2):
        for n in range(HD // TILE):
            tile = kind * (HD // TILE) + n
            tiles[tile] = low(dot(lefts[kind][pl.ds(0, half)], right_tile(kind, n)))
            tile_move(tile).start()
    states.combine()
    for kind in range(2):
        for n in range(HD // TILE):
            tile = kind * (HD // TILE) + n
            block = dot(lefts[kind][pl.ds(half, half)], right_tile(kind, n))
            tile_move(tile).wait_recv()
            block = low(block + tiles_got[tile].astype(F32))
            at = slice(tile * TILE, (tile + 1) * TILE)
            early_away[:, at] = block[:quarter]
            early_keep[:, at] = block[quarter:]
    states.spread()
    side_add(1)
    for move in highs_moves[1]:
        move.start()
    sides[2].start()
    states.finish()

    upper = (
        lax.broadcasted_iota(jnp.int32, (CHUNK, CHUNK), 0)
        <= lax.broadcasted_iota(jnp.int32, (CHUNK, CHUNK), 1)
    ).astype(F32)
    up_grad[...] = jnp.zeros_like(up_grad)

    def chunk_step(i, _):
        n = chunks - 1 - i
        pair, visible, keep, last = masks(n)
        b = cumulated[n]
        mid, end = b[CHUNK // 2 - 1 : CHUNK // 2], b[CHUNK - 1 :]
        q, k, v = projected[0, n], projected[1, n], low(projected[2, n])
        do = douts[n]
        eq, ek, el = jnp.exp(b - mid), jnp.exp(mid - b), jnp.exp(end - b) * last
        qh, kh, kc = low(q * eq), low(k * ek), k * el
        scores = low(jnp.where(pair, dot_last(qh, kh), 0.0))
        gs = low(jnp.where(pair, dot_last(do, v), 0.0))
        ds = low(state[...])
        proj[n, :, 2 * HD : 3 * HD] = low(dot_rows(scores, do) + dot_last(low(kc), ds))
        dq = dot(gs, kh) * eq + dot(do, low(befores[n])) * (jnp.exp(b) * visible)
        gkc = dot(v, ds)
        dk = dot_rows(gs, qh) * ek + gkc * el
        proj[n, :, :HD] = low(dq * HD ** (-0.5))
        proj[n, :, HD : 2 * HD] = low(dk)
        carry = keep * jnp.exp(end)
        extra = jnp.sum(gkc * kc, axis=0, keepdims=True)
        extra = extra + carry * jnp.sum(befores[n] * state[...], axis=0, keepdims=True)
        dlog = extra + jnp.dot(
            upper, dq * q - dk * k, precision=lax.Precision.HIGHEST, preferred_element_type=F32
        )
        state[...] = carry * state[...] + dot_rows(do, query_rows(n, visible))
        da = dlog * jax.nn.sigmoid(-gate[n]) / 16.0
        heads[16:17] = heads[16:17] + jnp.sum(da, axis=0, keepdims=True)
        dar = low(da)
        up_grad[...] = up_grad[...] + dot_rows(low_rank[n], dar)
        ranks[n] = low(dot_last(dar, up_pad[...]))
        return 0

    lax.fori_loop(0, chunks, chunk_step, 0)
    heads[0:16] = up_grad[2:18]
    high_add(0)
    side_add(2)
    high_add(1)
    for move in highs_moves[0] + highs_moves[1]:
        move.wait_send()
    for transfer in sums:
        transfer.wait_sent()
    for tile in range(tiles.shape[0]):
        tile_move(tile).wait_send()
    states.wait_sent()


def backward(
    back, cot, middle, gain, pair, down, merge_w, gated, projected, mixed, cumulated, gate, befores, decay,
    low_rank, up_pad, head_gain, hidden, starts,
):
    highs, members, owner_rows, units = down[0].shape
    rows, width = cot.shape
    chunks = hidden.shape[0]

    def shape(*dims, kind=BF):
        return jax.ShapeDtypeStruct(dims, kind)

    arrays = [
        back, cot, middle, gain, *pair, *down, merge_w, gated, projected, mixed, cumulated, gate, befores, decay,
        low_rank, up_pad, head_gain, hidden, *starts_arrays(starts),
    ]
    away = {4, 6}
    quarter = width // 4
    shapes = [
        shape(rows, width, kind=F32),
        shape(1, width, kind=F32),
        shape(chunks, CHUNK, 4 * HD),
        shape(chunks, CHUNK, LANES),
        shape(24, HD, kind=F32),
        shape(quarter, 2 * HD),
        shape(quarter, 2 * HD),
        shape(members, owner_rows, units),
        shape(highs, members, owner_rows, units),
        shape(members, owner_rows, units),
    ]
    tiles = 2 * HD // TILE
    scratch = [
        shape(2, rows, width),
        shape(1, rows, width),
        shape(1, rows, width),
        shape(rows, width),
        shape(TEAM, rows, width),
        shape(width, chunks * CHUNK),
        shape(width, chunks * CHUNK),
        shape(8, HD, kind=F32),
        shape(chunks, CHUNK, HD),
        shape(tiles, width // 2, TILE),
        shape(tiles, width // 2, TILE),
        shape(highs, members, owner_rows, 2 * units),
        shape(highs, members, owner_rows, units),
        shape(highs - 1, members, owner_rows, units),
        shape(highs - 1, members, owner_rows, units),
        shape(LANES, HD, kind=F32),
        shape(HD, HD, kind=F32),
    ]
    used = [a for n, a in enumerate(arrays) if n not in away] + shapes + scratch
    size = sum(a.size * a.dtype.itemsize for a in used)
    sems = [
        (STEPS, 3), (STEPS, 3), (STEPS, 5), (STEPS, 4), (3,), (3,), (2, highs), (2, highs), (tiles,), (tiles,),
    ]
    return pl.pallas_call(
        backward_kernel,
        out_shape=shapes,
        in_specs=[ANY if n in away else VMEM for n in range(len(arrays))],
        out_specs=[VMEM] * len(shapes),
        scratch_shapes=[pltpu.VMEM(a.shape, a.dtype) for a in scratch]
        + [DMA(n) for n in sems]
        + state_pass_scratch(highs),
        compiler_params=pltpu.CompilerParams(
            collective_id=3, has_side_effects=True, vmem_limit_bytes=min(size + (14 << 20), 62 << 20)
        ),
        name="backward",
    )(*arrays)


def closing_kernel(*refs):
    (
        partial, own, grad_middle, gain, down, gain_two_grad, heads, late_away, late_keep, early_away, early_keep,
        pair, gates, downs,
        out, late_home, early_home, pair_home, gate_home, down_home, wide_out, heads_out, gains_out,
        got, relayed, staged, line, late_side, late, early_side, early, late_got, early_got, pair_got, late_sum, early_sum, pair_sum,
        wide, wide_got, heads_got, heads_sum, wide_twin, gain_grad, rank_grad,
        send, arrive, twin_send, twin_arrive, here, side_sem, high_send, high_arrive, home_send, home_arrive,
        wide_send, wide_arrive, heads_send, heads_arrive, near, out_send, out_arrive, gain_send, gain_arrive,
    ) = refs
    me = Place()
    zh, y, highs = lax.axis_index("zh"), lax.axis_index("y"), lax.axis_size("zh")
    greet_all(me)
    steps = send.shape[0]
    rows, width = own.shape[0] // steps, own.shape[1]
    twin = {"c": 1 - me.c}

    def high_copies(kind, source, target):
        return [
            copy_to(
                source.at[k],
                target.at[k - 1],
                high_send.at[kind, k],
                high_arrive.at[kind, k],
                {"zh": lax.rem(zh + k, highs)},
            )
            for k in range(1, highs)
        ]

    side = copy_to(late_away, late_side, side_sem.at[0], side_sem.at[1], {"y": 1 - y})
    early_move = copy_to(early_away, early_side, side_sem.at[2], side_sem.at[3], {"y": 1 - y})
    early_move.start()
    side.start()
    early_moves = high_copies(0, early, early_got)
    pair_moves = high_copies(1, pair, pair_got)
    late_moves = high_copies(2, late, late_got)

    def part(ref, k, n):
        return ref.at[k, pl.ds(n * rows, rows)]

    sums = [
        OwnersSum(
            me,
            lambda k, n=n: part(partial, k, n),
            lambda k, n=n: part(got, k, n),
            lambda k, n=n: part(relayed, k, n),
            lambda k, n=n: part(staged, k, n),
            send.at[n],
            arrive.at[n],
        )
        for n in range(steps)
    ]
    for transfer in sums:
        transfer.start()
    for move in pair_moves:
        move.start()

    def home(n, source, target):
        return Transfer(
            route_weights_home(me),
            lambda k: source.at[k],
            lambda k: target.at[k],
            home_send.at[n],
            home_arrive.at[n],
        )

    homes = [
        home(0, downs, down_home),
        home(1, early_sum, early_home),
        home(2, pair_sum, pair_home),
        home(3, late_sum, late_home),
        home(4, gates, gate_home),
    ]

    def twin_copy(n):
        return copy_to(
            line.at[pl.ds(n * rows, rows)], part(out, me.c, n), twin_send.at[n], twin_arrive.at[n], twin
        )

    def own_copy(n):
        return pltpu.make_async_copy(line.at[pl.ds(n * rows, rows)], part(out, me.c, n), here.at[n])

    for transfer in sums:
        transfer.relay()
    homes[0].start()
    homes[4].start()
    early_move.wait()
    for k in range(highs):
        for m in range(2):
            add_rows(early.at[k, m], early_keep.at[k, m], early_side.at[k, m])
    for move in early_moves:
        move.start()
    for n in range(steps):
        at = pl.ds(n * rows, rows)
        x = own[at].astype(F32)
        scale = lax.rsqrt(jnp.mean(x * x, -1, keepdims=True) + EPSILON)
        normed = x * scale
        total = sums[n].total()
        rank = low(total[:, width:])
        total = total[:, :width] + dot(rank, down[...])
        gsum = jnp.sum(total * normed, axis=0, keepdims=True)
        hidden = low(normed * gain[...])
        rsum = dot_rows(rank, hidden)
        gain_grad[...] = gsum if n == 0 else gain_grad[...] + gsum
        rank_grad[...] = rsum if n == 0 else rank_grad[...] + rsum
        scaled = total * gain[...]
        line[at] = low(
            grad_middle[at]
            + scale * (scaled - normed * jnp.mean(scaled * normed, -1, keepdims=True))
        )
        twin_copy(n).start()
        own_copy(n).start()

    owner_rows = wide.shape[2]
    for n in range(wide.shape[0]):
        at = slice(n * owner_rows, (n + 1) * owner_rows)
        wide[n, 0:1] = gain_grad[:, at]
        wide[n, 1:2] = gain_two_grad[:, at]
        wide[n, 2:8] = jnp.zeros((6, owner_rows), F32)
        wide[n, 8:24] = rank_grad[:16, at]
    spreads = Transfer(
        route_all(me), lambda k: wide.at[k], lambda k: wide_got.at[k], wide_send, wide_arrive
    )
    spreads.start()
    group_out, group_arrive = [], []
    for n in range(highs):
        for f in range(4):
            to_zh, to_y, to_c = lax.rem(zh + n, highs), flip(y, f & 2), flip(me.c, f & 1)
            to = {"zh": to_zh, "y": to_y, "c": to_c}
            group_out.append((0, (zh * 2 + y) * 2 + me.c, to, n + f == 0))
            group_arrive.append(((to_zh * 2 + to_y) * 2 + to_c, n + f == 0))
    heads_move = Transfer(
        (group_out, group_arrive), lambda _: heads, lambda k: heads_got.at[k], heads_send, heads_arrive
    )
    heads_move.start()

    side.wait()
    for k in range(highs):
        for m in range(2):
            add_rows(late.at[k, m], late_keep.at[k, m], late_side.at[k, m])
    for move in late_moves:
        move.start()

    heads_move.wait()
    total = heads_got[0]
    for n in range(1, highs * 4):
        total = total + heads_got[n]
    heads_sum[...] = total
    tail = gains_out.shape[1]
    gains = Transfer(
        route_member(me),
        lambda _: heads_sum.at[pl.ds(heads_sum.shape[0] - tail, tail)],
        lambda k: gains_out.at[k],
        gain_send,
        gain_arrive,
    )
    gains.start()
    moves = [
        copy_to(
            heads_sum,
            heads_out.at[me.x],
            out_send.at[n],
            out_arrive.at[me.x],
            {"zl": flip(me.zl, fz), "x": flip(me.x, fx)},
        )
        for n, (fz, fx) in enumerate(FLIPS[:3])
    ]

    @pl.when(me.c == me.zl)
    def _():
        for move in moves:
            move.start()
        heads_out[me.x] = heads_sum[...]

    spreads.wait()
    total = wide_got[0]
    for n in range(1, wide.shape[0]):
        total = total + wide_got[n]
    wide_out[...] = total
    swap = copy_to(wide_out, wide_twin, near.at[0], near.at[1], twin)
    swap.start()

    for n, kind_moves, source, target, total in (
        (2, pair_moves, pair, pair_got, pair_sum),
        (1, early_moves, early, early_got, early_sum),
        (3, late_moves, late, late_got, late_sum),
    ):
        for k in range(1, highs):
            wait_for(target.at[k - 1], high_arrive.at[n - 1, k])
        for m in range(2):
            add_rows(total.at[m], source.at[0, m], *(target.at[k - 1, m] for k in range(1, highs)))
        homes[n].start()
    for k in range(2):
        own_slot = (me.c == me.zl) & (me.x == k)
        unless(own_slot, lambda k=k: wait_for(heads_out.at[k], out_arrive.at[k]))

    @pl.when(me.c == me.zl)
    def _():
        for move in moves:
            move.wait_send()

    swap.wait()
    wide_out[...] = wide_out[...] + wide_twin[...]
    gains.wait()
    for transfer in sums:
        transfer.wait_sent()
    for n in range(steps):
        twin_copy(n).wait()
        own_copy(n).wait()
    for transfer in homes:
        transfer.wait()
    for move in early_moves + pair_moves + late_moves:
        move.wait_send()


def closing(partial, own, grad_middle, gain, down, gain_two_grad, heads, late, early, pair, gates, downs):
    rows, width = own.shape
    lanes = partial.shape[-1] - width
    highs, _, owner_rows, late_cols = late[0].shape
    chips = highs * 8
    arrays = [partial, own, grad_middle, gain, down, gain_two_grad, heads, *late, *early, pair, gates, downs]

    def shape(*dims, kind=BF):
        return jax.ShapeDtypeStruct(dims, kind)

    cols = late_cols, early[0].shape[-1], pair.shape[-1], gates.shape[-1], downs.shape[-1]
    shapes = [shape(2, rows, width)] + [shape(2, owner_rows, n) for n in cols]
    shapes += [
        shape(24, owner_rows, kind=F32),
        shape(2, *heads.shape, kind=F32),
        shape(TEAM, 8, heads.shape[1], kind=F32),
    ]
    scratch = [shape(n, rows, width + lanes) for n in (3, 2, 2)] + [shape(rows, width)]
    scratch += [shape(*late[0].shape)] * 2 + [shape(*early[0].shape)] * 2
    scratch += [shape(highs - 1, 2, owner_rows, n) for n in cols[:3]]
    scratch += [shape(2, owner_rows, n) for n in cols[:3]]
    scratch += [
        shape(chips, 24, owner_rows, kind=F32),
        shape(chips, 24, owner_rows, kind=F32),
        shape(highs * 4, *heads.shape, kind=F32),
        shape(*heads.shape, kind=F32),
        shape(24, owner_rows, kind=F32),
        shape(1, width, kind=F32),
        shape(lanes, width, kind=F32),
    ]
    size = sum(a.size * a.dtype.itemsize for a in arrays + shapes + scratch)
    sems = [
        (STEPS, 6), (STEPS, 5), (STEPS,), (STEPS,), (STEPS,), (4,), (3, highs), (3, highs), (5, 2), (5, 2),
        (chips,), (chips,), (highs * 4,), (highs * 4,), (2,), (3,), (2,), (TEAM,), (TEAM,),
    ]
    return pl.pallas_call(
        closing_kernel,
        out_shape=shapes,
        in_specs=[VMEM] * len(arrays),
        out_specs=[VMEM] * len(shapes),
        scratch_shapes=[pltpu.VMEM(a.shape, a.dtype) for a in scratch] + [DMA(n) for n in sems],
        compiler_params=pltpu.CompilerParams(
            collective_id=4, has_side_effects=True, vmem_limit_bytes=size + (10 << 20)
        ),
        name="closing",
    )(*arrays)


def shards(
    tokens,
    cotangent,
    lengths,
    attn_gain,
    ffn_gain,
    mixer_in,
    decay_down,
    decay_up,
    decay_bias,
    head_gain,
    mixer_out,
    ffn_in,
    ffn_out,
):
    zh, zl, y, x, c = (lax.axis_index(a) for a in SEQ + ("c",))
    block, width = tokens.shape
    half = block // 2
    rows = mixer_in.shape[1]
    units = ffn_out.shape[0] // 2
    team_tokens = 2 * block
    rank = decay_down.shape[1]

    small = jnp.concatenate([attn_gain[:, None], ffn_gain[:, None], decay_down], axis=1)
    small = jnp.pad(small, ((0, 0), (0, LANES - small.shape[1])))
    up_head = lax.dynamic_slice_in_dim(decay_up, HD * x, HD, 1).astype(F32)
    bias_head = lax.dynamic_slice_in_dim(decay_bias, HD * x, HD, 0)
    ups = jnp.concatenate([up_head, bias_head[None], jnp.zeros((7, HD), F32)], axis=0)
    own = lax.dynamic_slice_in_dim(tokens, half * c, half, 0)
    own_dy = lax.dynamic_slice_in_dim(cotangent, half * c, half, 0)
    starts = jnp.cumsum(lengths) - lengths
    (
        mixer_w, merge_w, pair_w, down_w, gains, ffn_dy, hidden_one, low_rank, gate_input, cumulated, projected,
        mixed, gated, befores, decay, hidden_two, middle,
    ) = forward(
        mixer_in, mixer_out.T, ffn_in, ffn_out.T, small, ups, own, own_dy, starts, head_gain[None]
    )
    up_head = jnp.where(c == zl, up_head, lax.ppermute(up_head, "c", CROSS)).astype(BF)
    mixer_w, merge_w = mixer_w.reshape(width, 4 * HD), merge_w.reshape(width, HD)
    pair_w, down_w = pair_w.reshape(width, 2 * units), down_w.reshape(width, units)
    gain_one, gain_two, rank_down = gains[:1], gains[1:2], gains[2 : 2 + rank].astype(BF)
    ffn_dy = ffn_dy.reshape(team_tokens, width)
    hidden_two = hidden_two.reshape(team_tokens, width)

    up_pair = dot(hidden_two, pair_w)
    up_a, up_b = up_pair[:, :units], up_pair[:, units:]
    ffn_sig = jax.nn.sigmoid(up_a)
    ffn_silu = up_a * ffn_sig
    activated = low(ffn_silu * up_b)
    down = dot_last(activated, down_w).astype(BF)
    down = lax.psum_scatter(down, ("zl", "x"), scatter_dimension=0, tiled=True).astype(F32)
    result = (middle + down).astype(BF)
    twin = lax.ppermute(result, "c", CROSS)
    result = jnp.concatenate([jnp.where(c == 0, result, twin), jnp.where(c == 0, twin, result)], axis=0)

    grad_act = dot(ffn_dy, down_w)
    grad_gate = low(grad_act * up_b * ffn_sig * (1.0 + up_a * (1.0 - ffn_sig)))
    grad_upper = low(grad_act * ffn_silu)
    grad_pair = jnp.concatenate([grad_gate, grad_upper], axis=1)
    back = dot_last(grad_pair, pair_w)
    ffn_sums = weight_grads(12, [(ffn_dy, activated)]), weight_grads(13, [(hidden_two, grad_pair)])
    back, ffn_sums = together(back, ffn_sums)
    back = low(back).reshape(TEAM, half, width)
    lanes = LANES
    (
        grad_middle, grad_gain_two, grad_proj, grad_rank_part, heads, early_away, early_keep, gate_sum, up_part, down_sum,
    ) = backward(
        back, own_dy, middle, gain_two, ffn_sums[1], ffn_sums[0], merge_w, gated, projected, mixed, cumulated,
        gate_input, befores, decay, low_rank, jnp.pad(up_head, ((0, lanes - rank), (0, 0))), head_gain[None],
        hidden_one, starts,
    )
    grad_proj = grad_proj.reshape(team_tokens, 4 * HD)
    hidden_part = dot_last(grad_proj, mixer_w)
    hidden_part = jnp.concatenate(
        [low(hidden_part).reshape(TEAM, half, width), grad_rank_part], axis=2
    )
    late_sums = weight_grads(15, [(hidden_one.reshape(team_tokens, width), grad_proj[:, : 3 * HD])])
    early_shape = late_sums[0].shape[:3] + (2 * HD,)
    early_sums = early_away.reshape(early_shape), early_keep.reshape(early_shape)
    down_pad = jnp.pad(rank_down, ((0, lanes - rank), (0, 0)))
    grad_inputs, late_home, early_home, up_home, gate_home, ffn_down, wide, heads, gains = closing(
        hidden_part, own, grad_middle, gain_one, down_pad, grad_gain_two, heads, late_sums, early_sums, up_part,
        gate_sum, down_sum,
    )
    grad_inputs = grad_inputs.reshape(block, width)
    ffn_pair = jnp.stack([gate_home, up_home]).astype(F32)
    ffn_down = ffn_down.astype(F32)
    early_home = early_home.reshape(2, rows, 2, HD).astype(F32)
    late_home = late_home.reshape(2, rows, 3, HD).astype(F32)
    mixer_home = jnp.concatenate([late_home, early_home[:, :, 1:]], axis=2)
    return (
        result,
        grad_inputs,
        wide[0],
        wide[1],
        mixer_home.transpose(2, 1, 0, 3).reshape(4, rows, 2 * HD),
        wide[8 : 8 + rank].T,
        heads[:, :rank].transpose(1, 0, 2).reshape(rank, 2 * HD),
        heads[:, rank].reshape(2 * HD),
        jnp.sum(gains[:, rank + 1 - 16], axis=0),
        early_home[:, :, 0].transpose(0, 2, 1).reshape(2 * HD, rows),
        ffn_pair.transpose(0, 2, 1, 3).reshape(2, rows, 2 * units),
        ffn_down.transpose(0, 2, 1).reshape(2 * units, rows),
    )


def solution(mesh):
    devices = mesh.devices
    inner = Mesh(devices.reshape(devices.shape[0] // 8, 2, 2, 2, devices.shape[1]), SEQ + ("c",))
    in_specs = (
        P(SEQ, None),
        P(SEQ, None),
        P(),
        P(SEQ),
        P(SEQ),
        P(None, SEQ, "c"),
        P(SEQ, None),
        P(None, "c"),
        P("c"),
        P(),
        P("c", SEQ),
        P(None, SEQ, "c"),
        P("c", SEQ),
    )
    out_specs = (
        P(SEQ, None),
        P(SEQ, None),
        P(SEQ),
        P(SEQ),
        P(None, SEQ, "c"),
        P(SEQ, None),
        P(None, "c"),
        P("c"),
        P(),
        P("c", SEQ),
        P(None, SEQ, "c"),
        P("c", SEQ),
    )
    return jax.shard_map(shards, mesh=inner, in_specs=in_specs, out_specs=out_specs, check_vma=False)
```

time: 1420 us -> 734 us (0.52)
  waiting for transfers between devices: 781 us -> 0.02 us
  Pallas kernels: 0 us -> 579 us
  blocking collectives: 211 us -> 0 us
  matrix products: 141 us -> 37.7 us
  other arithmetic: 94.6 us -> 13.1 us
  local copies, waits for them, and re-layouts: 151 us -> 70.3 us
    pallas_call x0 -> x6, Pallas kernels: none -> 579 us  [the longest x1 253 us: forward(): pl.pallas_call(forward_kernel, out_shape=[a for a, _ in shapes], in_specs...]
    all_gather x12 -> x0, waiting for transfers between devices: 378 us -> none  [the longest x2 199 us: gather_weights(): everything = lax.all_gather(pieces, 'g')]
    reduce_scatter x6 -> x1, waiting for transfers between devices: 362 us -> 0.01 us  [shards(): lax.psum_scatter(down, ('zl', 'x'), scatter_dimension=0, tiled=True)]
    all_to_all x9 -> x0, blocking collectives: 95 us -> none  [the longest x2 52.6 us: gather_weights(): pieces = lax.all_to_all(pieces, 't', 0, 0)]
    all_gather x5 -> x0, blocking collectives: 65.4 us -> none  [the longest x1 39.3 us: shards(): small = lax.all_gather(small, ('g', 't'), axis=0, tiled=True)]
    psum x3 -> x0, blocking collectives: 50.5 us -> none  [the longest x1 29.6 us: shards(): head_small = lax.psum(head_small, ('g', 'c'))]
    dot_general x28 -> x0, matrix products: 44.2 us -> none  [the longest x23 39.4 us: dot_rows(): lax.dot_general(a, b, (((0,), (0,)), ((), ())), preferred_element_type=F32)]
    unnamed x24 -> x1, waiting for transfers between devices: 40.5 us -> 0.02 us
  transfers between devices with their start and end apart: 24 -> 3, of which waited for: 20 -> 0; matrix products, arithmetic and copies ran while one was open for 16% -> 10% of each run, Pallas kernels for 0% -> 45%
where the time goes in v3:
time: 734 us; the launch traced here: 728 us
  Pallas kernels  579 us (79%)
  local copies, waits for them, and re-layouts  70.3 us (10%)
  matrix products  37.7 us (5%)
  between operations  15 us (2%)
  other arithmetic  13.1 us (2%)
  starting transfers between devices  12.9 us (2%)
    pallas_call x1, Pallas kernels, forward(): pl.pallas_call(forward_kernel, out_shape=[a for a, _ in shapes], in_specs...  253 us
    pallas_call x1, Pallas kernels, backward(): pl.pallas_call(backward_kernel, out_shape=shapes, in_specs=[ANY if n in a...  183 us
    pallas_call x1, Pallas kernels, closing(): pl.pallas_call(closing_kernel, out_shape=shapes, in_specs=[VMEM] * len(ar...  119 us
    unnamed x95, local copies, waits for them, and re-layouts  30.7 us
    pallas_call x3, Pallas kernels, weight_grads(): pl.pallas_call(functools.partial(grads_kernel, count), out_shape=(shape,...  24.2 us
    dot_general x3, matrix products, dot_last(): lax.dot_general(a, b, (((1,), (1,)), ((), ())), preferred_element_type=F32)  23 us
    dot_general x2, matrix products, dot(): return jnp.dot(a, b, preferred_element_type=F32)  14.7 us
  transfers between devices with their start and end apart: 3, of which 0 were waited for; matrix products, arithmetic and copies ran while one was open for 10% of the time, Pallas kernels for 45%

profile of v3, /device:TPU:0, one launch (start us, length us, event | category | flops | bytes accessed | tf_op | source)
XLA Modules:
  0.0 727.7 jit_solution(15812214495621206658)
XLA Ops:
  7.3 1.9 copy.67
  9.2 2.2 copy.68
  18.3 252.8 %forward.1 = (bf16[2,2,2,2,128,2048]{5,4,3,2,1,0:T(8,128)(2,1)}, bf16[2,2,2,2,128,512]{5,4,3,2,1,0:T(8,128)(2,1)}, bf16[2,2,2,2,128,2816]{5,4,3,2,1,0:T(8,128)(2...) custom-call(bf16[4,128,1024]{2,1,0:T(8,128)(2,1)} %refs_0_.1, ...), custom_call_target="tpu_custom_call" | custom-call | tf_op jit(solution)/shard_map/forward/pallas_call | solution.py:935
  271.1 10.3 %fusion.5 = f32[512,2816]{1,0:T(8,128)S(1)} fusion(bf16[512,2048]{1,0:T(8,128)(2,1)} %bitcast.96, bf16[2048,2816]{1,0:T(8,128)(2,1)} %bitcast.113), kind=kOutput, calls=%fused_computation.34 | convolution fusion | flops 5905580032 | bytes 19398656 | tf_op jit(solution)/shard_map/dot_general | solution.py:28
  281.4 4.4 multiply_convert_fusion.1
  285.9 4.7 convolution_convert_fusion.1
  292.4 10.0 %fusion.1 = bf16[512,2048]{1,0:T(8,128)(2,1)} fusion(bf16[2048,2816]{1,0:T(8,128)(2,1)} %bitcast.114, bf16[512,1408]{1,0:T(8,128)(2,1)S(1)} %get-tuple-element.145, bf16[512,1408]{1,0:T(8,128)(2,1)S(1)} %get-tuple-element.144), kind=kOutput, calls=%fused_computation.30 | convolution fusion | flops 5911347200 | bytes 16515072 | tf_op jit(solution)/shard_map/dot_general | solution.py:36
  303.9 2.0 pad_maximum_fusion.refs_1_
  305.9 3.9 copy.70
  309.9 3.9 copy.71
  314.7 1.6 copy-done.3
  317.7 6.7 grads_12.1
  326.6 10.9 %grads_13.1 = (bf16[512,2816]{1,0:T(8,128)(2,1)S(1)}, bf16[512,2816]{1,0:T(8,128)(2,1)S(1)}) custom-call(bf16[16,128,512]{2,1,0:T(8,128)(2,1)S(1)} %bitcast.77, bf16[512,2816]{1,0:T(8,128)(2,1)S(1)} %pad_maximum_fusion.refs_1_), custom_call_target="tpu_custom_call" | custom-call | tf_op jit(solution)/shard_map/grads_13/pallas_call | solution.py:1055
  337.5 1.6 copy-done.6
  339.1 1.6 copy-done.7
  340.7 3.9 copy.72
  345.4 182.8 %backward.1 = (f32[128,2048]{1,0:T(8,128)}, f32[1,2048]{1,0:T(1,128)}, bf16[4,128,2048]{2,1,0:T(8,128)(2,1)}, bf16[4,128,128]{2,1,0:T(8,128)(2,1)}, f32[24,512]{...) custom-call(bf16[4,128,2048]{2,1,0:T(8,128)(2,1)} %bitcast.95, ...), custom_call_target="tpu_custom_call" | custom-call | tf_op jit(solution)/shard_map/backward/pallas_call | solution.py:1407
  528.2 1.7 slice.65.refs_1_
  530.3 6.7 grads_15.1
  539.2 8.3 %convolution_convert_fusion = bf16[512,2048]{1,0:T(8,128)(2,1)S(1)} fusion(bf16[512,2048]{1,0:T(8,128)(2,1)S(1)} %bitcast.103, bf16[2048,2048]{1,0:T(8,128)(2,1)} %bitcast.115), kind=kOutput, calls=%fused_computation | convolution fusion | flops 4296015872 | bytes 12582912 | tf_op jit(solution)/shard_map/dot_general | solution.py:36
  547.6 1.6 pad_maximum_fusion.1.refs_0_
  550.5 118.8 %closing.1 = (bf16[2,128,2048]{2,1,0:T(8,128)(2,1)S(1)}, bf16[2,128,1536]{2,1,0:T(8,128)(2,1)S(1)}, bf16[2,128,1024]{2,1,0:T(8,128)(2,1)S(1)}, bf16[2,128,1408]{...) custom-call(bf16[4,128,2176]{2,1,0:T(8,128)(2,1)} %pad_maximum_fusio, ...), custom_call_target="tpu_custom_call" | custom-call | tf_op jit(solution)/shard_map/closing/pallas_call | solution.py:1672
  673.7 3.0 reshape.177
  676.7 3.4 fusion.3
  682.8 1.6 maximum_bitcast_fusion
  685.8 3.0 copy.80
  690.1 1.9 copy.84
  692.0 1.8 convert_bitcast_fusion
  693.8 3.3 copy.78
  697.1 3.4 copy.81
  700.6 1.5 copy.79
  703.3 12.3 %collective-permute-start = (bf16[128,2048]{1,0:T(8,128)(2,1)S(1)}, bf16[128,2048]{1,0:T(8,128)(2,1)S(1)}, u32[]{:S(2)}, u32[]{:S(2)}) collective-permute-start(bf16[128,2048]{1,0:T(8,128)(2,1)S(1)} %add_convert_fusion), channel_id=1, source_target_pairs={{0,1},{1,0},{2,3},{3,2},{4,5},{5,4},{6,7},{7,6},{8,9},{9,8},{10,11... | collective-permute-start | bytes 1572872 | tf_op jit(solution)/shard_map/ppermute | solution.py:1737
  (126 shorter events, 35.2 us)
Async XLA Ops:
  7.2 6.6 copy-start
  7.2 7.4 %copy-start.39 = (bf16[256,2048]{1,0:T(8,128)(2,1)S(1)}, bf16[256,2048]{1,0:T(8,128)(2,1)}, u32[]{:S(2)}) copy-start(bf16[256,2048]{1,0:T(8,128)(2,1)} %param.14) | copy-start | bytes 3145732
  7.2 8.2 %copy-start.43 = (s32[13]{0:T(128)S(1)}, s32[13]{0:T(128)}, u32[]{:S(2)}) copy-start(s32[13]{0:T(128)} %param.15) | copy-start | bytes 160
  7.2 694.9 %reduce-scatter.2.cloned.1.call-start = ((), (), s32[]{:S(2)}) async-start(), calls=%async_computation.1 | async-start | bytes 2621440 | tf_op jit(solution)/shard_map/reduce_scatter | solution.py:1735
  271.1 10.3 %copy-start.34 = (bf16[4,128,2048]{2,1,0:T(8,128)(2,1)S(1)}, bf16[4,128,2048]{2,1,0:T(8,128)(2,1)}, u32[]{:S(2)}) copy-start(bf16[4,128,2048]{2,1,0:T(8,128)(2,1)} %get-tuple-element.63) | copy-start | bytes 6291460
  271.1 10.3 %copy-start.42 = (bf16[2,2,2,2,128,1408]{5,4,3,2,1,0:T(8,128)(2,1)S(1)}, bf16[2,2,2,2,128,1408]{5,4,3,2,1,0:T(8,128)(2,1)}, u32[]{:S(2)}) copy-start(bf16[2,2,2,2,128,1408]{5,4,3,2,1,0:T(8,128)(2,1)} %get-tuple-element.62) | copy-start | bytes 17301508
  285.9 6.6 copy-start.36
  285.9 6.6 copy-start.37
  291.8 52.9 %collective-permute-start.1 = (bf16[16,512]{1,0:T(8,128)(2,1)S(1)}, bf16[16,512]{1,0:T(8,128)(2,1)S(1)}, u32[]{:S(2)}, u32[]{:S(2)}) collective-permute-start(bf16[16,512]{1,0:T(8,128)(2,1)S(1)} %get-tuple-element.142), channel_id=1, source_target_pairs={{0,1},{1,0},{2,3},{3,2},{4,5},{5,4},{6,7},{7,6},{8,9},{9,8},{10,11... | collective-permute-start | bytes 49160 | tf_op jit(solution)/shard_map/ppermute | solution.py:1722
  314.7 1.6 copy-start.3
  317.7 8.9 %copy-start.4 = (bf16[512,2048]{0,1:T(8,128)(2,1)S(1)}, bf16[512,2048]{0,1:T(8,128)(2,1)}, u32[]{:S(2)}) copy-start(bf16[512,2048]{0,1:T(8,128)(2,1)} %copy.71) | copy-start | bytes 6291460
  339.1 1.6 copy-start.7
  340.7 4.0 copy-start.41
  528.2 2.1 copy-start.2
  529.9 9.4 %copy-start.38 = (bf16[4,128,2048]{2,1,0:T(8,128)(2,1)S(1)}, bf16[4,128,2048]{2,1,0:T(8,128)(2,1)}, u32[]{:S(2)}) copy-start(bf16[4,128,2048]{2,1,0:T(8,128)(2,1)} %get-tuple-element.84) | copy-start | bytes 6291460
  539.2 8.3 %copy-start.40 = (bf16[4,128,128]{2,1,0:T(8,128)(2,1)S(1)}, bf16[4,128,128]{2,1,0:T(8,128)(2,1)}, u32[]{:S(2)}) copy-start(bf16[4,128,128]{2,1,0:T(8,128)(2,1)} %get-tuple-element.86) | copy-start | bytes 393220
  539.2 10.0 %copy-start.17 = (bf16[512,1024]{1,0:T(8,128)(2,1)S(1)}, bf16[512,1024]{1,0:T(8,128)(2,1)}, u32[]{:S(2)}) copy-start(bf16[512,1024]{1,0:T(8,128)(2,1)} %get-tuple-element.93) | copy-start | bytes 3145732
  539.2 10.0 %copy-start.18 = (bf16[2,128,1408]{2,1,0:T(8,128)(2,1)S(1)}, bf16[2,128,1408]{2,1,0:T(8,128)(2,1)}, u32[]{:S(2)}) copy-start(bf16[2,128,1408]{2,1,0:T(8,128)(2,1)} %get-tuple-element.95.refs_12_) | copy-start | bytes 2162692
  539.2 10.0 %copy-start.19 = (bf16[2,128,1408]{2,1,0:T(8,128)(2,1)S(1)}, bf16[2,128,1408]{2,1,0:T(8,128)(2,1)}, u32[]{:S(2)}) copy-start(bf16[2,128,1408]{2,1,0:T(8,128)(2,1)} %get-tuple-element.96.refs_13_) | copy-start | bytes 2162692
  547.6 1.7 copy-start.5
  547.6 2.2 copy-start.10
  547.6 2.6 copy-start.15
  547.6 2.9 copy-start.16
  547.6 2.9 copy-start.27
  547.6 2.9 copy-start.28
  547.6 2.9 copy-start.29
  685.8 3.0 copy-start.26
  685.8 6.2 copy-start.21
  685.8 6.2 copy-start.23
  700.6 16.4 %copy-start.31 = (f32[24,128]{1,0:T(8,128)S(1)}, f32[24,128]{1,0:T(8,128)}, u32[]{:S(2)}) copy-start(f32[24,128]{1,0:T(8,128)} %copy-done.30) | copy-start | bytes 36868
  703.3 14.8 %collective-permute-start = (bf16[128,2048]{1,0:T(8,128)(2,1)S(1)}, bf16[128,2048]{1,0:T(8,128)(2,1)S(1)}, u32[]{:S(2)}, u32[]{:S(2)}) collective-permute-start(bf16[128,2048]{1,0:T(8,128)(2,1)S(1)} %add_convert_fusion), channel_id=1, source_target_pairs={{0,1},{1,0},{2,3},{3,2},{4,5},{5,4},{6,7},{7,6},{8,9},{9,8},{10,11... | collective-permute-start | bytes 1572872 | tf_op jit(solution)/shard_map/ppermute | solution.py:1737
  718.2 2.1 copy-start.1
  (15 other events, 15.9 us)
Sparse Core Ops, SparseCore 0:
  291.9 74.6 reduce-scatter.1

commit v4 on v3

--- a/solution.py
+++ b/solution.py
@@ -577,7 +577,7 @@
         mixer_in, mixer_out, ffn_in, ffn_out, small, ups, own, cot, starts_row, starts_column, head_gain,
         mixer_w, merge_w, pair_w, down_w, gains, cots, hidden, low_rank, gate, cumulated, projected, mixed, gated,
         befores, decay, second, middle,
-        mixer_v, merge_v, projected_v, befores_v, inputs, smalls, ups_got, columns, state, partial, got, relayed, staged, line,
+        mixer_v, merge_v, projected_v, updates, inputs, smalls, ups_got, columns, state, partial, got, relayed, staged, line,
         own_send, own_arrive, far_send, arrive, small_send, small_arrive, ups_sem, inputs_send, inputs_arrive,
         cot_send, cot_arrive, sum_send, sum_arrive, spread_send, spread_arrive, saves,
     ) = refs[:-STATE_REFS]
@@ -728,6 +728,8 @@
     pass_side(1)
     pass_side(2)
     pass_high(0)
+    for part in (5, 6, 7):
+        send_own(part)
     complete(1)
     project(1)
     complete(2)
@@ -746,7 +748,7 @@
         end = b[CHUNK - 1 :]
         kc = low(projected_v[1, n] * jnp.exp(end - b) * last)
         update = dot_rows(low(projected_v[2, n]), kc)
-        befores_v[n] = update
+        updates[n] = update
         carry = keep * jnp.exp(end)
         state[...] = carry * state[...] + update
         decay[...] = decay[...] * carry
@@ -757,8 +759,6 @@
     states.begin()
     pass_side(0)
     pass_high(4)
-    for part in (5, 6, 7):
-        send_own(part)
     complete(0)
     project(0)
     states.combine()
@@ -788,16 +788,14 @@
         qd = low(projected_v[0, n] * jnp.exp(b) * visible)
         out = mixed[n] + dot_last(qd, low(before))
         mixed[n] = out
-        update = befores_v[n]
-        befores_v[n] = before
-        state[...] = keep * jnp.exp(b[CHUNK - 1 :]) * before + update
+        befores[n] = low(before)
+        state[...] = keep * jnp.exp(b[CHUNK - 1 :]) * before + updates[n]
         scale = lax.rsqrt(jnp.mean(out * out, -1, keepdims=True) + HEAD_FLOOR)
         u = projected_v[3, n]
         gated[n] = low(out * scale * head_gain[...] * (u * jax.nn.sigmoid(u)))
         return 0
 
     lax.fori_loop(0, chunks, outer_step, 0)
-    save(befores_v, befores)
     complete(4)
 
     def merge_step(n, _):
@@ -903,7 +901,7 @@
         (shape(4, chunks, CHUNK, HD, kind=F32), ANY),
         (shape(chunks, CHUNK, HD, kind=F32), VMEM),
         (shape(chunks, CHUNK, HD), VMEM),
-        (shape(chunks, HD, HD, kind=F32), ANY),
+        (shape(chunks, HD, HD), VMEM),
         (shape(8, HD, kind=F32), VMEM),
         (shape(TEAM, half, width), VMEM),
         (shape(half, width, kind=F32), VMEM),
@@ -913,7 +911,7 @@
         shapes[0][0],
         shapes[1][0],
         shapes[10][0],
-        shapes[13][0],
+        shape(chunks, HD, HD, kind=F32),
         shape(TEAM, half, width),
         shape(chips, rows, LANES),
         shape(*ups.shape, kind=F32),
@@ -956,125 +954,190 @@
 TILE = 256
 
 
-def grads_kernel(count, *refs):
-    lefts, rights = refs[:count], refs[count : 2 * count]
-    away, keep = refs[2 * count : 2 * count + 2]
-    ordered = refs[2 * count + 2 : 3 * count + 2]
-    out, got, send, arrive = refs[3 * count + 2 :]
-    zh, y, c = lax.axis_index("zh"), lax.axis_index("y"), lax.axis_index("c")
-    highs = lax.axis_size("zh")
-    chips, rows, _ = lefts[0].shape
-    half = chips // 2 * rows
+def turn_rows(me, source, target):
+    zh, y, highs = lax.axis_index("zh"), lax.axis_index("y"), lax.axis_size("zh")
+    chunks, _, width = source.shape
+    owners = highs * 8
+    rows = width // owners
+    for n in range(chunks):
+        turned = source[n].T
+        for chip in range(owners):
+            at_zh, zl, at_y, x = chip // 8, chip // 4 % 2, chip // 2 % 2, chip % 2
+            x_place = me.c if x == 1 else 1 - me.c
+            y_place = y if at_y == 1 else 1 - y
+            place = ((x_place * 2 + y_place) * highs + lax.rem(at_zh - zh + highs, highs)) * 2 + zl
+            at = pl.ds(pl.multiple_of(place * rows, rows), rows)
+            target[at, n * CHUNK : (n + 1) * CHUNK] = turned[chip * rows : (chip + 1) * rows]
+
+
+def feed_forward_kernel(
+    hidden, cots, pair_w, down_w,
+    forth, back, pair_away, pair_keep, down_part,
+    pair_v, down_v, act, grad_gate, grad_up, left_hidden, left_cots, tiles, tiles_got, down_away, down_keep,
+    loads, tile_send, tile_arrive, side,
+):
+    me = Place()
+    y = lax.axis_index("y")
+    chunks, _, width = hidden.shape
+    units = down_w.shape[1]
+    tokens = chunks * CHUNK
+    barrier = pltpu.get_barrier_semaphore()
+    for to in ({"c": 1 - me.c}, {"y": 1 - y}):
+        pl.semaphore_signal(barrier, inc=1, device_id=to, device_id_type=MESH)
+    spans = [(n * TILE, min(TILE, units - n * TILE)) for n in range(-(-units // TILE))]
+
+    def load(kind, n):
+        start, size = spans[n]
+        if kind == 2:
+            return pltpu.make_async_copy(
+                down_w.at[:, pl.ds(start, size)], down_v.at[:, pl.ds(start, size)], loads.at[2, n]
+            )
+        at = pl.ds(kind * units + start, size)
+        return pltpu.make_async_copy(pair_w.at[:, at], pair_v.at[:, at], loads.at[kind, n])
+
+    for n in range(len(spans)):
+        for kind in range(3):
+            load(kind, n).start()
+    turn_rows(me, cots, left_cots)
+
+    def units_step(start, size):
+        at = pl.ds(start, size)
+        rows = hidden[...].reshape(tokens, width)
+        a = dot(rows, pair_v[:, at])
+        b = dot(rows, pair_v[:, pl.ds(units + start, size)])
+        da = dot(cots[...].reshape(tokens, width), down_v[:, at])
+        sig = jax.nn.sigmoid(a)
+        silu = a * sig
+        act[:, at] = low(silu * b)
+        grad_gate[:, at] = low(da * b * sig * (1.0 + a * (1.0 - sig)))
+        grad_up[:, at] = low(da * silu)
+
+    for n, (start, size) in enumerate(spans):
+        for kind in range(3):
+            load(kind, n).wait()
+        if size < TILE:
+            units_step(start, size)
+    whole = units // TILE
+
+    def whole_step(n, _):
+        units_step(pl.multiple_of(n * TILE, TILE), TILE)
+        return 0
+
+    lax.fori_loop(0, whole, whole_step, 0)
+    pl.semaphore_wait(barrier, 2)
+
+    half = width // 2
     quarter = half // 2
-    barrier = pltpu.get_barrier_semaphore()
-    pl.semaphore_signal(barrier, inc=1, device_id={"c": 1 - c}, device_id_type=MESH)
-    for left, order in zip(lefts, ordered):
-        n = 0
-        for x in (1 - c, c):
-            for at_y in (1 - y, y):
-                for k in range(highs):
-                    for zl in range(2):
-                        chip = chip_index(lax.rem(zh + k, highs), zl, at_y, x)
-                        order[pl.ds(n * rows, rows)] = left[chip]
-                        n += 1
-    pl.semaphore_wait(barrier, 1)
+    count = len(spans)
 
     def move(n):
-        return pltpu.make_async_remote_copy(
-            src_ref=out.at[n],
-            dst_ref=got.at[n],
-            send_sem=send.at[n],
-            recv_sem=arrive.at[n],
-            device_id={"c": 1 - c},
-            device_id_type=MESH,
+        return copy_to(
+            tiles.at[lax.rem(n, count)], tiles_got.at[n], tile_send.at[n], tile_arrive.at[n], {"c": 1 - me.c}
         )
 
-    def send_tile(order, right, n, column, width):
-        block = dot(order[pl.ds(0, half)], right[:, pl.ds(column, width)])
-        if width == TILE:
-            out[n] = low(block)
+    def send_tile(left, right, n, start, size):
+        block = low(dot(left[pl.ds(0, half)], right[:, pl.ds(start, size)]))
+        if size == TILE:
+            tiles[lax.rem(n, count)] = block
         else:
-            out[n, :, pl.ds(0, width)] = low(block)
+            tiles[lax.rem(n, count), :, pl.ds(0, size)] = block
         move(n).start()
 
-    def add_tile(order, right, n, column, width, start):
-        block = dot(order[pl.ds(half, half)], right[:, pl.ds(column, width)])
+    def add_tile(left, right, n, start, size, away, keep, base):
+        block = dot(left[pl.ds(half, half)], right[:, pl.ds(start, size)])
         move(n).wait_recv()
-        block = low(block + got[n, :, pl.ds(0, width)].astype(F32))
-        away[:, pl.ds(start + column, width)] = block[:quarter]
-        keep[:, pl.ds(start + column, width)] = block[quarter:]
-
-    tile, start = 0, 0
-    for order, right in zip(ordered, rights):
-        whole, odd = right.shape[1] // TILE, right.shape[1] % TILE
-
-        def send_step(n, _, order=order, right=right, tile=tile):
-            send_tile(order, right, tile + n, pl.multiple_of(n * TILE, TILE), TILE)
+        block = low(block + tiles_got[n, :, pl.ds(0, size)].astype(F32))
+        away[:, pl.ds(base + start, size)] = block[:quarter]
+        keep[:, pl.ds(base + start, size)] = block[quarter:]
+
+    def weight_grad(part, left, right, away, keep, base):
+        first = part * count
+
+        def send_step(n, _):
+            if part:
+                move(first + n - count).wait_send()
+            send_tile(left, right, first + n, pl.multiple_of(n * TILE, TILE), TILE)
             return 0
 
+        def add_step(n, _):
+            add_tile(left, right, first + n, pl.multiple_of(n * TILE, TILE), TILE, away, keep, base)
+            return 0
+
         lax.fori_loop(0, whole, send_step, 0)
-        if odd:
-            send_tile(order, right, tile + whole, whole * TILE, odd)
-        tile += whole + (odd > 0)
-    total = tile
-    tile = 0
-    for order, right in zip(ordered, rights):
-        whole, odd = right.shape[1] // TILE, right.shape[1] % TILE
-
-        def add_step(n, _, order=order, right=right, tile=tile, start=start):
-            add_tile(order, right, tile + n, pl.multiple_of(n * TILE, TILE), TILE, start)
-            return 0
-
+        if whole < count:
+            if part:
+                move(first + whole - count).wait_send()
+            send_tile(left, right, first + whole, *spans[whole])
         lax.fori_loop(0, whole, add_step, 0)
-        if odd:
-            add_tile(order, right, tile + whole, whole * TILE, odd, start)
-        tile += whole + (odd > 0)
-        start += right.shape[1]
-
-    def sent(n, _):
+        if whole < count:
+            add_tile(left, right, first + whole, *spans[whole], away, keep, base)
+
+    weight_grad(0, left_cots, act, down_away, down_keep, 0)
+    side_move = copy_to(down_away, down_part, side.at[0], side.at[1], {"y": 1 - y})
+    side_move.start()
+
+    def back_step(n, _):
+        at = pl.ds(pl.multiple_of(n * TILE, TILE), TILE)
+        block = dot_last(grad_gate[...], pair_v[at, pl.ds(0, units)])
+        block = low(block + dot_last(grad_up[...], pair_v[at, pl.ds(units, units)]))
+        ahead = low(dot_last(act[...], down_v[at]))
+        for k in range(chunks):
+            back[k, :, at] = block[k * CHUNK : (k + 1) * CHUNK]
+            forth[k, :, at] = ahead[k * CHUNK : (k + 1) * CHUNK]
+        return 0
+
+    lax.fori_loop(0, width // TILE, back_step, 0)
+    turn_rows(me, hidden, left_hidden)
+    weight_grad(1, left_hidden, grad_gate, pair_away, pair_keep, 0)
+    weight_grad(2, left_hidden, grad_up, pair_away, pair_keep, units)
+    for n in range(2 * count, 3 * count):
         move(n).wait_send()
-        return 0
-
-    lax.fori_loop(0, total, sent, 0)
-
-
-def weight_grads(call_id, pairs):
-    highs = lax.axis_size("zh")
-    count = len(pairs)
-    team_tokens, width = pairs[0][0].shape
-    chips = highs * 8
-    rows = width // chips
-    lefts = [left.T.reshape(chips, rows, team_tokens) for left, _ in pairs]
-    rights = [right for _, right in pairs]
-    cols = sum(r.shape[1] for r in rights)
-    tiles = sum(-(-r.shape[1] // TILE) for r in rights)
-    half = width // 2
-    shape = jax.ShapeDtypeStruct((half // 2, cols), BF)
-    size = 4 * count * width * team_tokens + 2 * team_tokens * cols + 2 * half * cols
-    size += 4 * half * tiles * TILE
-    away, keep = pl.pallas_call(
-        functools.partial(grads_kernel, count),
-        out_shape=(shape, shape),
-        in_specs=[VMEM] * (2 * count),
-        out_specs=(VMEM, VMEM),
-        scratch_shapes=[pltpu.VMEM((width, team_tokens), BF)] * count
-        + [
-            pltpu.VMEM((tiles, half, TILE), BF),
-            pltpu.VMEM((tiles, half, TILE), BF),
-            DMA((tiles,)),
-            DMA((tiles,)),
-        ],
+    side_move.wait()
+    add_rows(down_part, down_keep, down_part)
+
+
+def feed_forward(hidden, cots, pair_w, down_w):
+    chunks, _, width = hidden.shape
+    units = down_w.shape[1]
+    tokens, half = chunks * CHUNK, width // 2
+    count = -(-units // TILE)
+
+    def shape(*dims, kind=BF):
+        return jax.ShapeDtypeStruct(dims, kind)
+
+    shapes = [
+        shape(*hidden.shape),
+        shape(*hidden.shape),
+        shape(half // 2, 2 * units),
+        shape(half // 2, 2 * units),
+        shape(half // 2, units),
+    ]
+    scratch = [
+        shape(width, 2 * units),
+        shape(width, units),
+        shape(tokens, units),
+        shape(tokens, units),
+        shape(tokens, units),
+        shape(width, tokens),
+        shape(width, tokens),
+        shape(count, half, TILE),
+        shape(3 * count, half, TILE),
+        shape(half // 2, units),
+        shape(half // 2, units),
+    ]
+    size = sum(a.size * a.dtype.itemsize for a in [hidden, cots] + shapes + scratch)
+    sems = [(3, count), (3 * count,), (3 * count,), (2,)]
+    return pl.pallas_call(
+        feed_forward_kernel,
+        out_shape=shapes,
+        in_specs=[VMEM, VMEM, ANY, ANY],
+        out_specs=[VMEM] * len(shapes),
+        scratch_shapes=[pltpu.VMEM(a.shape, a.dtype) for a in scratch] + [DMA(n) for n in sems],
         compiler_params=pltpu.CompilerParams(
-            collective_id=call_id, has_side_effects=True, vmem_limit_bytes=size + (8 << 20)
+            collective_id=5, has_side_effects=True, vmem_limit_bytes=min(size + (10 << 20), 63 << 20)
         ),
-        name=f"grads_{call_id}",
-    )(*lefts, *rights)
-    shape = (highs, 2, rows, cols)
-    return away.reshape(shape), keep.reshape(shape)
-
-
-def together(*values):
-    return lax.optimization_barrier(values)
+        name="feed_forward",
+    )(hidden, cots, pair_w, down_w)
 
 
 def add_rows(out, *parts):
@@ -1091,64 +1154,66 @@
 
 def backward_kernel(*refs):
     (
-        back, cot, middle, gain, pair_away, pair_keep, down_away, down_keep, merge_w, gated, projected, mixed,
+        back, forth, cot, middle, gain, pair_away, pair_keep, downs, merge_w, gated, projected, mixed,
         cumulated, gate, befores, decay, low_rank, up_pad, head_gain, hidden, starts_row, starts_column,
-        grad_middle, gain_grad, proj, ranks, heads, early_away, early_keep, gate_sum, up_part, down_sum,
-        got, relayed, staged, line, branch, left_hidden, left_branch, normed_grad, douts, tiles, tiles_got,
-        pair_side, down_side, gate_got, down_got, up_grad, state,
+        grad_middle, gain_grad, proj, ranks, heads, early_away, early_keep, gate_sum, up_sum, down_sum, left_hidden,
+        result, got, relayed, staged, line, got2, relayed2, staged2, line2, branch, left_branch, douts, tiles, tiles_got,
+        pair_side, gate_got, up_got, down_got, up_grad, state,
         send, arrive, send2, arrive2, side_send, side_arrive, high_send, high_arrive, tile_send, tile_arrive,
+        send3, arrive3, twin_send, twin_arrive, here,
     ) = refs[:-STATE_REFS]
     me = Place()
     zh, y, highs = lax.axis_index("zh"), lax.axis_index("y"), lax.axis_size("zh")
     chunks, _, width = hidden.shape
-    units = down_keep.shape[-1]
+    units = downs.shape[-1]
     first = ((zh * 2 + me.c) * 2 + y) * (chunks * CHUNK)
     greet_all(me)
 
-    def side_part(part, pair, down):
-        return down if part == 0 else pair.at[:, :, :, pl.ds((part - 1) * units, units)]
+    def columns(ref, part):
+        return ref.at[:, :, :, pl.ds((part - 1) * units, units)]
+
+    def source(part):
+        return downs if part == 0 else columns(pair_side, part)
 
     sides = [
-        copy_to(
-            side_part(p, pair_away, down_away),
-            side_part(p, pair_side, down_side),
-            side_send.at[p],
-            side_arrive.at[p],
-            {"y": 1 - y},
-        )
-        for p in range(3)
-    ]
+        copy_to(columns(pair_away, p), columns(pair_side, p), side_send.at[p], side_arrive.at[p], {"y": 1 - y})
+        for p in (1, 2)
+    ]
+    high_got, high_sum = (down_got, gate_got, up_got), (down_sum, gate_sum, up_sum)
     highs_moves = [
         [
             copy_to(
-                side_part(p, pair_side, down_side).at[k],
-                (down_got if p == 0 else gate_got).at[k - 1],
+                source(p).at[k],
+                high_got[p].at[k - 1],
                 high_send.at[p, k],
                 high_arrive.at[p, k],
                 {"zh": lax.rem(zh + k, highs)},
             )
             for k in range(1, highs)
         ]
-        for p in range(2)
-    ]
-
-    def side_add(part):
-        sides[part].wait()
-        mine, there = side_part(part, pair_keep, down_keep), side_part(part, pair_side, down_side)
-        out = up_part if part == 2 else there
-        for k in range(highs):
-            for m in range(2):
-                add_rows(out.at[k, m], mine.at[k, m], there.at[k, m])
+        for p in range(3)
+    ]
+
+    def high_start(part):
+        if part:
+            sides[part - 1].wait()
+            mine, there = columns(pair_keep, part), columns(pair_side, part)
+            for k in range(highs):
+                for m in range(2):
+                    add_rows(there.at[k, m], mine.at[k, m], there.at[k, m])
+        for move in highs_moves[part]:
+            move.start()
 
     def high_add(part):
-        source, there = side_part(part, pair_side, down_side), (down_got if part == 0 else gate_got)
-        out = down_sum if part == 0 else gate_sum
+        there, out = high_got[part], high_sum[part]
         for k in range(1, highs):
             wait_for(there.at[k - 1], high_arrive.at[part, k])
         for m in range(2):
-            add_rows(out.at[m], source.at[0, m], *(there.at[k - 1, m] for k in range(1, highs)))
-
-    sides[0].start()
+            add_rows(out.at[m], source(part).at[0, m], *(there.at[k - 1, m] for k in range(1, highs)))
+
+    for move in sides:
+        move.start()
+    high_start(0)
 
     steps = send.shape[0]
     rows = cot.shape[0] // steps
@@ -1179,25 +1244,35 @@
         )
         for n in range(steps)
     ]
+    forth_sums = [
+        MemberSum(
+            me,
+            lambda k, n=n: part(forth, k, n),
+            lambda k, n=n: part(got2, k, n),
+            lambda k, n=n: part(relayed2, k, n),
+            lambda k, n=n: part(staged2, k, n),
+            send3.at[n],
+            arrive3.at[n],
+        )
+        for n in range(steps)
+    ]
+
+    def twin_copy(n):
+        return copy_to(
+            line2.at[pl.ds(n * rows, rows)],
+            part(result, me.c, n),
+            twin_send.at[n],
+            twin_arrive.at[n],
+            {"c": 1 - me.c},
+        )
+
+    def own_copy(n):
+        return pltpu.make_async_copy(line2.at[pl.ds(n * rows, rows)], part(result, me.c, n), here.at[n])
+
     for transfer in sums:
         transfer.start()
 
-    owners = highs * 8
-    owner_rows = width // owners
-
-    def transpose(source, target):
-        for n in range(chunks):
-            turned = source[n].T
-            for chip in range(owners):
-                at_zh, zl, at_y, x = chip // 8, chip // 4 % 2, chip // 2 % 2, chip % 2
-                x_place = me.c if x == 1 else 1 - me.c
-                x_place = jnp.where(x_place == 1, 1, 0)
-                y_place = jnp.where((y if at_y == 1 else 1 - y) == 1, 1, 0)
-                place = ((x_place * 2 + y_place) * highs + lax.rem(at_zh - zh + highs, highs)) * 2 + zl
-                at = pl.ds(pl.multiple_of(place * owner_rows, owner_rows), owner_rows)
-                target[at, n * CHUNK : (n + 1) * CHUNK] = turned[chip * owner_rows : (chip + 1) * owner_rows]
-
-    transpose(hidden, left_hidden)
+    turn_rows(me, hidden, left_hidden)
     for transfer in sums:
         transfer.relay()
     for n in range(steps):
@@ -1217,13 +1292,13 @@
         spreads[n].start()
         if n:
             spreads[n - 1].relay()
+        if n == 2:
+            high_start(1)
     spreads[steps - 1].relay()
-    side_add(0)
-    for move in highs_moves[0]:
-        move.start()
-    sides[1].start()
     for transfer in spreads:
         transfer.wait()
+    for transfer in forth_sums:
+        transfer.start()
 
     heads[...] = jnp.zeros_like(heads)
 
@@ -1261,8 +1336,9 @@
     lax.fori_loop(0, chunks, local_step, 0)
     states = StatePass(True, state, decay, state, *refs[-STATE_REFS:])
     states.begin()
-
-    transpose(branch, left_branch)
+    high_start(2)
+
+    turn_rows(me, branch, left_branch)
     half = width // 2
     quarter = half // 2
 
@@ -1292,10 +1368,8 @@
             early_away[:, at] = block[:quarter]
             early_keep[:, at] = block[quarter:]
     states.spread()
-    side_add(1)
-    for move in highs_moves[1]:
-        move.start()
-    sides[2].start()
+    for transfer in forth_sums:
+        transfer.relay()
     states.finish()
 
     upper = (
@@ -1338,11 +1412,21 @@
 
     lax.fori_loop(0, chunks, chunk_step, 0)
     heads[0:16] = up_grad[2:18]
-    high_add(0)
-    side_add(2)
-    high_add(1)
-    for move in highs_moves[0] + highs_moves[1]:
-        move.wait_send()
+    for n in range(steps):
+        at = pl.ds(n * rows, rows)
+        line2[at] = low(middle[at] + forth_sums[n].total())
+        twin_copy(n).start()
+        own_copy(n).start()
+    for p in range(3):
+        high_add(p)
+    for n in range(steps):
+        twin_copy(n).wait()
+        own_copy(n).wait()
+    for transfer in forth_sums:
+        transfer.wait_sent()
+    for group in highs_moves:
+        for move in group:
+            move.wait_send()
     for transfer in sums:
         transfer.wait_sent()
     for tile in range(tiles.shape[0]):
@@ -1351,10 +1435,10 @@
 
 
 def backward(
-    back, cot, middle, gain, pair, down, merge_w, gated, projected, mixed, cumulated, gate, befores, decay,
+    back, forth, cot, middle, gain, pair, downs, merge_w, gated, projected, mixed, cumulated, gate, befores, decay,
     low_rank, up_pad, head_gain, hidden, starts,
 ):
-    highs, members, owner_rows, units = down[0].shape
+    highs, members, owner_rows, units = downs.shape
     rows, width = cot.shape
     chunks = hidden.shape[0]
 
@@ -1362,10 +1446,10 @@
         return jax.ShapeDtypeStruct(dims, kind)
 
     arrays = [
-        back, cot, middle, gain, *pair, *down, merge_w, gated, projected, mixed, cumulated, gate, befores, decay,
+        back, forth, cot, middle, gain, *pair, downs, merge_w, gated, projected, mixed, cumulated, gate, befores, decay,
         low_rank, up_pad, head_gain, hidden, *starts_arrays(starts),
     ]
-    away = {4, 6}
+    away = {5}
     quarter = width // 4
     shapes = [
         shape(rows, width, kind=F32),
@@ -1376,8 +1460,10 @@
         shape(quarter, 2 * HD),
         shape(quarter, 2 * HD),
         shape(members, owner_rows, units),
-        shape(highs, members, owner_rows, units),
         shape(members, owner_rows, units),
+        shape(members, owner_rows, units),
+        shape(width, chunks * CHUNK),
+        shape(2, rows, width),
     ]
     tiles = 2 * HD // TILE
     scratch = [
@@ -1385,15 +1471,17 @@
         shape(1, rows, width),
         shape(1, rows, width),
         shape(rows, width),
+        shape(2, rows, width),
+        shape(1, rows, width),
+        shape(1, rows, width),
+        shape(rows, width),
         shape(TEAM, rows, width),
         shape(width, chunks * CHUNK),
-        shape(width, chunks * CHUNK),
-        shape(8, HD, kind=F32),
         shape(chunks, CHUNK, HD),
         shape(tiles, width // 2, TILE),
         shape(tiles, width // 2, TILE),
         shape(highs, members, owner_rows, 2 * units),
-        shape(highs, members, owner_rows, units),
+        shape(highs - 1, members, owner_rows, units),
         shape(highs - 1, members, owner_rows, units),
         shape(highs - 1, members, owner_rows, units),
         shape(LANES, HD, kind=F32),
@@ -1402,7 +1490,8 @@
     used = [a for n, a in enumerate(arrays) if n not in away] + shapes + scratch
     size = sum(a.size * a.dtype.itemsize for a in used)
     sems = [
-        (STEPS, 3), (STEPS, 3), (STEPS, 5), (STEPS, 4), (3,), (3,), (2, highs), (2, highs), (tiles,), (tiles,),
+        (STEPS, 3), (STEPS, 3), (STEPS, 5), (STEPS, 4), (3,), (3,), (3, highs), (3, highs), (tiles,), (tiles,),
+        (STEPS, 3), (STEPS, 3), (STEPS,), (STEPS,), (STEPS,),
     ]
     return pl.pallas_call(
         backward_kernel,
@@ -1421,12 +1510,14 @@
 
 def closing_kernel(*refs):
     (
-        partial, own, grad_middle, gain, down, gain_two_grad, heads, late_away, late_keep, early_away, early_keep,
-        pair, gates, downs,
-        out, late_home, early_home, pair_home, gate_home, down_home, wide_out, heads_out, gains_out,
-        got, relayed, staged, line, late_side, late, early_side, early, late_got, early_got, pair_got, late_sum, early_sum, pair_sum,
+        proj, ranks, mixer_w, left, own, grad_middle, gain, down, gain_two_grad, heads, early_away, early_keep,
+        ups, gates, downs,
+        out, mixer_grad, merge_grad, pair_grad, down_grad, wide_out, heads_out, gains_out,
+        partial, got, relayed, staged, line, tiles, tiles_got, late_away, late_keep, late_side, early_side,
+        late_got, early_got, late_sum, early_sum, late_home, early_home, ups_home, gate_home, down_home,
         wide, wide_got, heads_got, heads_sum, wide_twin, gain_grad, rank_grad,
-        send, arrive, twin_send, twin_arrive, here, side_sem, high_send, high_arrive, home_send, home_arrive,
+        send, arrive, twin_send, twin_arrive, here, tile_send, tile_arrive, side_send, side_arrive,
+        high_send, high_arrive, home_send, home_arrive,
         wide_send, wide_arrive, heads_send, heads_arrive, near, out_send, out_arrive, gain_send, gain_arrive,
     ) = refs
     me = Place()
@@ -1434,6 +1525,7 @@
     greet_all(me)
     steps = send.shape[0]
     rows, width = own.shape[0] // steps, own.shape[1]
+    chunks = proj.shape[0]
     twin = {"c": 1 - me.c}
 
     def high_copies(kind, source, target):
@@ -1448,13 +1540,67 @@
             for k in range(1, highs)
         ]
 
-    side = copy_to(late_away, late_side, side_sem.at[0], side_sem.at[1], {"y": 1 - y})
-    early_move = copy_to(early_away, early_side, side_sem.at[2], side_sem.at[3], {"y": 1 - y})
+    def side_copy(kind, source, target):
+        return copy_to(source, target, side_send.at[kind], side_arrive.at[kind], {"y": 1 - y})
+
+    def home(kind, source, target):
+        return Transfer(
+            route_weights_home(me),
+            lambda k: source.at[k],
+            lambda k: target.at[k],
+            home_send.at[kind],
+            home_arrive.at[kind],
+        )
+
+    early_move = side_copy(3, early_away, early_side)
+    late_moves = [side_copy(j, late_away.at[j], late_side.at[j]) for j in range(3)]
+    high_moves = [high_copies(j, late_side.at[j], late_got.at[j]) for j in range(3)]
+    high_moves += [high_copies(3, early_side, early_got)]
+    homes = [home(j, late_sum.at[j], late_home.at[j]) for j in range(3)]
+    homes += [home(3, early_sum, early_home), home(4, ups, ups_home)]
+    homes += [home(5, gates, gate_home), home(6, downs, down_home)]
+    group_out, group_arrive = [], []
+    for n in range(highs):
+        for f in range(4):
+            to_zh, to_y, to_c = lax.rem(zh + n, highs), flip(y, f & 2), flip(me.c, f & 1)
+            to = {"zh": to_zh, "y": to_y, "c": to_c}
+            group_out.append((0, (zh * 2 + y) * 2 + me.c, to, n + f == 0))
+            group_arrive.append(((to_zh * 2 + to_y) * 2 + to_c, n + f == 0))
+    heads_move = Transfer(
+        (group_out, group_arrive), lambda _: heads, lambda k: heads_got.at[k], heads_send, heads_arrive
+    )
+    heads_move.start()
+
     early_move.start()
-    side.start()
-    early_moves = high_copies(0, early, early_got)
-    pair_moves = high_copies(1, pair, pair_got)
-    late_moves = high_copies(2, late, late_got)
+
+    half = width // 2
+    quarter = half // 2
+    owner_rows = early_keep.shape[2]
+
+    def tile_move(n):
+        return copy_to(tiles.at[n], tiles_got.at[n], tile_send.at[n], tile_arrive.at[n], twin)
+
+    def right_tile(n):
+        return proj[:, :, pl.ds(pl.multiple_of(n * TILE, TILE), TILE)].reshape(chunks * CHUNK, TILE)
+
+    def tile_step(n, _):
+        tiles[n] = low(dot(left[pl.ds(0, half)], right_tile(n)))
+        tile_move(n).start()
+        return 0
+
+    lax.fori_loop(0, 3 * HD // TILE, tile_step, 0)
+
+    for n in range(chunks):
+        partial[n, :, width:] = ranks[n]
+
+    def hidden_step(n, _):
+        at = pl.ds(pl.multiple_of(n * TILE, TILE), TILE)
+        block = low(dot_last(proj[...].reshape(chunks * CHUNK, 4 * HD), mixer_w[at]))
+        for k in range(chunks):
+            partial[k, :, at] = block[k * CHUNK : (k + 1) * CHUNK]
+        return 0
+
+    lax.fori_loop(0, width // TILE, hidden_step, 0)
 
     def part(ref, k, n):
         return ref.at[k, pl.ds(n * rows, rows)]
@@ -1473,25 +1619,38 @@
     ]
     for transfer in sums:
         transfer.start()
-    for move in pair_moves:
+
+    for j in range(3):
+        for i in range(HD // TILE):
+            n = j * (HD // TILE) + i
+            block = dot(left[pl.ds(half, half)], right_tile(n))
+            tile_move(n).wait_recv()
+            block = low(block + tiles_got[n].astype(F32))
+            columns = slice(i * TILE, (i + 1) * TILE)
+            for k in range(highs):
+                for m in range(2):
+                    at = (k * 2 + m) * owner_rows
+                    late_away[j, k, m, :, columns] = block[at : at + owner_rows]
+                    late_keep[j, k, m, :, columns] = block[quarter + at : quarter + at + owner_rows]
+        late_moves[j].start()
+    for n in (6, 5, 4):
+        homes[n].start()
+
+    def side_add(move, keep, there):
+        move.wait()
+        for k in range(highs):
+            for m in range(2):
+                add_rows(there.at[k, m], keep.at[k, m], there.at[k, m])
+
+    side_add(early_move, early_keep, early_side)
+    for move in high_moves[3]:
         move.start()
-
-    def home(n, source, target):
-        return Transfer(
-            route_weights_home(me),
-            lambda k: source.at[k],
-            lambda k: target.at[k],
-            home_send.at[n],
-            home_arrive.at[n],
-        )
-
-    homes = [
-        home(0, downs, down_home),
-        home(1, early_sum, early_home),
-        home(2, pair_sum, pair_home),
-        home(3, late_sum, late_home),
-        home(4, gates, gate_home),
-    ]
+    for transfer in sums:
+        transfer.relay()
+    for j in range(3):
+        side_add(late_moves[j], late_keep.at[j], late_side.at[j])
+        for move in high_moves[j]:
+            move.start()
 
     def twin_copy(n):
         return copy_to(
@@ -1501,16 +1660,6 @@
     def own_copy(n):
         return pltpu.make_async_copy(line.at[pl.ds(n * rows, rows)], part(out, me.c, n), here.at[n])
 
-    for transfer in sums:
-        transfer.relay()
-    homes[0].start()
-    homes[4].start()
-    early_move.wait()
-    for k in range(highs):
-        for m in range(2):
-            add_rows(early.at[k, m], early_keep.at[k, m], early_side.at[k, m])
-    for move in early_moves:
-        move.start()
     for n in range(steps):
         at = pl.ds(n * rows, rows)
         x = own[at].astype(F32)
@@ -1532,7 +1681,6 @@
         twin_copy(n).start()
         own_copy(n).start()
 
-    owner_rows = wide.shape[2]
     for n in range(wide.shape[0]):
         at = slice(n * owner_rows, (n + 1) * owner_rows)
         wide[n, 0:1] = gain_grad[:, at]
@@ -1543,24 +1691,13 @@
         route_all(me), lambda k: wide.at[k], lambda k: wide_got.at[k], wide_send, wide_arrive
     )
     spreads.start()
-    group_out, group_arrive = [], []
-    for n in range(highs):
-        for f in range(4):
-            to_zh, to_y, to_c = lax.rem(zh + n, highs), flip(y, f & 2), flip(me.c, f & 1)
-            to = {"zh": to_zh, "y": to_y, "c": to_c}
-            group_out.append((0, (zh * 2 + y) * 2 + me.c, to, n + f == 0))
-            group_arrive.append(((to_zh * 2 + to_y) * 2 + to_c, n + f == 0))
-    heads_move = Transfer(
-        (group_out, group_arrive), lambda _: heads, lambda k: heads_got.at[k], heads_send, heads_arrive
-    )
-    heads_move.start()
-
-    side.wait()
-    for k in range(highs):
+    def high_add(kind, source, target, total):
+        for k in range(1, highs):
+            wait_for(target.at[k - 1], high_arrive.at[kind, k])
         for m in range(2):
-            add_rows(late.at[k, m], late_keep.at[k, m], late_side.at[k, m])
-    for move in late_moves:
-        move.start()
+            add_rows(total.at[m], source.at[0, m], *(target.at[k - 1, m] for k in range(1, highs)))
+        homes[kind].start()
+
 
     heads_move.wait()
     total = heads_got[0]
@@ -1601,16 +1738,23 @@
     swap = copy_to(wide_out, wide_twin, near.at[0], near.at[1], twin)
     swap.start()
 
-    for n, kind_moves, source, target, total in (
-        (2, pair_moves, pair, pair_got, pair_sum),
-        (1, early_moves, early, early_got, early_sum),
-        (3, late_moves, late, late_got, late_sum),
-    ):
-        for k in range(1, highs):
-            wait_for(target.at[k - 1], high_arrive.at[n - 1, k])
-        for m in range(2):
-            add_rows(total.at[m], source.at[0, m], *(target.at[k - 1, m] for k in range(1, highs)))
-        homes[n].start()
+    units = gates.shape[-1]
+
+    def spread_columns(source, target, cols):
+        for k in range(2):
+            target[:, k * cols : (k + 1) * cols] = source[k].astype(F32)
+
+    def spread_rows(source, target, cols):
+        for k in range(2):
+            target[k * cols : (k + 1) * cols] = source[k, :, :cols].astype(F32).T
+
+    homes[6].wait()
+    spread_rows(down_home, down_grad, units)
+    homes[5].wait()
+    spread_columns(gate_home, pair_grad.at[0], units)
+    homes[4].wait()
+    spread_columns(ups_home, pair_grad.at[1], units)
+    high_add(3, early_side, early_got, early_sum)
     for k in range(2):
         own_slot = (me.c == me.zl) & (me.x == k)
         unless(own_slot, lambda k=k: wait_for(heads_out.at[k], out_arrive.at[k]))
@@ -1623,38 +1767,65 @@
     swap.wait()
     wide_out[...] = wide_out[...] + wide_twin[...]
     gains.wait()
+    for j in range(3):
+        high_add(j, late_side.at[j], late_got.at[j], late_sum.at[j])
+    homes[3].wait()
+    spread_rows(early_home, merge_grad, HD)
+    for k in range(2):
+        mixer_grad[3, :, k * HD : (k + 1) * HD] = early_home[k, :, HD:].astype(F32)
+    for j in range(3):
+        homes[j].wait()
+        spread_columns(late_home.at[j], mixer_grad.at[j], HD)
     for transfer in sums:
         transfer.wait_sent()
     for n in range(steps):
         twin_copy(n).wait()
         own_copy(n).wait()
-    for transfer in homes:
-        transfer.wait()
-    for move in early_moves + pair_moves + late_moves:
-        move.wait_send()
-
-
-def closing(partial, own, grad_middle, gain, down, gain_two_grad, heads, late, early, pair, gates, downs):
+    for group in high_moves:
+        for move in group:
+            move.wait_send()
+
+    def tile_sent(n, _):
+        tile_move(n).wait_send()
+        return 0
+
+    lax.fori_loop(0, tiles.shape[0], tile_sent, 0)
+
+
+def closing(proj, ranks, mixer_w, left, own, grad_middle, gain, down, gain_two_grad, heads, early, ups, gates, downs):
     rows, width = own.shape
-    lanes = partial.shape[-1] - width
-    highs, _, owner_rows, late_cols = late[0].shape
+    chunks = proj.shape[0]
+    highs, _, owner_rows, _ = early[0].shape
+    units = ups.shape[-1]
     chips = highs * 8
-    arrays = [partial, own, grad_middle, gain, down, gain_two_grad, heads, *late, *early, pair, gates, downs]
+    arrays = [
+        proj, ranks, mixer_w, left, own, grad_middle, gain, down, gain_two_grad, heads, *early, ups, gates, downs,
+    ]
 
     def shape(*dims, kind=BF):
         return jax.ShapeDtypeStruct(dims, kind)
 
-    cols = late_cols, early[0].shape[-1], pair.shape[-1], gates.shape[-1], downs.shape[-1]
-    shapes = [shape(2, rows, width)] + [shape(2, owner_rows, n) for n in cols]
-    shapes += [
+    shapes = [
+        shape(2, rows, width),
+        shape(4, owner_rows, 2 * HD, kind=F32),
+        shape(2 * HD, owner_rows, kind=F32),
+        shape(2, owner_rows, 2 * units, kind=F32),
+        shape(2 * units, owner_rows, kind=F32),
         shape(24, owner_rows, kind=F32),
         shape(2, *heads.shape, kind=F32),
         shape(TEAM, 8, heads.shape[1], kind=F32),
     ]
-    scratch = [shape(n, rows, width + lanes) for n in (3, 2, 2)] + [shape(rows, width)]
-    scratch += [shape(*late[0].shape)] * 2 + [shape(*early[0].shape)] * 2
-    scratch += [shape(highs - 1, 2, owner_rows, n) for n in cols[:3]]
-    scratch += [shape(2, owner_rows, n) for n in cols[:3]]
+    tiles = 3 * HD // TILE
+    late = (3, highs, 2, owner_rows, HD)
+    scratch = [shape(chunks, CHUNK, width + LANES)]
+    scratch += [shape(n, rows, width + LANES) for n in (3, 2, 2)] + [shape(rows, width)]
+    scratch += [shape(tiles, width // 2, TILE)] * 2 + [shape(*late)] * 3 + [shape(*early[0].shape)]
+    scratch += [
+        shape(3, highs - 1, 2, owner_rows, HD),
+        shape(highs - 1, 2, owner_rows, 2 * HD),
+    ]
+    sums = [shape(3, 2, owner_rows, HD), shape(2, owner_rows, 2 * HD)]
+    scratch += sums + sums + [shape(2, owner_rows, units)] * 3
     scratch += [
         shape(chips, 24, owner_rows, kind=F32),
         shape(chips, 24, owner_rows, kind=F32),
@@ -1662,12 +1833,12 @@
         shape(*heads.shape, kind=F32),
         shape(24, owner_rows, kind=F32),
         shape(1, width, kind=F32),
-        shape(lanes, width, kind=F32),
+        shape(LANES, width, kind=F32),
     ]
     size = sum(a.size * a.dtype.itemsize for a in arrays + shapes + scratch)
     sems = [
-        (STEPS, 6), (STEPS, 5), (STEPS,), (STEPS,), (STEPS,), (4,), (3, highs), (3, highs), (5, 2), (5, 2),
-        (chips,), (chips,), (highs * 4,), (highs * 4,), (2,), (3,), (2,), (TEAM,), (TEAM,),
+        (STEPS, 6), (STEPS, 5), (STEPS,), (STEPS,), (STEPS,), (tiles,), (tiles,), (4,), (4,), (4, highs), (4, highs),
+        (7, 2), (7, 2), (chips,), (chips,), (highs * 4,), (highs * 4,), (2,), (3,), (2,), (TEAM,), (TEAM,),
     ]
     return pl.pallas_call(
         closing_kernel,
@@ -1676,7 +1847,7 @@
         out_specs=[VMEM] * len(shapes),
         scratch_shapes=[pltpu.VMEM(a.shape, a.dtype) for a in scratch] + [DMA(n) for n in sems],
         compiler_params=pltpu.CompilerParams(
-            collective_id=4, has_side_effects=True, vmem_limit_bytes=size + (10 << 20)
+            collective_id=4, has_side_effects=True, vmem_limit_bytes=min(size + (10 << 20), 62 << 20)
         ),
         name="closing",
     )(*arrays)
@@ -1723,68 +1894,37 @@
     mixer_w, merge_w = mixer_w.reshape(width, 4 * HD), merge_w.reshape(width, HD)
     pair_w, down_w = pair_w.reshape(width, 2 * units), down_w.reshape(width, units)
     gain_one, gain_two, rank_down = gains[:1], gains[1:2], gains[2 : 2 + rank].astype(BF)
-    ffn_dy = ffn_dy.reshape(team_tokens, width)
-    hidden_two = hidden_two.reshape(team_tokens, width)
-
-    up_pair = dot(hidden_two, pair_w)
-    up_a, up_b = up_pair[:, :units], up_pair[:, units:]
-    ffn_sig = jax.nn.sigmoid(up_a)
-    ffn_silu = up_a * ffn_sig
-    activated = low(ffn_silu * up_b)
-    down = dot_last(activated, down_w).astype(BF)
-    down = lax.psum_scatter(down, ("zl", "x"), scatter_dimension=0, tiled=True).astype(F32)
-    result = (middle + down).astype(BF)
-    twin = lax.ppermute(result, "c", CROSS)
-    result = jnp.concatenate([jnp.where(c == 0, result, twin), jnp.where(c == 0, twin, result)], axis=0)
-
-    grad_act = dot(ffn_dy, down_w)
-    grad_gate = low(grad_act * up_b * ffn_sig * (1.0 + up_a * (1.0 - ffn_sig)))
-    grad_upper = low(grad_act * ffn_silu)
-    grad_pair = jnp.concatenate([grad_gate, grad_upper], axis=1)
-    back = dot_last(grad_pair, pair_w)
-    ffn_sums = weight_grads(12, [(ffn_dy, activated)]), weight_grads(13, [(hidden_two, grad_pair)])
-    back, ffn_sums = together(back, ffn_sums)
-    back = low(back).reshape(TEAM, half, width)
-    lanes = LANES
+    forth, back, *pair_sides, down_part = feed_forward(hidden_two, ffn_dy, pair_w, down_w)
+    highs = lax.axis_size("zh")
+    pair_sides = [a.reshape(highs, 2, rows, 2 * units) for a in pair_sides]
+    down_part = down_part.reshape(highs, 2, rows, units)
+    pad_rank = ((0, LANES - rank), (0, 0))
     (
-        grad_middle, grad_gain_two, grad_proj, grad_rank_part, heads, early_away, early_keep, gate_sum, up_part, down_sum,
+        grad_middle, grad_gain_two, grad_proj, grad_ranks, heads, early_away, early_keep, gate_sum, up_sum, down_sum,
+        left_hidden, result,
     ) = backward(
-        back, own_dy, middle, gain_two, ffn_sums[1], ffn_sums[0], merge_w, gated, projected, mixed, cumulated,
-        gate_input, befores, decay, low_rank, jnp.pad(up_head, ((0, lanes - rank), (0, 0))), head_gain[None],
-        hidden_one, starts,
+        back, forth, own_dy, middle, gain_two, pair_sides, down_part, merge_w, gated, projected, mixed, cumulated,
+        gate_input, befores, decay, low_rank, jnp.pad(up_head, pad_rank), head_gain[None], hidden_one, starts,
     )
-    grad_proj = grad_proj.reshape(team_tokens, 4 * HD)
-    hidden_part = dot_last(grad_proj, mixer_w)
-    hidden_part = jnp.concatenate(
-        [low(hidden_part).reshape(TEAM, half, width), grad_rank_part], axis=2
+    early_shape = (highs, 2, rows, 2 * HD)
+    early_sums = early_away.reshape(early_shape), early_keep.reshape(early_shape)
+    grad_inputs, mixer_home, merge_home, pair_home, down_home, wide, heads, gains = closing(
+        grad_proj, grad_ranks, mixer_w, left_hidden, own, grad_middle, gain_one, jnp.pad(rank_down, pad_rank),
+        grad_gain_two, heads, early_sums, up_sum, gate_sum, down_sum,
     )
-    late_sums = weight_grads(15, [(hidden_one.reshape(team_tokens, width), grad_proj[:, : 3 * HD])])
-    early_shape = late_sums[0].shape[:3] + (2 * HD,)
-    early_sums = early_away.reshape(early_shape), early_keep.reshape(early_shape)
-    down_pad = jnp.pad(rank_down, ((0, lanes - rank), (0, 0)))
-    grad_inputs, late_home, early_home, up_home, gate_home, ffn_down, wide, heads, gains = closing(
-        hidden_part, own, grad_middle, gain_one, down_pad, grad_gain_two, heads, late_sums, early_sums, up_part,
-        gate_sum, down_sum,
-    )
-    grad_inputs = grad_inputs.reshape(block, width)
-    ffn_pair = jnp.stack([gate_home, up_home]).astype(F32)
-    ffn_down = ffn_down.astype(F32)
-    early_home = early_home.reshape(2, rows, 2, HD).astype(F32)
-    late_home = late_home.reshape(2, rows, 3, HD).astype(F32)
-    mixer_home = jnp.concatenate([late_home, early_home[:, :, 1:]], axis=2)
     return (
-        result,
-        grad_inputs,
+        result.reshape(block, width),
+        grad_inputs.reshape(block, width),
         wide[0],
         wide[1],
-        mixer_home.transpose(2, 1, 0, 3).reshape(4, rows, 2 * HD),
+        mixer_home,
         wide[8 : 8 + rank].T,
         heads[:, :rank].transpose(1, 0, 2).reshape(rank, 2 * HD),
         heads[:, rank].reshape(2 * HD),
         jnp.sum(gains[:, rank + 1 - 16], axis=0),
-        early_home[:, :, 0].transpose(0, 2, 1).reshape(2 * HD, rows),
-        ffn_pair.transpose(0, 2, 1, 3).reshape(2, rows, 2 * units),
-        ffn_down.transpose(0, 2, 1).reshape(2 * units, rows),
+        merge_home,
+        pair_home,
+        down_home,
     )
 
 

time: 734 us -> 634 us (0.86)
  local copies, waits for them, and re-layouts: 70.3 us -> 26.6 us
  matrix products: 37.7 us -> 0 us
  Pallas kernels: 579 us -> 596 us
  between operations: 15 us -> 1.25 us
  starting transfers between devices: 12.9 us -> 0.45 us
  other arithmetic: 13.1 us -> 3.15 us
    pallas_call x3 -> x1, Pallas kernels: 24.2 us -> 64.2 us  [feed_forward(): pl.pallas_call(feed_forward_kernel, out_shape=shapes, in_specs=[VMEM, VME...]
    dot_general x5 -> x0, matrix products: 37.7 us -> none  [the longest x3 23 us: dot_last(): lax.dot_general(a, b, (((1,), (1,)), ((), ())), preferred_element_type=F32)]
    unnamed x95 -> x35, local copies, waits for them, and re-layouts: 30.7 us -> 11.4 us
    pallas_call x1, Pallas kernels: 183 us -> 164 us  [backward(): pl.pallas_call(backward_kernel, out_shape=shapes, in_specs=[ANY if n in a...]
    reshape x5 -> x0, local copies, waits for them, and re-layouts: 16.7 us -> none  [the longest x1 3.95 us: shards(): ffn_dy = ffn_dy.reshape(team_tokens, width)]
    ppermute x1 -> x0, starting transfers between devices: 12.3 us -> none  [shards(): twin = lax.ppermute(result, 'c', CROSS)]
    pallas_call x1, Pallas kernels: 253 us -> 244 us  [forward(): pl.pallas_call(forward_kernel, out_shape=[a for a, _ in shapes], in_specs...]
  transfers between devices with their start and end apart: 3 -> 1, of which waited for: 0 -> 0; matrix products, arithmetic and copies ran while one was open for 10% -> 2% of each run, Pallas kernels for 45% -> 49%
where the time goes in v4:
time: 634 us; the launch traced here: 627 us
  Pallas kernels  596 us (94%)
  local copies, waits for them, and re-layouts  26.6 us (4%)
    pallas_call x1, Pallas kernels, forward(): pl.pallas_call(forward_kernel, out_shape=[a for a, _ in shapes], in_specs...  244 us
    pallas_call x1, Pallas kernels, backward(): pl.pallas_call(backward_kernel, out_shape=shapes, in_specs=[ANY if n in a...  164 us
    pallas_call x1, Pallas kernels, closing(): pl.pallas_call(closing_kernel, out_shape=shapes, in_specs=[VMEM] * len(ar...  124 us
    pallas_call x1, Pallas kernels, feed_forward(): pl.pallas_call(feed_forward_kernel, out_shape=shapes, in_specs=[VMEM, VME...  64.2 us
  transfers between devices with their start and end apart: 1, of which 0 were waited for; matrix products, arithmetic and copies ran while one was open for 2% of the time, Pallas kernels for 49%

profile of v4, /device:TPU:0, one launch (start us, length us, event | category | flops | bytes accessed | tf_op | source)
XLA Modules:
  0.0 627.3 jit_solution(18444777864604983378)
XLA Ops:
  0.7 0.8 fusion
  2.0 0.8 dynamic_slice.13
  2.7 1.9 constant_dynamic-slice_fusion.refs_7_.refs_2_
  4.6 1.9 constant_dynamic-slice_fusion.1.refs_6_.refs_4_
  6.7 1.1 copy.37
  7.8 0.8 copy.36
  8.9 0.6 pad.17.refs_4_
  9.6 0.7 maximum_maximum_fusion.refs_5_
  10.2 0.7 broadcast_in_dim.19.refs_9_.refs_21_
  10.9 0.6 broadcast_in_dim.18.refs_8_.refs_20_
  11.5 244.0 %forward.1 = (bf16[2,2,2,2,128,2048]{5,4,3,2,1,0:T(8,128)(2,1)}, bf16[2,2,2,2,128,512]{5,4,3,2,1,0:T(8,128)(2,1)}, bf16[2,2,2,2,128,2816]{5,4,3,2,1,0:T(8,128)(2...) custom-call(bf16[4,128,1024]{2,1,0:T(8,128)(2,1)} %refs_0_.1, ...), custom_call_target="tpu_custom_call" | custom-call | tf_op jit(solution)/shard_map/forward/pallas_call | solution.py:933
  255.5 1.5 fusion.1
  257.0 0.9 slice.50
  258.0 0.8 pad.20.refs_7_
  258.8 64.2 %feed_forward.1 = (bf16[4,128,2048]{2,1,0:T(8,128)(2,1)}, bf16[4,128,2048]{2,1,0:T(8,128)(2,1)}, bf16[512,2816]{1,0:T(8,128)(2,1)}, bf16[512,2816]{1,0:T(8,128)(2,1)}, bf16[512,1408]{1,0:T(8,128)(2,1)}) custom-call(bf16[4,128,2048]{2,1,0:T(8,128)(2,1)} %get-tuple-element.54.hidden, bf16[4,128,2048]{2,1,0:T(8,128)(2,1)} %get-tuple-element.55.cots, ...), custom_call_target="tpu_custom_call" | custom-call | tf_op jit(solution)/shard_map/feed_forward/pallas_call | solution.py:1130
  323.1 0.7 pad.19.refs_17_
  323.7 164.1 %backward.1 = (f32[128,2048]{1,0:T(8,128)}, f32[1,2048]{1,0:T(1,128)}, bf16[4,128,2048]{2,1,0:T(8,128)(2,1)}, bf16[4,128,128]{2,1,0:T(8,128)(2,1)}, f32[24,512]{...) custom-call(bf16[4,128,2048]{2,1,0:T(8,128)(2,1)} %get-tuple-element, ...), custom_call_target="tpu_custom_call" | custom-call | tf_op jit(solution)/shard_map/backward/pallas_call | solution.py:1496
  487.8 123.6 %closing.1 = (bf16[2,128,2048]{2,1,0:T(8,128)(2,1)}, f32[4,128,1024]{2,1,0:T(8,128)}, f32[1024,128]{1,0:T(8,128)}, f32[2,128,2816]{2,1,0:T(8,128)}, f32[2816,128...) custom-call(bf16[4,128,2048]{2,1,0:T(8,128)(2,1)} %get-tuple-element.76.refs_0_, ...), custom_call_target="tpu_custom_call" | custom-call | tf_op jit(solution)/shard_map/closing/pallas_call | solution.py:1843
  611.4 0.9 slice_bitcast_fusion
  612.4 1.4 slice.40
  613.7 1.3 slice_bitcast_fusion.1
  615.0 1.3 slice_bitcast_fusion.2
  616.3 0.6 copy.40
  616.9 1.4 slice_reduce_fusion
  618.4 1.0 copy.47
  619.3 1.0 copy.48
  620.4 1.3 copy.49
  621.7 0.8 copy.50
  622.5 0.8 copy-done
  623.3 1.6 copy.51
  624.9 0.8 copy-done.2
  625.7 1.1 copy.52
  (35 shorter events, 1.1 us)
Async XLA Ops:
  0.6 5.8 copy-start.12
  0.7 6.0 copy-start.5
  0.7 7.2 %copy-start.7 = (bf16[1024,128]{1,0:T(8,128)(2,1)S(1)}, bf16[1024,128]{1,0:T(8,128)(2,1)}, u32[]{:S(2)}) copy-start(bf16[1024,128]{1,0:T(8,128)(2,1)} %param.23) | copy-start | bytes 786436
  0.7 8.0 %copy-start.11 = (bf16[128]{0:T(256)(128)(2,1)S(1)}, bf16[128]{0:T(256)(128)(2,1)}, u32[]{:S(2)}) copy-start(bf16[128]{0:T(256)(128)(2,1)} %param.16) | copy-start | bytes 772
  0.7 8.0 %copy-start.10 = (bf16[128]{0:T(256)(128)(2,1)S(1)}, bf16[128]{0:T(256)(128)(2,1)}, u32[]{:S(2)}) copy-start(bf16[128]{0:T(256)(128)(2,1)} %param.17) | copy-start | bytes 772
  0.7 8.0 %copy-start.9 = (bf16[128,16]{0,1:T(8,128)(2,1)S(1)}, bf16[128,16]{0,1:T(8,128)(2,1)}, u32[]{:S(2)}) copy-start(bf16[128,16]{0,1:T(8,128)(2,1)} %param.19) | copy-start | bytes 12292
  1.5 321.5 %collective-permute-start = (bf16[16,512]{1,0:T(8,128)(2,1)S(1)}, bf16[16,512]{1,0:T(8,128)(2,1)S(1)}, u32[]{:S(2)}, u32[]{:S(2)}) collective-permute-start(bf16[16,512]{1,0:T(8,128)(2,1)S(1)} %get-tuple-element.96), channel_id=1, source_target_pairs={{0,1},{1,0},{2,3},{3,2},{4,5},{5,4},{6,7},{7,6},{8,9},{9,8},{10,11... | collective-permute-start | bytes 49160 | tf_op jit(solution)/shard_map/ppermute | solution.py:1893
  258.8 64.2 %copy-start.8 = (bf16[16,1024]{1,0:T(8,128)(2,1)S(1)}, bf16[16,1024]{1,0:T(8,128)(2,1)}, u32[]{:S(2)}) copy-start(bf16[16,1024]{1,0:T(8,128)(2,1)} %param.20) | copy-start | bytes 98308
  487.8 130.6 %copy-start.3 = (bf16[2,128,2048]{2,1,0:T(8,128)(2,1)S(1)}, bf16[2,128,2048]{2,1,0:T(8,128)(2,1)}, u32[]{:S(2)}) copy-start(bf16[2,128,2048]{2,1,0:T(8,128)(2,1)} %get-tuple-element.75) | copy-start | bytes 3145732
  611.4 7.9 %copy-start.4 = (bf16[2,128,2048]{2,1,0:T(8,128)(2,1)S(1)}, bf16[2,128,2048]{2,1,0:T(8,128)(2,1)}, u32[]{:S(2)}) copy-start(bf16[2,128,2048]{2,1,0:T(8,128)(2,1)} %get-tuple-element.88) | copy-start | bytes 3145732
  618.4 2.0 copy-start.1
  620.4 1.4 copy-start.6
  620.4 2.9 copy-start
  623.3 2.4 copy-start.2

commit v5 on v4

--- a/solution.py
+++ b/solution.py
@@ -428,6 +428,7 @@
 
 
 LANES = 128
+RANKS = 32
 
 
 def keyed_mask(start, starts_row, starts_column):
@@ -577,7 +578,7 @@
         mixer_in, mixer_out, ffn_in, ffn_out, small, ups, own, cot, starts_row, starts_column, head_gain,
         mixer_w, merge_w, pair_w, down_w, gains, cots, hidden, low_rank, gate, cumulated, projected, mixed, gated,
         befores, decay, second, middle,
-        mixer_v, merge_v, projected_v, updates, inputs, smalls, ups_got, columns, state, partial, got, relayed, staged, line,
+        mixer_v, merge_v, projected_v, updates, inputs, smalls, ups_got, state, partial, got, relayed, staged, line,
         own_send, own_arrive, far_send, arrive, small_send, small_arrive, ups_sem, inputs_send, inputs_arrive,
         cot_send, cot_arrive, sum_send, sum_arrive, spread_send, spread_arrive, saves,
     ) = refs[:-STATE_REFS]
@@ -620,21 +621,24 @@
     count = [0]
     sent = []
 
-    def forward(at_zh, at_y, part, to):
+    def forward(at_zh, at_y, part, to, start=True):
         place = piece(at_zh, at_y, me.c, part)
         copy = copy_to(place, place, far_send.at[count[0]], arrive.at[at_zh, at_y, me.c, part], to)
-        copy.start()
+        if start:
+            copy.start()
         count[0] += 1
         sent.append(copy)
+        return copy
 
     def arrived(at_zh, at_y, x, part):
         wait_for(piece(at_zh, at_y, x, part), arrive.at[at_zh, at_y, x, part])
 
-    def send_own(part):
+    def own_high(part, start=True):
         firsts[part].wait_arrive()
         firsts[part].wait_local()
-        for k in range(1, highs):
-            forward(zh, y, part, {"zh": lax.rem(zh + k, highs)})
+        return [forward(zh, y, part, {"zh": lax.rem(zh + k, highs)}, start) for k in range(1, highs)]
+
+    def own_near(part):
         forward(zh, y, part, side)
         forward(zh, y, part, twin)
 
@@ -674,26 +678,29 @@
     lend = copy_to(ups, ups_got, ups_sem.at[0], ups_sem.at[1], twin)
     lend.start()
     for part in order:
-        send_own(part)
+        own_high(part)
+        if part in order[:2]:
+            own_near(part)
     move_inputs = HalvesSpread(me, own, lambda k: inputs.at[k], inputs_send, inputs_arrive)
     move_cot = MemberSpread(me, cot, lambda k: cots.at[k], cot_send, cot_arrive)
     move_inputs.start()
-    for part in (5, 6, 7):
-        firsts[part].start()
     move_inputs.relay()
     pass_high(1)
     move_small.wait()
     lend.wait()
-    owner_rows = smalls.shape[1]
+    owner_rows = smalls.shape[2]
     for n in range(smalls.shape[0]):
-        columns[pl.ds(n * owner_rows, owner_rows)] = smalls[n].astype(F32)
-    gains[...] = columns[...].T
+        gains[:, n * owner_rows : (n + 1) * owner_rows] = smalls[n].astype(F32)
     pass_high(2)
+    for part in (5, 6, 7):
+        firsts[part].start()
+    for part in order[2:]:
+        own_near(part)
     move_inputs.wait()
 
     up = jnp.where(me.c == me.zl, ups[...], ups_got[...])
     rank_up, bias = low(up[:16]), up[16:17]
-    down = low(columns[...])
+    down = low(gains[...])
     lower = (
         lax.broadcasted_iota(jnp.int32, (CHUNK, CHUNK), 0)
         >= lax.broadcasted_iota(jnp.int32, (CHUNK, CHUNK), 1)
@@ -704,7 +711,7 @@
         scale = lax.rsqrt(jnp.mean(x * x, -1, keepdims=True) + EPSILON)
         h = low(x * scale * gains[0:1])
         hidden[n] = h
-        z = low(dot(h, down))
+        z = low(dot_last(h, down))
         low_rank[n] = z
         a = dot(z[:, 2:18], rank_up) + bias
         gate[n] = a
@@ -727,14 +734,10 @@
 
     pass_side(1)
     pass_side(2)
-    pass_high(0)
-    for part in (5, 6, 7):
-        send_own(part)
     complete(1)
     project(1)
     complete(2)
     project(2)
-    pass_high(3)
 
     state[...] = jnp.zeros_like(state)
     decay[...] = jnp.ones_like(decay)
@@ -757,13 +760,20 @@
     lax.fori_loop(0, chunks, local_step, 0)
     states = StatePass(False, state, decay, state, *refs[-STATE_REFS:])
     states.begin()
+    pass_high(0)
+    states.combine()
+    held = [copy for part in (5, 6, 7) for copy in own_high(part, False)]
+
+    @pl.when(me.zl == 1)
+    def _():
+        for copy in held:
+            copy.start()
+
+    pass_high(3)
     pass_side(0)
-    pass_high(4)
     complete(0)
     project(0)
-    states.combine()
     pass_side(3)
-    pass_side(4)
 
     def inner_step(n, _):
         pair, _, _, _ = masks(n)
@@ -777,6 +787,15 @@
 
     lax.fori_loop(0, chunks, inner_step, 0)
     states.spread()
+
+    @pl.when(me.zl == 0)
+    def _():
+        for copy in held:
+            copy.start()
+
+    pass_high(4)
+    for part in (5, 6, 7):
+        own_near(part)
     complete(3)
     project(3)
     states.finish()
@@ -796,6 +815,7 @@
         return 0
 
     lax.fori_loop(0, chunks, outer_step, 0)
+    pass_side(4)
     complete(4)
 
     def merge_step(n, _):
@@ -834,9 +854,9 @@
     ]
     for transfer in sums:
         transfer.start()
-    pass_high(5)
     for transfer in sums:
         transfer.relay()
+    pass_high(5)
     for n in range(steps):
         at = pl.ds(n * rows, rows)
         total = own[at].astype(F32) + sums[n].total()
@@ -847,13 +867,13 @@
         if n:
             spreads[n - 1].relay()
     spreads[steps - 1].relay()
+    pass_high(6)
+    pass_side(5)
     move_cot.start()
     save(mixer_v, mixer_w)
     save(merge_v, merge_w)
-    pass_high(6)
-    pass_side(5)
+    pass_high(7)
     move_cot.relay()
-    pass_high(7)
     for part in (6, 7):
         pass_side(part)
     for part in (5, 6, 7):
@@ -880,7 +900,7 @@
 def forward(mixer_in, mixer_out, ffn_in, ffn_out, small, ups, own, cot, starts, head_gain):
     highs = lax.axis_size("zh")
     chips = highs * 8
-    rows, half, width = small.shape[0], own.shape[0], own.shape[1]
+    rows, half, width = small.shape[1], own.shape[0], own.shape[1]
     units = ffn_out.shape[1] // 2
     chunks = TEAM * half // CHUNK
 
@@ -892,10 +912,10 @@
         (shape(highs, 2, 2, 2, rows, HD), ANY),
         (shape(highs, 2, 2, 2, rows, 2 * units), ANY),
         (shape(highs, 2, 2, 2, rows, units), ANY),
-        (shape(LANES, width, kind=F32), VMEM),
+        (shape(RANKS, width, kind=F32), VMEM),
         (shape(TEAM, half, width), ANY),
         (shape(chunks, CHUNK, width), VMEM),
-        (shape(chunks, CHUNK, LANES), VMEM),
+        (shape(chunks, CHUNK, RANKS), VMEM),
         (shape(chunks, CHUNK, HD, kind=F32), VMEM),
         (shape(chunks, CHUNK, HD, kind=F32), VMEM),
         (shape(4, chunks, CHUNK, HD, kind=F32), ANY),
@@ -913,9 +933,8 @@
         shapes[10][0],
         shape(chunks, HD, HD, kind=F32),
         shape(TEAM, half, width),
-        shape(chips, rows, LANES),
+        shape(chips, RANKS, rows),
         shape(*ups.shape, kind=F32),
-        shape(width, LANES, kind=F32),
         shape(HD, HD, kind=F32),
         shape(TEAM, half, width),
         shape(3, half, width),
@@ -1156,9 +1175,9 @@
     (
         back, forth, cot, middle, gain, pair_away, pair_keep, downs, merge_w, gated, projected, mixed,
         cumulated, gate, befores, decay, low_rank, up_pad, head_gain, hidden, starts_row, starts_column,
-        grad_middle, gain_grad, proj, ranks, heads, early_away, early_keep, gate_sum, up_sum, down_sum, left_hidden,
+        grad_middle, gain_grad, proj, ranks, heads, early, gate_sum, up_sum, down_sum, left_hidden,
         result, got, relayed, staged, line, got2, relayed2, staged2, line2, branch, left_branch, douts, tiles, tiles_got,
-        pair_side, gate_got, up_got, down_got, up_grad, state,
+        pair_side, gate_got, up_got, down_got, early_away, early_keep, up_grad, state,
         send, arrive, send2, arrive2, side_send, side_arrive, high_send, high_arrive, tile_send, tile_arrive,
         send3, arrive3, twin_send, twin_arrive, here,
     ) = refs[:-STATE_REFS]
@@ -1336,7 +1355,6 @@
     lax.fori_loop(0, chunks, local_step, 0)
     states = StatePass(True, state, decay, state, *refs[-STATE_REFS:])
     states.begin()
-    high_start(2)
 
     turn_rows(me, branch, left_branch)
     half = width // 2
@@ -1358,6 +1376,7 @@
             tiles[tile] = low(dot(lefts[kind][pl.ds(0, half)], right_tile(kind, n)))
             tile_move(tile).start()
     states.combine()
+    high_start(2)
     for kind in range(2):
         for n in range(HD // TILE):
             tile = kind * (HD // TILE) + n
@@ -1367,6 +1386,8 @@
             at = slice(tile * TILE, (tile + 1) * TILE)
             early_away[:, at] = block[:quarter]
             early_keep[:, at] = block[quarter:]
+    early_move = copy_to(early_away, early, side_send.at[0], side_arrive.at[0], {"y": 1 - y})
+    early_move.start()
     states.spread()
     for transfer in forth_sums:
         transfer.relay()
@@ -1417,6 +1438,8 @@
         line2[at] = low(middle[at] + forth_sums[n].total())
         twin_copy(n).start()
         own_copy(n).start()
+    early_move.wait()
+    add_rows(early, early_keep, early)
     for p in range(3):
         high_add(p)
     for n in range(steps):
@@ -1457,7 +1480,6 @@
         shape(chunks, CHUNK, 4 * HD),
         shape(chunks, CHUNK, LANES),
         shape(24, HD, kind=F32),
-        shape(quarter, 2 * HD),
         shape(quarter, 2 * HD),
         shape(members, owner_rows, units),
         shape(members, owner_rows, units),
@@ -1484,7 +1506,9 @@
         shape(highs - 1, members, owner_rows, units),
         shape(highs - 1, members, owner_rows, units),
         shape(highs - 1, members, owner_rows, units),
-        shape(LANES, HD, kind=F32),
+        shape(quarter, 2 * HD),
+        shape(quarter, 2 * HD),
+        shape(RANKS, HD, kind=F32),
         shape(HD, HD, kind=F32),
     ]
     used = [a for n, a in enumerate(arrays) if n not in away] + shapes + scratch
@@ -1510,10 +1534,9 @@
 
 def closing_kernel(*refs):
     (
-        proj, ranks, mixer_w, left, own, grad_middle, gain, down, gain_two_grad, heads, early_away, early_keep,
-        ups, gates, downs,
+        proj, ranks, mixer_w, left, own, grad_middle, gain, down, gain_two_grad, heads, early, ups, gates, downs,
         out, mixer_grad, merge_grad, pair_grad, down_grad, wide_out, heads_out, gains_out,
-        partial, got, relayed, staged, line, tiles, tiles_got, late_away, late_keep, late_side, early_side,
+        partial, got, relayed, staged, line, tiles, tiles_got, late_away, late_keep, late_side,
         late_got, early_got, late_sum, early_sum, late_home, early_home, ups_home, gate_home, down_home,
         wide, wide_got, heads_got, heads_sum, wide_twin, gain_grad, rank_grad,
         send, arrive, twin_send, twin_arrive, here, tile_send, tile_arrive, side_send, side_arrive,
@@ -1552,10 +1575,9 @@
             home_arrive.at[kind],
         )
 
-    early_move = side_copy(3, early_away, early_side)
     late_moves = [side_copy(j, late_away.at[j], late_side.at[j]) for j in range(3)]
     high_moves = [high_copies(j, late_side.at[j], late_got.at[j]) for j in range(3)]
-    high_moves += [high_copies(3, early_side, early_got)]
+    high_moves += [high_copies(3, early, early_got)]
     homes = [home(j, late_sum.at[j], late_home.at[j]) for j in range(3)]
     homes += [home(3, early_sum, early_home), home(4, ups, ups_home)]
     homes += [home(5, gates, gate_home), home(6, downs, down_home)]
@@ -1571,11 +1593,12 @@
     )
     heads_move.start()
 
-    early_move.start()
+    for move in high_moves[3]:
+        move.start()
 
     half = width // 2
     quarter = half // 2
-    owner_rows = early_keep.shape[2]
+    owner_rows = early.shape[2]
 
     def tile_move(n):
         return copy_to(tiles.at[n], tiles_got.at[n], tile_send.at[n], tile_arrive.at[n], twin)
@@ -1642,9 +1665,6 @@
             for m in range(2):
                 add_rows(there.at[k, m], keep.at[k, m], there.at[k, m])
 
-    side_add(early_move, early_keep, early_side)
-    for move in high_moves[3]:
-        move.start()
     for transfer in sums:
         transfer.relay()
     for j in range(3):
@@ -1754,7 +1774,7 @@
     spread_columns(gate_home, pair_grad.at[0], units)
     homes[4].wait()
     spread_columns(ups_home, pair_grad.at[1], units)
-    high_add(3, early_side, early_got, early_sum)
+    high_add(3, early, early_got, early_sum)
     for k in range(2):
         own_slot = (me.c == me.zl) & (me.x == k)
         unless(own_slot, lambda k=k: wait_for(heads_out.at[k], out_arrive.at[k]))
@@ -1795,11 +1815,11 @@
 def closing(proj, ranks, mixer_w, left, own, grad_middle, gain, down, gain_two_grad, heads, early, ups, gates, downs):
     rows, width = own.shape
     chunks = proj.shape[0]
-    highs, _, owner_rows, _ = early[0].shape
+    highs, _, owner_rows, _ = early.shape
     units = ups.shape[-1]
     chips = highs * 8
     arrays = [
-        proj, ranks, mixer_w, left, own, grad_middle, gain, down, gain_two_grad, heads, *early, ups, gates, downs,
+        proj, ranks, mixer_w, left, own, grad_middle, gain, down, gain_two_grad, heads, early, ups, gates, downs,
     ]
 
     def shape(*dims, kind=BF):
@@ -1819,7 +1839,7 @@
     late = (3, highs, 2, owner_rows, HD)
     scratch = [shape(chunks, CHUNK, width + LANES)]
     scratch += [shape(n, rows, width + LANES) for n in (3, 2, 2)] + [shape(rows, width)]
-    scratch += [shape(tiles, width // 2, TILE)] * 2 + [shape(*late)] * 3 + [shape(*early[0].shape)]
+    scratch += [shape(tiles, width // 2, TILE)] * 2 + [shape(*late)] * 3
     scratch += [
         shape(3, highs - 1, 2, owner_rows, HD),
         shape(highs - 1, 2, owner_rows, 2 * HD),
@@ -1837,7 +1857,7 @@
     ]
     size = sum(a.size * a.dtype.itemsize for a in arrays + shapes + scratch)
     sems = [
-        (STEPS, 6), (STEPS, 5), (STEPS,), (STEPS,), (STEPS,), (tiles,), (tiles,), (4,), (4,), (4, highs), (4, highs),
+        (STEPS, 6), (STEPS, 5), (STEPS,), (STEPS,), (STEPS,), (tiles,), (tiles,), (3,), (3,), (4, highs), (4, highs),
         (7, 2), (7, 2), (chips,), (chips,), (highs * 4,), (highs * 4,), (2,), (3,), (2,), (TEAM,), (TEAM,),
     ]
     return pl.pallas_call(
@@ -1876,8 +1896,8 @@
     team_tokens = 2 * block
     rank = decay_down.shape[1]
 
-    small = jnp.concatenate([attn_gain[:, None], ffn_gain[:, None], decay_down], axis=1)
-    small = jnp.pad(small, ((0, 0), (0, LANES - small.shape[1])))
+    small = jnp.concatenate([attn_gain[None], ffn_gain[None], decay_down.T], axis=0)
+    small = jnp.pad(small, ((0, RANKS - small.shape[0]), (0, 0)))
     up_head = lax.dynamic_slice_in_dim(decay_up, HD * x, HD, 1).astype(F32)
     bias_head = lax.dynamic_slice_in_dim(decay_bias, HD * x, HD, 0)
     ups = jnp.concatenate([up_head, bias_head[None], jnp.zeros((7, HD), F32)], axis=0)
@@ -1900,17 +1920,16 @@
     down_part = down_part.reshape(highs, 2, rows, units)
     pad_rank = ((0, LANES - rank), (0, 0))
     (
-        grad_middle, grad_gain_two, grad_proj, grad_ranks, heads, early_away, early_keep, gate_sum, up_sum, down_sum,
+        grad_middle, grad_gain_two, grad_proj, grad_ranks, heads, early, gate_sum, up_sum, down_sum,
         left_hidden, result,
     ) = backward(
         back, forth, own_dy, middle, gain_two, pair_sides, down_part, merge_w, gated, projected, mixed, cumulated,
         gate_input, befores, decay, low_rank, jnp.pad(up_head, pad_rank), head_gain[None], hidden_one, starts,
     )
-    early_shape = (highs, 2, rows, 2 * HD)
-    early_sums = early_away.reshape(early_shape), early_keep.reshape(early_shape)
+    early = early.reshape(highs, 2, rows, 2 * HD)
     grad_inputs, mixer_home, merge_home, pair_home, down_home, wide, heads, gains = closing(
         grad_proj, grad_ranks, mixer_w, left_hidden, own, grad_middle, gain_one, jnp.pad(rank_down, pad_rank),
-        grad_gain_two, heads, early_sums, up_sum, gate_sum, down_sum,
+        grad_gain_two, heads, early, up_sum, gate_sum, down_sum,
     )
     return (
         result.reshape(block, width),

time: 634 us -> 613 us (0.967)
  Pallas kernels: 596 us -> 575 us
    pallas_call x1, Pallas kernels: 164 us -> 139 us  [backward(): pl.pallas_call(backward_kernel, out_shape=shapes, in_specs=[ANY if n in a...]
  transfers between devices with their start and end apart: 1 -> 1, of which waited for: 0 -> 0; matrix products, arithmetic and copies ran while one was open for 2% -> 2% of each run, Pallas kernels for 49% -> 51%
where the time goes in v5:
time: 613 us; the launch traced here: 606 us
  Pallas kernels  575 us (94%)
  local copies, waits for them, and re-layouts  25.8 us (4%)
    pallas_call x1, Pallas kernels, forward(): pl.pallas_call(forward_kernel, out_shape=[a for a, _ in shapes], in_specs...  246 us
    pallas_call x1, Pallas kernels, backward(): pl.pallas_call(backward_kernel, out_shape=shapes, in_specs=[ANY if n in a...  139 us
    pallas_call x1, Pallas kernels, closing(): pl.pallas_call(closing_kernel, out_shape=shapes, in_specs=[VMEM] * len(ar...  126 us
    pallas_call x1, Pallas kernels, feed_forward(): pl.pallas_call(feed_forward_kernel, out_shape=shapes, in_specs=[VMEM, VME...  64.2 us
  transfers between devices with their start and end apart: 1, of which 0 were waited for; matrix products, arithmetic and copies ran while one was open for 2% of the time, Pallas kernels for 51%

profile of v5, /device:TPU:0, one launch (start us, length us, event | category | flops | bytes accessed | tf_op | source)
XLA Modules:
  0.0 606.4 jit_solution(7708867667725754336)
XLA Ops:
  0.7 0.8 fusion.5
  2.0 0.8 dynamic_slice.13
  2.8 1.9 constant_dynamic-slice_fusion.refs_7_.refs_2_
  4.7 1.9 constant_dynamic-slice_fusion.1.refs_6_.refs_4_
  6.8 1.1 copy.28
  7.9 0.8 copy.27
  8.8 0.7 maximum_maximum_fusion.refs_5_
  9.5 0.6 fusion.4.refs_4_
  10.1 0.7 broadcast_in_dim.19.refs_9_.refs_21_
  10.8 0.6 broadcast_in_dim.18.refs_8_.refs_20_
  11.4 245.8 %forward.1 = (bf16[2,2,2,2,128,2048]{5,4,3,2,1,0:T(8,128)(2,1)}, bf16[2,2,2,2,128,512]{5,4,3,2,1,0:T(8,128)(2,1)}, bf16[2,2,2,2,128,2816]{5,4,3,2,1,0:T(8,128)(2...) custom-call(bf16[4,128,1024]{2,1,0:T(8,128)(2,1)} %refs_0_.1, ...), custom_call_target="tpu_custom_call" | custom-call | tf_op jit(solution)/shard_map/forward/pallas_call | solution.py:952
  257.2 1.5 fusion.6
  258.7 0.9 slice.50
  259.7 0.8 pad.20.refs_7_
  260.5 64.2 %feed_forward.1 = (bf16[4,128,2048]{2,1,0:T(8,128)(2,1)}, bf16[4,128,2048]{2,1,0:T(8,128)(2,1)}, bf16[512,2816]{1,0:T(8,128)(2,1)}, bf16[512,2816]{1,0:T(8,128)(2,1)}, bf16[512,1408]{1,0:T(8,128)(2,1)}) custom-call(bf16[4,128,2048]{2,1,0:T(8,128)(2,1)} %get-tuple-element.53.hidden, bf16[4,128,2048]{2,1,0:T(8,128)(2,1)} %get-tuple-element.54.cots, ...), custom_call_target="tpu_custom_call" | custom-call | tf_op jit(solution)/shard_map/feed_forward/pallas_call | solution.py:1149
  324.7 0.7 pad.19.refs_17_
  325.4 139.2 %backward.1 = (f32[128,2048]{1,0:T(8,128)}, f32[1,2048]{1,0:T(1,128)}, bf16[4,128,2048]{2,1,0:T(8,128)(2,1)}, bf16[4,128,128]{2,1,0:T(8,128)(2,1)}, f32[24,512]{...) custom-call(bf16[4,128,2048]{2,1,0:T(8,128)(2,1)} %get-tuple-element, ...), custom_call_target="tpu_custom_call" | custom-call | tf_op jit(solution)/shard_map/backward/pallas_call | solution.py:1520
  464.6 125.9 %closing.1 = (bf16[2,128,2048]{2,1,0:T(8,128)(2,1)}, f32[4,128,1024]{2,1,0:T(8,128)}, f32[1024,128]{1,0:T(8,128)}, f32[2,128,2816]{2,1,0:T(8,128)}, f32[2816,128...) custom-call(bf16[4,128,2048]{2,1,0:T(8,128)(2,1)} %get-tuple-element.75.refs_0_, ...), custom_call_target="tpu_custom_call" | custom-call | tf_op jit(solution)/shard_map/closing/pallas_call | solution.py:1863
  590.6 0.9 slice_bitcast_fusion
  591.5 1.4 slice.40
  592.8 1.3 slice_bitcast_fusion.1
  594.1 1.3 slice_bitcast_fusion.2
  595.4 0.6 copy.30
  596.0 1.4 slice_reduce_fusion
  597.5 1.0 copy.37
  598.5 1.0 copy.38
  599.5 1.3 copy.39
  600.9 0.8 copy.40
  601.7 0.8 copy-done
  602.4 1.6 copy.41
  604.0 0.8 copy-done.2
  604.8 1.1 copy.42
  (33 shorter events, 1.0 us)
Async XLA Ops:
  0.6 5.9 copy-start.12
  0.7 6.1 %copy-start.5 = (bf16[2816,128]{1,0:T(8,128)(2,1)S(1)}, bf16[2816,128]{1,0:T(8,128)(2,1)}, u32[]{:S(2)}) copy-start(bf16[2816,128]{1,0:T(8,128)(2,1)} %param.25) | copy-start | bytes 2162692
  0.7 7.2 %copy-start.7 = (bf16[1024,128]{1,0:T(8,128)(2,1)S(1)}, bf16[1024,128]{1,0:T(8,128)(2,1)}, u32[]{:S(2)}) copy-start(bf16[1024,128]{1,0:T(8,128)(2,1)} %param.23) | copy-start | bytes 786436
  1.5 8.0 %copy-start.9 = (bf16[128,16]{0,1:T(8,128)(2,1)S(1)}, bf16[128,16]{0,1:T(8,128)(2,1)}, u32[]{:S(2)}) copy-start(bf16[128,16]{0,1:T(8,128)(2,1)} %param.19) | copy-start | bytes 12292
  1.5 8.0 %copy-start.10 = (bf16[128]{0:T(256)(128)(2,1)S(1)}, bf16[128]{0:T(256)(128)(2,1)}, u32[]{:S(2)}) copy-start(bf16[128]{0:T(256)(128)(2,1)} %param.17) | copy-start | bytes 772
  1.5 8.0 %copy-start.11 = (bf16[128]{0:T(256)(128)(2,1)S(1)}, bf16[128]{0:T(256)(128)(2,1)}, u32[]{:S(2)}) copy-start(bf16[128]{0:T(256)(128)(2,1)} %param.16) | copy-start | bytes 772
  1.5 323.2 %collective-permute-start = (bf16[16,512]{1,0:T(8,128)(2,1)S(1)}, bf16[16,512]{1,0:T(8,128)(2,1)S(1)}, u32[]{:S(2)}, u32[]{:S(2)}) collective-permute-start(bf16[16,512]{1,0:T(8,128)(2,1)S(1)} %get-tuple-element.94), channel_id=1, source_target_pairs={{0,1},{1,0},{2,3},{3,2},{4,5},{5,4},{6,7},{7,6},{8,9},{9,8},{10,11... | collective-permute-start | bytes 49160 | tf_op jit(solution)/shard_map/ppermute | solution.py:1913
  260.5 64.2 %copy-start.8 = (bf16[16,1024]{1,0:T(8,128)(2,1)S(1)}, bf16[16,1024]{1,0:T(8,128)(2,1)}, u32[]{:S(2)}) copy-start(bf16[16,1024]{1,0:T(8,128)(2,1)} %param.20) | copy-start | bytes 98308
  464.6 132.9 %copy-start.3 = (bf16[2,128,2048]{2,1,0:T(8,128)(2,1)S(1)}, bf16[2,128,2048]{2,1,0:T(8,128)(2,1)}, u32[]{:S(2)}) copy-start(bf16[2,128,2048]{2,1,0:T(8,128)(2,1)} %get-tuple-element.74) | copy-start | bytes 3145732
  590.5 7.9 %copy-start.4 = (bf16[2,128,2048]{2,1,0:T(8,128)(2,1)S(1)}, bf16[2,128,2048]{2,1,0:T(8,128)(2,1)}, u32[]{:S(2)}) copy-start(bf16[2,128,2048]{2,1,0:T(8,128)(2,1)} %get-tuple-element.86) | copy-start | bytes 3145732
  597.5 2.0 copy-start.1
  599.5 1.4 copy-start.6
  599.5 2.9 copy-start
  602.4 2.4 copy-start.2

commit v6 on v5

--- a/solution.py
+++ b/solution.py
@@ -992,8 +992,8 @@
 def feed_forward_kernel(
     hidden, cots, pair_w, down_w,
     forth, back, pair_away, pair_keep, down_part,
-    pair_v, down_v, act, grad_gate, grad_up, left_hidden, left_cots, tiles, tiles_got, down_away, down_keep,
-    loads, tile_send, tile_arrive, side,
+    forth_v, back_v, away_v, keep_v, pair_v, down_v, act, grad_gate, grad_up, left_hidden, left_cots, tiles, tiles_got, down_away, down_keep,
+    loads, tile_send, tile_arrive, side_send, side_arrive, saves,
 ):
     me = Place()
     y = lax.axis_index("y")
@@ -1031,20 +1031,8 @@
         grad_gate[:, at] = low(da * b * sig * (1.0 + a * (1.0 - sig)))
         grad_up[:, at] = low(da * silu)
 
-    for n, (start, size) in enumerate(spans):
-        for kind in range(3):
-            load(kind, n).wait()
-        if size < TILE:
-            units_step(start, size)
     whole = units // TILE
-
-    def whole_step(n, _):
-        units_step(pl.multiple_of(n * TILE, TILE), TILE)
-        return 0
-
-    lax.fori_loop(0, whole, whole_step, 0)
     pl.semaphore_wait(barrier, 2)
-
     half = width // 2
     quarter = half // 2
     count = len(spans)
@@ -1091,9 +1079,39 @@
         if whole < count:
             add_tile(left, right, first + whole, *spans[whole], away, keep, base)
 
-    weight_grad(0, left_cots, act, down_away, down_keep, 0)
-    side_move = copy_to(down_away, down_part, side.at[0], side.at[1], {"y": 1 - y})
-    side_move.start()
+    def side_move(n, start, size):
+        at = pl.ds(start, size)
+        return copy_to(down_away.at[:, at], down_part.at[:, at], side_send.at[n], side_arrive.at[n], {"y": 1 - y})
+
+    def down_tile(n, start, size):
+        add_tile(left_cots, act, n, start, size, down_away, down_keep, 0)
+        side_move(n, start, size).start()
+
+    def tile_step(n, _):
+        for kind in range(3):
+            start = n * TILE if kind == 2 else kind * units + n * TILE
+            at = pl.ds(pl.multiple_of(start, LANES), TILE)
+            source, target = (down_w, down_v) if kind == 2 else (pair_w, pair_v)
+            pltpu.make_async_copy(source.at[:, at], target.at[:, at], loads.at[kind, n]).wait()
+        start = pl.multiple_of(n * TILE, TILE)
+        units_step(start, TILE)
+        send_tile(left_cots, act, n, start, TILE)
+
+        @pl.when(n > 0)
+        def _():
+            down_tile(n - 1, pl.multiple_of((n - 1) * TILE, TILE), TILE)
+
+        return 0
+
+    lax.fori_loop(0, whole, tile_step, 0)
+    if whole < count:
+        for kind in range(3):
+            load(kind, whole).wait()
+        units_step(*spans[whole])
+        send_tile(left_cots, act, whole, *spans[whole])
+    down_tile(whole - 1, *spans[whole - 1])
+    if whole < count:
+        down_tile(whole, *spans[whole])
 
     def back_step(n, _):
         at = pl.ds(pl.multiple_of(n * TILE, TILE), TILE)
@@ -1101,18 +1119,31 @@
         block = low(block + dot_last(grad_up[...], pair_v[at, pl.ds(units, units)]))
         ahead = low(dot_last(act[...], down_v[at]))
         for k in range(chunks):
-            back[k, :, at] = block[k * CHUNK : (k + 1) * CHUNK]
-            forth[k, :, at] = ahead[k * CHUNK : (k + 1) * CHUNK]
+            back_v[k, :, at] = block[k * CHUNK : (k + 1) * CHUNK]
+            forth_v[k, :, at] = ahead[k * CHUNK : (k + 1) * CHUNK]
         return 0
 
     lax.fori_loop(0, width // TILE, back_step, 0)
+    saved = [
+        pltpu.make_async_copy(source, target, saves.at[n])
+        for n, (source, target) in enumerate(
+            ((back_v, back), (forth_v, forth), (away_v, pair_away), (keep_v, pair_keep))
+        )
+    ]
+    for copy in saved[:2]:
+        copy.start()
     turn_rows(me, hidden, left_hidden)
-    weight_grad(1, left_hidden, grad_gate, pair_away, pair_keep, 0)
-    weight_grad(2, left_hidden, grad_up, pair_away, pair_keep, units)
+    weight_grad(1, left_hidden, grad_gate, away_v, keep_v, 0)
+    weight_grad(2, left_hidden, grad_up, away_v, keep_v, units)
+    for copy in saved[2:]:
+        copy.start()
     for n in range(2 * count, 3 * count):
         move(n).wait_send()
-    side_move.wait()
+    for n, span in enumerate(spans):
+        side_move(n, *span).wait()
     add_rows(down_part, down_keep, down_part)
+    for copy in saved:
+        copy.wait()
 
 
 def feed_forward(hidden, cots, pair_w, down_w):
@@ -1131,7 +1162,7 @@
         shape(half // 2, 2 * units),
         shape(half // 2, units),
     ]
-    scratch = [
+    scratch = shapes[:4] + [
         shape(width, 2 * units),
         shape(width, units),
         shape(tokens, units),
@@ -1144,13 +1175,13 @@
         shape(half // 2, units),
         shape(half // 2, units),
     ]
-    size = sum(a.size * a.dtype.itemsize for a in [hidden, cots] + shapes + scratch)
-    sems = [(3, count), (3 * count,), (3 * count,), (2,)]
+    size = sum(a.size * a.dtype.itemsize for a in [hidden, cots] + shapes[4:] + scratch)
+    sems = [(3, count), (3 * count,), (3 * count,), (count,), (count,), (4,)]
     return pl.pallas_call(
         feed_forward_kernel,
         out_shape=shapes,
         in_specs=[VMEM, VMEM, ANY, ANY],
-        out_specs=[VMEM] * len(shapes),
+        out_specs=[ANY] * 4 + [VMEM],
         scratch_shapes=[pltpu.VMEM(a.shape, a.dtype) for a in scratch] + [DMA(n) for n in sems],
         compiler_params=pltpu.CompilerParams(
             collective_id=5, has_side_effects=True, vmem_limit_bytes=min(size + (10 << 20), 63 << 20)
@@ -1173,13 +1204,13 @@
 
 def backward_kernel(*refs):
     (
-        back, forth, cot, middle, gain, pair_away, pair_keep, downs, merge_w, gated, projected, mixed,
-        cumulated, gate, befores, decay, low_rank, up_pad, head_gain, hidden, starts_row, starts_column,
+        back, forth, cot, middle, gain, pair_away, pair_keep_far, downs, merge_far, gated, projected_far, mixed_far,
+        cumulated_far, gate_far, befores_far, decay, low_rank, up_pad, head_gain, hidden, starts_row, starts_column,
         grad_middle, gain_grad, proj, ranks, heads, early, gate_sum, up_sum, down_sum, left_hidden,
         result, got, relayed, staged, line, got2, relayed2, staged2, line2, branch, left_branch, douts, tiles, tiles_got,
-        pair_side, gate_got, up_got, down_got, early_away, early_keep, up_grad, state,
+        pair_keep, merge_w, projected, mixed, cumulated, gate, befores, pair_side, gate_got, up_got, down_got, early_away, early_keep, up_grad, state,
         send, arrive, send2, arrive2, side_send, side_arrive, high_send, high_arrive, tile_send, tile_arrive,
-        send3, arrive3, twin_send, twin_arrive, here,
+        send3, arrive3, twin_send, twin_arrive, here, loads,
     ) = refs[:-STATE_REFS]
     me = Place()
     zh, y, highs = lax.axis_index("zh"), lax.axis_index("y"), lax.axis_size("zh")
@@ -1187,6 +1218,17 @@
     units = downs.shape[-1]
     first = ((zh * 2 + me.c) * 2 + y) * (chunks * CHUNK)
     greet_all(me)
+    loaded = [
+        pltpu.make_async_copy(source, target, loads.at[n])
+        for n, (source, target) in enumerate(
+            (
+                (pair_keep_far, pair_keep), (merge_far, merge_w), (mixed_far, mixed), (projected_far, projected),
+                (cumulated_far, cumulated), (befores_far, befores), (gate_far, gate),
+            )
+        )
+    ]
+    for copy in loaded:
+        copy.start()
 
     def columns(ref, part):
         return ref.at[:, :, :, pl.ds((part - 1) * units, units)]
@@ -1312,6 +1354,7 @@
         if n:
             spreads[n - 1].relay()
         if n == 2:
+            loaded[0].wait()
             high_start(1)
     spreads[steps - 1].relay()
     for transfer in spreads:
@@ -1319,6 +1362,8 @@
     for transfer in forth_sums:
         transfer.start()
 
+    for copy in loaded[1:]:
+        copy.wait()
     heads[...] = jnp.zeros_like(heads)
 
     def head_step(n, _):
@@ -1472,7 +1517,7 @@
         back, forth, cot, middle, gain, *pair, downs, merge_w, gated, projected, mixed, cumulated, gate, befores, decay,
         low_rank, up_pad, head_gain, hidden, *starts_arrays(starts),
     ]
-    away = {5}
+    away = {5, 6, 8, 10, 11, 12, 13, 14}
     quarter = width // 4
     shapes = [
         shape(rows, width, kind=F32),
@@ -1502,6 +1547,7 @@
         shape(chunks, CHUNK, HD),
         shape(tiles, width // 2, TILE),
         shape(tiles, width // 2, TILE),
+        *(shape(*arrays[n].shape, kind=arrays[n].dtype) for n in (6, 8, 10, 11, 12, 13, 14)),
         shape(highs, members, owner_rows, 2 * units),
         shape(highs - 1, members, owner_rows, units),
         shape(highs - 1, members, owner_rows, units),
@@ -1515,7 +1561,7 @@
     size = sum(a.size * a.dtype.itemsize for a in used)
     sems = [
         (STEPS, 3), (STEPS, 3), (STEPS, 5), (STEPS, 4), (3,), (3,), (3, highs), (3, highs), (tiles,), (tiles,),
-        (STEPS, 3), (STEPS, 3), (STEPS,), (STEPS,), (STEPS,),
+        (STEPS, 3), (STEPS, 3), (STEPS,), (STEPS,), (STEPS,), (7,),
     ]
     return pl.pallas_call(
         backward_kernel,
@@ -1534,17 +1580,19 @@
 
 def closing_kernel(*refs):
     (
-        proj, ranks, mixer_w, left, own, grad_middle, gain, down, gain_two_grad, heads, early, ups, gates, downs,
+        proj, ranks, mixer_far, left, own, grad_middle, gain, down, gain_two_grad, heads, early, ups, gates, downs,
         out, mixer_grad, merge_grad, pair_grad, down_grad, wide_out, heads_out, gains_out,
-        partial, got, relayed, staged, line, tiles, tiles_got, late_away, late_keep, late_side,
+        mixer_w, partial, got, relayed, staged, line, tiles, tiles_got, late_away, late_keep, late_side,
         late_got, early_got, late_sum, early_sum, late_home, early_home, ups_home, gate_home, down_home,
         wide, wide_got, heads_got, heads_sum, wide_twin, gain_grad, rank_grad,
         send, arrive, twin_send, twin_arrive, here, tile_send, tile_arrive, side_send, side_arrive,
         high_send, high_arrive, home_send, home_arrive,
-        wide_send, wide_arrive, heads_send, heads_arrive, near, out_send, out_arrive, gain_send, gain_arrive,
+        wide_send, wide_arrive, heads_send, heads_arrive, near, out_send, out_arrive, gain_send, gain_arrive, loads,
     ) = refs
     me = Place()
     zh, y, highs = lax.axis_index("zh"), lax.axis_index("y"), lax.axis_size("zh")
+    load = pltpu.make_async_copy(mixer_far, mixer_w, loads.at[0])
+    load.start()
     greet_all(me)
     steps = send.shape[0]
     rows, width = own.shape[0] // steps, own.shape[1]
@@ -1623,6 +1671,7 @@
             partial[k, :, at] = block[k * CHUNK : (k + 1) * CHUNK]
         return 0
 
+    load.wait()
     lax.fori_loop(0, width // TILE, hidden_step, 0)
 
     def part(ref, k, n):
@@ -1837,7 +1886,7 @@
     ]
     tiles = 3 * HD // TILE
     late = (3, highs, 2, owner_rows, HD)
-    scratch = [shape(chunks, CHUNK, width + LANES)]
+    scratch = [shape(*mixer_w.shape), shape(chunks, CHUNK, width + LANES)]
     scratch += [shape(n, rows, width + LANES) for n in (3, 2, 2)] + [shape(rows, width)]
     scratch += [shape(tiles, width // 2, TILE)] * 2 + [shape(*late)] * 3
     scratch += [
@@ -1855,15 +1904,15 @@
         shape(1, width, kind=F32),
         shape(LANES, width, kind=F32),
     ]
-    size = sum(a.size * a.dtype.itemsize for a in arrays + shapes + scratch)
+    size = sum(a.size * a.dtype.itemsize for a in arrays[:2] + arrays[3:] + shapes + scratch)
     sems = [
         (STEPS, 6), (STEPS, 5), (STEPS,), (STEPS,), (STEPS,), (tiles,), (tiles,), (3,), (3,), (4, highs), (4, highs),
-        (7, 2), (7, 2), (chips,), (chips,), (highs * 4,), (highs * 4,), (2,), (3,), (2,), (TEAM,), (TEAM,),
+        (7, 2), (7, 2), (chips,), (chips,), (highs * 4,), (highs * 4,), (2,), (3,), (2,), (TEAM,), (TEAM,), (1,),
     ]
     return pl.pallas_call(
         closing_kernel,
         out_shape=shapes,
-        in_specs=[VMEM] * len(arrays),
+        in_specs=[ANY if n == 2 else VMEM for n in range(len(arrays))],
         out_specs=[VMEM] * len(shapes),
         scratch_shapes=[pltpu.VMEM(a.shape, a.dtype) for a in scratch] + [DMA(n) for n in sems],
         compiler_params=pltpu.CompilerParams(

time: 613 us -> 592 us (0.966)
  Pallas kernels: 575 us -> 554 us
    pallas_call x1, Pallas kernels: 64.2 us -> 50.1 us  [feed_forward(): pl.pallas_call(feed_forward_kernel, out_shape=shapes, in_specs=[VMEM, VME...]
where the time goes in v6:
time: 592 us; the launch traced here: 585 us
  Pallas kernels  554 us (94%)
  local copies, waits for them, and re-layouts  25.8 us (4%)
    pallas_call x1, Pallas kernels, forward(): pl.pallas_call(forward_kernel, out_shape=[a for a, _ in shapes], in_specs...  246 us
    pallas_call x1, Pallas kernels, backward(): pl.pallas_call(backward_kernel, out_shape=shapes, in_specs=[ANY if n in a...  135 us
    pallas_call x1, Pallas kernels, closing(): pl.pallas_call(closing_kernel, out_shape=shapes, in_specs=[ANY if n == 2...  123 us
    pallas_call x1, Pallas kernels, feed_forward(): pl.pallas_call(feed_forward_kernel, out_shape=shapes, in_specs=[VMEM, VME...  50.1 us
  transfers between devices with their start and end apart: 1, of which 0 were waited for; matrix products, arithmetic and copies ran while one was open for 2% of the time, Pallas kernels for 51%

profile of v6, /device:TPU:0, one launch (start us, length us, event | category | flops | bytes accessed | tf_op | source)
XLA Modules:
  0.0 585.4 jit_solution(5590984549328827908)
XLA Ops:
  0.7 0.8 fusion.5
  2.0 0.8 dynamic_slice.13
  2.8 1.9 constant_dynamic-slice_fusion.refs_7_.refs_2_
  4.7 1.9 constant_dynamic-slice_fusion.1.refs_6_.refs_4_
  6.8 1.1 copy.28
  7.9 0.8 copy.27
  8.8 0.7 maximum_maximum_fusion.refs_5_
  9.5 0.6 fusion.4.refs_4_
  10.1 0.7 broadcast_in_dim.19.refs_9_.refs_21_
  10.8 0.6 broadcast_in_dim.18.refs_8_.refs_20_
  11.4 245.8 %forward.1 = (bf16[2,2,2,2,128,2048]{5,4,3,2,1,0:T(8,128)(2,1)}, bf16[2,2,2,2,128,512]{5,4,3,2,1,0:T(8,128)(2,1)}, bf16[2,2,2,2,128,2816]{5,4,3,2,1,0:T(8,128)(2...) custom-call(bf16[4,128,1024]{2,1,0:T(8,128)(2,1)} %refs_0_.1, ...), custom_call_target="tpu_custom_call" | custom-call | tf_op jit(solution)/shard_map/forward/pallas_call | solution.py:952
  257.2 1.5 fusion.6
  258.7 0.9 slice.50
  259.7 0.8 pad.20.refs_7_
  260.5 50.1 %feed_forward.1 = (bf16[4,128,2048]{2,1,0:T(8,128)(2,1)}, bf16[4,128,2048]{2,1,0:T(8,128)(2,1)}, bf16[512,2816]{1,0:T(8,128)(2,1)}, bf16[512,2816]{1,0:T(8,128)(2,1)}, bf16[512,1408]{1,0:T(8,128)(2,1)}) custom-call(bf16[4,128,2048]{2,1,0:T(8,128)(2,1)} %get-tuple-element.53.hidden, bf16[4,128,2048]{2,1,0:T(8,128)(2,1)} %get-tuple-element.54.cots, ...), custom_call_target="tpu_custom_call" | custom-call | tf_op jit(solution)/shard_map/feed_forward/pallas_call | solution.py:1180
  310.7 0.7 pad.19.refs_17_
  311.3 134.7 %backward.1 = (f32[128,2048]{1,0:T(8,128)}, f32[1,2048]{1,0:T(1,128)}, bf16[4,128,2048]{2,1,0:T(8,128)(2,1)}, bf16[4,128,128]{2,1,0:T(8,128)(2,1)}, f32[24,512]{...) custom-call(bf16[4,128,2048]{2,1,0:T(8,128)(2,1)} %get-tuple-element, ...), custom_call_target="tpu_custom_call" | custom-call | tf_op jit(solution)/shard_map/backward/pallas_call | solution.py:1566
  446.1 123.5 %closing.1 = (bf16[2,128,2048]{2,1,0:T(8,128)(2,1)}, f32[4,128,1024]{2,1,0:T(8,128)}, f32[1024,128]{1,0:T(8,128)}, f32[2,128,2816]{2,1,0:T(8,128)}, f32[2816,128...) custom-call(bf16[4,128,2048]{2,1,0:T(8,128)(2,1)} %get-tuple-element.75.refs_0_, ...), custom_call_target="tpu_custom_call" | custom-call | tf_op jit(solution)/shard_map/closing/pallas_call | solution.py:1912
  569.6 0.9 slice_bitcast_fusion
  570.5 1.4 slice.40
  571.9 1.3 slice_bitcast_fusion.1
  573.2 1.3 slice_bitcast_fusion.2
  574.4 0.6 copy.30
  575.1 1.4 slice_reduce_fusion
  576.5 1.0 copy.37
  577.5 1.0 copy.38
  578.5 1.3 copy.39
  579.9 0.8 copy.40
  580.7 0.8 copy-done
  581.5 1.6 copy.41
  583.0 0.8 copy-done.2
  583.9 1.1 copy.42
  (33 shorter events, 1.0 us)
Async XLA Ops:
  0.6 5.9 %copy-start.12 = (s32[13]{0:T(128)S(1)}, s32[13]{0:T(128)}, u32[]{:S(2)}) copy-start(s32[13]{0:T(128)} %param.15) | copy-start | bytes 160
  0.7 6.1 %copy-start.5 = (bf16[2816,128]{1,0:T(8,128)(2,1)S(1)}, bf16[2816,128]{1,0:T(8,128)(2,1)}, u32[]{:S(2)}) copy-start(bf16[2816,128]{1,0:T(8,128)(2,1)} %param.25) | copy-start | bytes 2162692
  0.7 7.2 %copy-start.7 = (bf16[1024,128]{1,0:T(8,128)(2,1)S(1)}, bf16[1024,128]{1,0:T(8,128)(2,1)}, u32[]{:S(2)}) copy-start(bf16[1024,128]{1,0:T(8,128)(2,1)} %param.23) | copy-start | bytes 786436
  1.5 8.0 %copy-start.9 = (bf16[128,16]{0,1:T(8,128)(2,1)S(1)}, bf16[128,16]{0,1:T(8,128)(2,1)}, u32[]{:S(2)}) copy-start(bf16[128,16]{0,1:T(8,128)(2,1)} %param.19) | copy-start | bytes 12292
  1.5 8.0 %copy-start.10 = (bf16[128]{0:T(256)(128)(2,1)S(1)}, bf16[128]{0:T(256)(128)(2,1)}, u32[]{:S(2)}) copy-start(bf16[128]{0:T(256)(128)(2,1)} %param.17) | copy-start | bytes 772
  1.5 8.0 %copy-start.11 = (bf16[128]{0:T(256)(128)(2,1)S(1)}, bf16[128]{0:T(256)(128)(2,1)}, u32[]{:S(2)}) copy-start(bf16[128]{0:T(256)(128)(2,1)} %param.16) | copy-start | bytes 772
  1.5 309.1 %collective-permute-start = (bf16[16,512]{1,0:T(8,128)(2,1)S(1)}, bf16[16,512]{1,0:T(8,128)(2,1)S(1)}, u32[]{:S(2)}, u32[]{:S(2)}) collective-permute-start(bf16[16,512]{1,0:T(8,128)(2,1)S(1)} %get-tuple-element.94), channel_id=1, source_target_pairs={{0,1},{1,0},{2,3},{3,2},{4,5},{5,4},{6,7},{7,6},{8,9},{9,8},{10,11... | collective-permute-start | bytes 49160 | tf_op jit(solution)/shard_map/ppermute | solution.py:1962
  260.5 50.1 %copy-start.8 = (bf16[16,1024]{1,0:T(8,128)(2,1)S(1)}, bf16[16,1024]{1,0:T(8,128)(2,1)}, u32[]{:S(2)}) copy-start(bf16[16,1024]{1,0:T(8,128)(2,1)} %param.20) | copy-start | bytes 98308
  446.1 130.4 %copy-start.3 = (bf16[2,128,2048]{2,1,0:T(8,128)(2,1)S(1)}, bf16[2,128,2048]{2,1,0:T(8,128)(2,1)}, u32[]{:S(2)}) copy-start(bf16[2,128,2048]{2,1,0:T(8,128)(2,1)} %get-tuple-element.74) | copy-start | bytes 3145732
  569.6 7.9 %copy-start.4 = (bf16[2,128,2048]{2,1,0:T(8,128)(2,1)S(1)}, bf16[2,128,2048]{2,1,0:T(8,128)(2,1)}, u32[]{:S(2)}) copy-start(bf16[2,128,2048]{2,1,0:T(8,128)(2,1)} %get-tuple-element.86) | copy-start | bytes 3145732
  576.5 2.0 copy-start.1
  578.5 1.4 copy-start.6
  578.5 2.9 copy-start
  581.5 2.4 copy-start.2

commit v7 on v6

--- a/solution.py
+++ b/solution.py
@@ -48,6 +48,10 @@
     def __init__(self):
         self.zl, self.x, self.c = lax.axis_index("zl"), lax.axis_index("x"), lax.axis_index("c")
         self.member = self.zl * 2 + self.x
+
+    def half(self, ref):
+        rows = ref.shape[0] // 2
+        return ref.at[pl.ds(pl.multiple_of(self.c * rows, rows), rows)]
 
 
 def greet_team(me, more=0):
@@ -575,17 +579,18 @@
 
 def forward_kernel(*refs):
     (
-        mixer_in, mixer_out, ffn_in, ffn_out, small, ups, own, cot, starts_row, starts_column, head_gain,
-        mixer_w, merge_w, pair_w, down_w, gains, cots, hidden, low_rank, gate, cumulated, projected, mixed, gated,
-        befores, decay, second, middle,
-        mixer_v, merge_v, projected_v, updates, inputs, smalls, ups_got, state, partial, got, relayed, staged, line,
+        mixer_in, mixer_out, ffn_in, ffn_out, small, ups, tokens, cotangent, starts_row, starts_column, head_gain,
+        mixer_w, merge_w, pair_w, down_w, gains, cots, hidden_far, low_rank, gate_far, cumulated_far, projected, mixed_far,
+        gated_far, befores_far, decay, second, middle_far,
+        hidden, gate, cumulated, mixed, gated, befores, middle, mixer_v, merge_v, projected_v, updates, inputs, smalls, ups_got, state, partial, got, relayed, staged, line,
         own_send, own_arrive, far_send, arrive, small_send, small_arrive, ups_sem, inputs_send, inputs_arrive,
         cot_send, cot_arrive, sum_send, sum_arrive, spread_send, spread_arrive, saves,
     ) = refs[:-STATE_REFS]
     me = Place()
+    own, cot = me.half(tokens), me.half(cotangent)
     zh, y, highs = lax.axis_index("zh"), lax.axis_index("y"), lax.axis_size("zh")
     units = down_w.shape[-1]
-    width = own.shape[1]
+    width = tokens.shape[1]
     chunks = hidden.shape[0]
     first = ((zh * 2 + me.c) * 2 + y) * (chunks * CHUNK)
     greet_all(me)
@@ -722,6 +727,9 @@
         return 0
 
     lax.fori_loop(0, chunks, gates_step, 0)
+    save(hidden, hidden_far)
+    save(gate, gate_far)
+    save(cumulated, cumulated_far)
 
     def project(part):
         rows = hidden[...].reshape(chunks * CHUNK, width)
@@ -762,11 +770,11 @@
     states.begin()
     pass_high(0)
     states.combine()
-    held = [copy for part in (5, 6, 7) for copy in own_high(part, False)]
+    held = [own_high(part, False) for part in (5, 6, 7)]
 
     @pl.when(me.zl == 1)
     def _():
-        for copy in held:
+        for copy in sum(held, []):
             copy.start()
 
     pass_high(3)
@@ -790,7 +798,7 @@
 
     @pl.when(me.zl == 0)
     def _():
-        for copy in held:
+        for copy in sum(held[:1], []):
             copy.start()
 
     pass_high(4)
@@ -815,6 +823,9 @@
         return 0
 
     lax.fori_loop(0, chunks, outer_step, 0)
+    save(mixed, mixed_far)
+    save(gated, gated_far)
+    save(befores, befores_far)
     pass_side(4)
     complete(4)
 
@@ -825,7 +836,7 @@
     lax.fori_loop(0, chunks, merge_step, 0)
 
     steps = sum_send.shape[0]
-    rows = own.shape[0] // steps
+    rows = tokens.shape[0] // 2 // steps
 
     def rows_of(ref, k, n):
         return ref.at[k, pl.ds(n * rows, rows)]
@@ -856,7 +867,6 @@
         transfer.start()
     for transfer in sums:
         transfer.relay()
-    pass_high(5)
     for n in range(steps):
         at = pl.ds(n * rows, rows)
         total = own[at].astype(F32) + sums[n].total()
@@ -867,9 +877,16 @@
         if n:
             spreads[n - 1].relay()
     spreads[steps - 1].relay()
+    @pl.when(me.zl == 0)
+    def _():
+        for copy in sum(held[1:], []):
+            copy.start()
+
+    pass_high(5)
     pass_high(6)
     pass_side(5)
     move_cot.start()
+    save(middle, middle_far)
     save(mixer_v, mixer_w)
     save(merge_v, merge_w)
     pass_high(7)
@@ -897,10 +914,10 @@
     return jnp.broadcast_to(starts[None], (8, LANES)), jnp.broadcast_to(starts[:16, None], (16, LANES))
 
 
-def forward(mixer_in, mixer_out, ffn_in, ffn_out, small, ups, own, cot, starts, head_gain):
+def forward(mixer_in, mixer_out, ffn_in, ffn_out, small, ups, tokens, cotangent, starts, head_gain):
     highs = lax.axis_size("zh")
     chips = highs * 8
-    rows, half, width = small.shape[1], own.shape[0], own.shape[1]
+    rows, half, width = small.shape[1], tokens.shape[0] // 2, tokens.shape[1]
     units = ffn_out.shape[1] // 2
     chunks = TEAM * half // CHUNK
 
@@ -914,20 +931,21 @@
         (shape(highs, 2, 2, 2, rows, units), ANY),
         (shape(RANKS, width, kind=F32), VMEM),
         (shape(TEAM, half, width), ANY),
-        (shape(chunks, CHUNK, width), VMEM),
+        (shape(chunks, CHUNK, width), ANY),
         (shape(chunks, CHUNK, RANKS), VMEM),
-        (shape(chunks, CHUNK, HD, kind=F32), VMEM),
-        (shape(chunks, CHUNK, HD, kind=F32), VMEM),
+        (shape(chunks, CHUNK, HD, kind=F32), ANY),
+        (shape(chunks, CHUNK, HD, kind=F32), ANY),
         (shape(4, chunks, CHUNK, HD, kind=F32), ANY),
-        (shape(chunks, CHUNK, HD, kind=F32), VMEM),
-        (shape(chunks, CHUNK, HD), VMEM),
-        (shape(chunks, HD, HD), VMEM),
+        (shape(chunks, CHUNK, HD, kind=F32), ANY),
+        (shape(chunks, CHUNK, HD), ANY),
+        (shape(chunks, HD, HD), ANY),
         (shape(8, HD, kind=F32), VMEM),
-        (shape(TEAM, half, width), VMEM),
-        (shape(half, width, kind=F32), VMEM),
-    ]
-    arrays = [mixer_in, mixer_out, ffn_in, ffn_out, small, ups, own, cot, *starts_arrays(starts), head_gain]
-    scratch = [
+        (shape(TEAM, half, width), ANY),
+        (shape(half, width, kind=F32), ANY),
+    ]
+    arrays = [mixer_in, mixer_out, ffn_in, ffn_out, small, ups, tokens, cotangent, *starts_arrays(starts), head_gain]
+    scratch = [shapes[n][0] for n in (6, 8, 9, 11, 12, 13, 16)]
+    scratch += [
         shapes[0][0],
         shapes[1][0],
         shapes[10][0],
@@ -947,7 +965,7 @@
     forwards = 8 * ((highs - 1) + highs + 2 * highs)
     sems = [
         (8, 2), (8, 2), (forwards,), (highs, 2, 2, 8), (chips,), (chips,), (2,), (5,), (4,), (3,), (4,),
-        (STEPS, 6), (STEPS, 5), (STEPS, 3), (STEPS, 4), (7,),
+        (STEPS, 6), (STEPS, 5), (STEPS, 3), (STEPS, 4), (14,),
     ]
     return pl.pallas_call(
         forward_kernel,
@@ -1204,7 +1222,7 @@
 
 def backward_kernel(*refs):
     (
-        back, forth, cot, middle, gain, pair_away, pair_keep_far, downs, merge_far, gated, projected_far, mixed_far,
+        back, forth, cotangent, middle, gain, pair_away, pair_keep_far, downs, merge_far, gated, projected_far, mixed_far,
         cumulated_far, gate_far, befores_far, decay, low_rank, up_pad, head_gain, hidden, starts_row, starts_column,
         grad_middle, gain_grad, proj, ranks, heads, early, gate_sum, up_sum, down_sum, left_hidden,
         result, got, relayed, staged, line, got2, relayed2, staged2, line2, branch, left_branch, douts, tiles, tiles_got,
@@ -1213,6 +1231,7 @@
         send3, arrive3, twin_send, twin_arrive, here, loads,
     ) = refs[:-STATE_REFS]
     me = Place()
+    cot = me.half(cotangent)
     zh, y, highs = lax.axis_index("zh"), lax.axis_index("y"), lax.axis_size("zh")
     chunks, _, width = hidden.shape
     units = downs.shape[-1]
@@ -1277,7 +1296,7 @@
     high_start(0)
 
     steps = send.shape[0]
-    rows = cot.shape[0] // steps
+    rows = cotangent.shape[0] // 2 // steps
 
     def part(ref, k, n):
         return ref.at[k, pl.ds(n * rows, rows)]
@@ -1507,7 +1526,7 @@
     low_rank, up_pad, head_gain, hidden, starts,
 ):
     highs, members, owner_rows, units = downs.shape
-    rows, width = cot.shape
+    rows, width = cot.shape[0] // 2, cot.shape[1]
     chunks = hidden.shape[0]
 
     def shape(*dims, kind=BF):
@@ -1580,7 +1599,7 @@
 
 def closing_kernel(*refs):
     (
-        proj, ranks, mixer_far, left, own, grad_middle, gain, down, gain_two_grad, heads, early, ups, gates, downs,
+        proj, ranks, mixer_far, left, tokens, grad_middle, gain, down, gain_two_grad, heads, early, ups, gates, downs,
         out, mixer_grad, merge_grad, pair_grad, down_grad, wide_out, heads_out, gains_out,
         mixer_w, partial, got, relayed, staged, line, tiles, tiles_got, late_away, late_keep, late_side,
         late_got, early_got, late_sum, early_sum, late_home, early_home, ups_home, gate_home, down_home,
@@ -1590,12 +1609,13 @@
         wide_send, wide_arrive, heads_send, heads_arrive, near, out_send, out_arrive, gain_send, gain_arrive, loads,
     ) = refs
     me = Place()
+    own = me.half(tokens)
     zh, y, highs = lax.axis_index("zh"), lax.axis_index("y"), lax.axis_size("zh")
     load = pltpu.make_async_copy(mixer_far, mixer_w, loads.at[0])
     load.start()
     greet_all(me)
     steps = send.shape[0]
-    rows, width = own.shape[0] // steps, own.shape[1]
+    rows, width = tokens.shape[0] // 2 // steps, tokens.shape[1]
     chunks = proj.shape[0]
     twin = {"c": 1 - me.c}
 
@@ -1862,7 +1882,7 @@
 
 
 def closing(proj, ranks, mixer_w, left, own, grad_middle, gain, down, gain_two_grad, heads, early, ups, gates, downs):
-    rows, width = own.shape
+    rows, width = own.shape[0] // 2, own.shape[1]
     chunks = proj.shape[0]
     highs, _, owner_rows, _ = early.shape
     units = ups.shape[-1]
@@ -1950,14 +1970,12 @@
     up_head = lax.dynamic_slice_in_dim(decay_up, HD * x, HD, 1).astype(F32)
     bias_head = lax.dynamic_slice_in_dim(decay_bias, HD * x, HD, 0)
     ups = jnp.concatenate([up_head, bias_head[None], jnp.zeros((7, HD), F32)], axis=0)
-    own = lax.dynamic_slice_in_dim(tokens, half * c, half, 0)
-    own_dy = lax.dynamic_slice_in_dim(cotangent, half * c, half, 0)
     starts = jnp.cumsum(lengths) - lengths
     (
         mixer_w, merge_w, pair_w, down_w, gains, ffn_dy, hidden_one, low_rank, gate_input, cumulated, projected,
         mixed, gated, befores, decay, hidden_two, middle,
     ) = forward(
-        mixer_in, mixer_out.T, ffn_in, ffn_out.T, small, ups, own, own_dy, starts, head_gain[None]
+        mixer_in, mixer_out.T, ffn_in, ffn_out.T, small, ups, tokens, cotangent, starts, head_gain[None]
     )
     up_head = jnp.where(c == zl, up_head, lax.ppermute(up_head, "c", CROSS)).astype(BF)
     mixer_w, merge_w = mixer_w.reshape(width, 4 * HD), merge_w.reshape(width, HD)
@@ -1972,12 +1990,12 @@
         grad_middle, grad_gain_two, grad_proj, grad_ranks, heads, early, gate_sum, up_sum, down_sum,
         left_hidden, result,
     ) = backward(
-        back, forth, own_dy, middle, gain_two, pair_sides, down_part, merge_w, gated, projected, mixed, cumulated,
+        back, forth, cotangent, middle, gain_two, pair_sides, down_part, merge_w, gated, projected, mixed, cumulated,
         gate_input, befores, decay, low_rank, jnp.pad(up_head, pad_rank), head_gain[None], hidden_one, starts,
     )
     early = early.reshape(highs, 2, rows, 2 * HD)
     grad_inputs, mixer_home, merge_home, pair_home, down_home, wide, heads, gains = closing(
-        grad_proj, grad_ranks, mixer_w, left_hidden, own, grad_middle, gain_one, jnp.pad(rank_down, pad_rank),
+        grad_proj, grad_ranks, mixer_w, left_hidden, tokens, grad_middle, gain_one, jnp.pad(rank_down, pad_rank),
         grad_gain_two, heads, early, up_sum, gate_sum, down_sum,
     )
     return (

time: 592 us -> 583 us (0.985)
  Pallas kernels: 554 us -> 545 us
    unnamed x35 -> x29, local copies, waits for them, and re-layouts: 11.4 us -> 13.4 us
where the time goes in v7:
time: 583 us; the launch traced here: 576 us
  Pallas kernels  545 us (93%)
  local copies, waits for them, and re-layouts  24.1 us (4%)
    pallas_call x1, Pallas kernels, forward(): pl.pallas_call(forward_kernel, out_shape=[a for a, _ in shapes], in_specs...  241 us
    pallas_call x1, Pallas kernels, backward(): pl.pallas_call(backward_kernel, out_shape=shapes, in_specs=[ANY if n in a...  132 us
    pallas_call x1, Pallas kernels, closing(): pl.pallas_call(closing_kernel, out_shape=shapes, in_specs=[ANY if n == 2...  123 us
    pallas_call x1, Pallas kernels, feed_forward(): pl.pallas_call(feed_forward_kernel, out_shape=shapes, in_specs=[VMEM, VME...  50.2 us
    unnamed x29, local copies, waits for them, and re-layouts  13.4 us
  transfers between devices with their start and end apart: 1, of which 0 were waited for; matrix products, arithmetic and copies ran while one was open for 2% of the time, Pallas kernels for 51%

profile of v7, /device:TPU:0, one launch (start us, length us, event | category | flops | bytes accessed | tf_op | source)
XLA Modules:
  0.0 575.7 jit_solution(3188348758269635565)
XLA Ops:
  0.7 0.7 fusion.5
  1.9 0.8 dynamic_slice.7
  2.6 0.8 reduce-window.9
  3.5 0.7 bitcast_subtract_fusion
  4.1 2.2 copy.28
  6.4 1.8 copy.27
  8.2 0.7 maximum_maximum_fusion.refs_5_
  8.9 0.6 fusion.4.refs_4_
  9.6 0.7 broadcast_in_dim.19.refs_9_.refs_21_
  10.2 0.6 broadcast_in_dim.18.refs_8_.refs_20_
  10.8 240.5 %forward.1 = (bf16[2,2,2,2,128,2048]{5,4,3,2,1,0:T(8,128)(2,1)}, bf16[2,2,2,2,128,512]{5,4,3,2,1,0:T(8,128)(2,1)}, bf16[2,2,2,2,128,2816]{5,4,3,2,1,0:T(8,128)(2...) custom-call(bf16[4,128,1024]{2,1,0:T(8,128)(2,1)} %refs_0_.1, ...), custom_call_target="tpu_custom_call" | custom-call | tf_op jit(solution)/shard_map/forward/pallas_call | solution.py:970
  251.4 1.5 fusion.6
  252.9 0.9 slice.50
  253.8 0.8 pad.20.refs_7_
  254.7 50.2 %feed_forward.1 = (bf16[4,128,2048]{2,1,0:T(8,128)(2,1)}, bf16[4,128,2048]{2,1,0:T(8,128)(2,1)}, bf16[512,2816]{1,0:T(8,128)(2,1)}, bf16[512,2816]{1,0:T(8,128)(2,1)}, bf16[512,1408]{1,0:T(8,128)(2,1)}) custom-call(bf16[4,128,2048]{2,1,0:T(8,128)(2,1)} %get-tuple-element.53.hidden, bf16[4,128,2048]{2,1,0:T(8,128)(2,1)} %get-tuple-element.54.cots, ...), custom_call_target="tpu_custom_call" | custom-call | tf_op jit(solution)/shard_map/feed_forward/pallas_call | solution.py:1198
  304.9 0.7 pad.19.refs_17_
  305.6 131.5 %backward.1 = (f32[128,2048]{1,0:T(8,128)}, f32[1,2048]{1,0:T(1,128)}, bf16[4,128,2048]{2,1,0:T(8,128)(2,1)}, bf16[4,128,128]{2,1,0:T(8,128)(2,1)}, f32[24,512]{...) custom-call(bf16[4,128,2048]{2,1,0:T(8,128)(2,1)} %get-tuple-element, ...), custom_call_target="tpu_custom_call" | custom-call | tf_op jit(solution)/shard_map/backward/pallas_call | solution.py:1585
  437.1 122.7 %closing.1 = (bf16[2,128,2048]{2,1,0:T(8,128)(2,1)}, f32[4,128,1024]{2,1,0:T(8,128)}, f32[1024,128]{1,0:T(8,128)}, f32[2,128,2816]{2,1,0:T(8,128)}, f32[2816,128...) custom-call(bf16[4,128,2048]{2,1,0:T(8,128)(2,1)} %get-tuple-element.75.refs_0_, ...), custom_call_target="tpu_custom_call" | custom-call | tf_op jit(solution)/shard_map/closing/pallas_call | solution.py:1932
  559.9 0.9 slice_bitcast_fusion
  560.8 1.4 slice.40
  562.2 1.3 slice_bitcast_fusion.1
  563.5 1.3 slice_bitcast_fusion.2
  564.7 0.6 copy.30
  565.4 1.4 slice_reduce_fusion
  566.8 1.0 copy.37
  567.8 1.0 copy.38
  568.8 1.3 copy.39
  570.2 0.8 copy.40
  571.0 0.8 copy-done
  571.8 1.6 copy.41
  573.3 0.8 copy-done.2
  574.2 1.1 copy.42
  (25 shorter events, 0.7 us)
Async XLA Ops:
  0.6 8.3 %copy-start.9 = (bf16[128]{0:T(256)(128)(2,1)S(1)}, bf16[128]{0:T(256)(128)(2,1)}, u32[]{:S(2)}) copy-start(bf16[128]{0:T(256)(128)(2,1)} %param.16) | copy-start | bytes 772
  0.7 8.3 %copy-start.8 = (bf16[128]{0:T(256)(128)(2,1)S(1)}, bf16[128]{0:T(256)(128)(2,1)}, u32[]{:S(2)}) copy-start(bf16[128]{0:T(256)(128)(2,1)} %param.17) | copy-start | bytes 772
  0.7 8.3 %copy-start.7 = (bf16[128,16]{0,1:T(8,128)(2,1)S(1)}, bf16[128,16]{0,1:T(8,128)(2,1)}, u32[]{:S(2)}) copy-start(bf16[128,16]{0,1:T(8,128)(2,1)} %param.19) | copy-start | bytes 12292
  1.4 303.5 %collective-permute-start = (bf16[16,512]{1,0:T(8,128)(2,1)S(1)}, bf16[16,512]{1,0:T(8,128)(2,1)S(1)}, u32[]{:S(2)}, u32[]{:S(2)}) collective-permute-start(bf16[16,512]{1,0:T(8,128)(2,1)S(1)} %get-tuple-element.94), channel_id=1, source_target_pairs={{0,1},{1,0},{2,3},{3,2},{4,5},{5,4},{6,7},{7,6},{8,9},{9,8},{10,11... | collective-permute-start | bytes 49160 | tf_op jit(solution)/shard_map/ppermute | solution.py:1980
  254.7 50.2 %copy-start.6 = (bf16[16,1024]{1,0:T(8,128)(2,1)S(1)}, bf16[16,1024]{1,0:T(8,128)(2,1)}, u32[]{:S(2)}) copy-start(bf16[16,1024]{1,0:T(8,128)(2,1)} %param.20) | copy-start | bytes 98308
  437.1 129.7 %copy-start.3 = (bf16[2,128,2048]{2,1,0:T(8,128)(2,1)S(1)}, bf16[2,128,2048]{2,1,0:T(8,128)(2,1)}, u32[]{:S(2)}) copy-start(bf16[2,128,2048]{2,1,0:T(8,128)(2,1)} %get-tuple-element.74) | copy-start | bytes 3145732
  559.9 7.9 %copy-start.4 = (bf16[2,128,2048]{2,1,0:T(8,128)(2,1)S(1)}, bf16[2,128,2048]{2,1,0:T(8,128)(2,1)}, u32[]{:S(2)}) copy-start(bf16[2,128,2048]{2,1,0:T(8,128)(2,1)} %get-tuple-element.86) | copy-start | bytes 3145732
  566.8 2.0 copy-start.1
  568.8 1.4 copy-start.5
  568.8 2.9 copy-start
  571.8 2.4 copy-start.2

commit v8 on v7

--- a/solution.py
+++ b/solution.py
@@ -1741,6 +1741,18 @@
         for move in high_moves[j]:
             move.start()
 
+    def high_add(kind, source, target, total):
+        for k in range(1, highs):
+            wait_for(target.at[k - 1], high_arrive.at[kind, k])
+        for m in range(2):
+            add_rows(total.at[m], source.at[0, m], *(target.at[k - 1, m] for k in range(1, highs)))
+        homes[kind].start()
+
+
+    high_add(3, early, early_got, early_sum)
+    for j in range(3):
+        high_add(j, late_side.at[j], late_got.at[j], late_sum.at[j])
+
     def twin_copy(n):
         return copy_to(
             line.at[pl.ds(n * rows, rows)], part(out, me.c, n), twin_send.at[n], twin_arrive.at[n], twin
@@ -1780,14 +1792,6 @@
         route_all(me), lambda k: wide.at[k], lambda k: wide_got.at[k], wide_send, wide_arrive
     )
     spreads.start()
-    def high_add(kind, source, target, total):
-        for k in range(1, highs):
-            wait_for(target.at[k - 1], high_arrive.at[kind, k])
-        for m in range(2):
-            add_rows(total.at[m], source.at[0, m], *(target.at[k - 1, m] for k in range(1, highs)))
-        homes[kind].start()
-
-
     heads_move.wait()
     total = heads_got[0]
     for n in range(1, highs * 4):
@@ -1843,7 +1847,6 @@
     spread_columns(gate_home, pair_grad.at[0], units)
     homes[4].wait()
     spread_columns(ups_home, pair_grad.at[1], units)
-    high_add(3, early, early_got, early_sum)
     for k in range(2):
         own_slot = (me.c == me.zl) & (me.x == k)
         unless(own_slot, lambda k=k: wait_for(heads_out.at[k], out_arrive.at[k]))
@@ -1856,8 +1859,6 @@
     swap.wait()
     wide_out[...] = wide_out[...] + wide_twin[...]
     gains.wait()
-    for j in range(3):
-        high_add(j, late_side.at[j], late_got.at[j], late_sum.at[j])
     homes[3].wait()
     spread_rows(early_home, merge_grad, HD)
     for k in range(2):

time: 583 us -> 579 us (level)
  no operation moved by 1% of the time
where the time goes in v8:
time: 579 us; the launch traced here: 571 us
  Pallas kernels  540 us (93%)
  local copies, waits for them, and re-layouts  24.1 us (4%)
    pallas_call x1, Pallas kernels, forward(): pl.pallas_call(forward_kernel, out_shape=[a for a, _ in shapes], in_specs...  241 us
    pallas_call x1, Pallas kernels, backward(): pl.pallas_call(backward_kernel, out_shape=shapes, in_specs=[ANY if n in a...  132 us
    pallas_call x1, Pallas kernels, closing(): pl.pallas_call(closing_kernel, out_shape=shapes, in_specs=[ANY if n == 2...  118 us
    pallas_call x1, Pallas kernels, feed_forward(): pl.pallas_call(feed_forward_kernel, out_shape=shapes, in_specs=[VMEM, VME...  50.2 us
    unnamed x29, local copies, waits for them, and re-layouts  13.4 us
  transfers between devices with their start and end apart: 1, of which 0 were waited for; matrix products, arithmetic and copies ran while one was open for 2% of the time, Pallas kernels for 51%

profile of v8, /device:TPU:0, one launch (start us, length us, event | category | flops | bytes accessed | tf_op | source)
XLA Modules:
  0.0 571.2 jit_solution(3162723267002150701)
XLA Ops:
  0.7 0.7 fusion.5
  1.9 0.8 dynamic_slice.7
  2.6 0.8 reduce-window.9
  3.5 0.7 bitcast_subtract_fusion
  4.1 2.2 copy.28
  6.4 1.8 copy.27
  8.2 0.7 maximum_maximum_fusion.refs_5_
  8.9 0.6 fusion.4.refs_4_
  9.6 0.7 broadcast_in_dim.19.refs_9_.refs_21_
  10.2 0.6 broadcast_in_dim.18.refs_8_.refs_20_
  10.8 240.5 %forward.1 = (bf16[2,2,2,2,128,2048]{5,4,3,2,1,0:T(8,128)(2,1)}, bf16[2,2,2,2,128,512]{5,4,3,2,1,0:T(8,128)(2,1)}, bf16[2,2,2,2,128,2816]{5,4,3,2,1,0:T(8,128)(2...) custom-call(bf16[4,128,1024]{2,1,0:T(8,128)(2,1)} %refs_0_.1, ...), custom_call_target="tpu_custom_call" | custom-call | tf_op jit(solution)/shard_map/forward/pallas_call | solution.py:970
  251.4 1.5 fusion.6
  252.9 0.9 slice.50
  253.8 0.8 pad.20.refs_7_
  254.7 50.2 %feed_forward.1 = (bf16[4,128,2048]{2,1,0:T(8,128)(2,1)}, bf16[4,128,2048]{2,1,0:T(8,128)(2,1)}, bf16[512,2816]{1,0:T(8,128)(2,1)}, bf16[512,2816]{1,0:T(8,128)(2,1)}, bf16[512,1408]{1,0:T(8,128)(2,1)}) custom-call(bf16[4,128,2048]{2,1,0:T(8,128)(2,1)} %get-tuple-element.53.hidden, bf16[4,128,2048]{2,1,0:T(8,128)(2,1)} %get-tuple-element.54.cots, ...), custom_call_target="tpu_custom_call" | custom-call | tf_op jit(solution)/shard_map/feed_forward/pallas_call | solution.py:1198
  304.9 0.7 pad.19.refs_17_
  305.6 131.5 %backward.1 = (f32[128,2048]{1,0:T(8,128)}, f32[1,2048]{1,0:T(1,128)}, bf16[4,128,2048]{2,1,0:T(8,128)(2,1)}, bf16[4,128,128]{2,1,0:T(8,128)(2,1)}, f32[24,512]{...) custom-call(bf16[4,128,2048]{2,1,0:T(8,128)(2,1)} %get-tuple-element, ...), custom_call_target="tpu_custom_call" | custom-call | tf_op jit(solution)/shard_map/backward/pallas_call | solution.py:1585
  437.1 118.2 %closing.1 = (bf16[2,128,2048]{2,1,0:T(8,128)(2,1)}, f32[4,128,1024]{2,1,0:T(8,128)}, f32[1024,128]{1,0:T(8,128)}, f32[2,128,2816]{2,1,0:T(8,128)}, f32[2816,128...) custom-call(bf16[4,128,2048]{2,1,0:T(8,128)(2,1)} %get-tuple-element.75.refs_0_, ...), custom_call_target="tpu_custom_call" | custom-call | tf_op jit(solution)/shard_map/closing/pallas_call | solution.py:1933
  555.3 0.9 slice_bitcast_fusion
  556.3 1.4 slice.40
  557.6 1.3 slice_bitcast_fusion.1
  558.9 1.3 slice_bitcast_fusion.2
  560.2 0.6 copy.30
  560.8 1.4 slice_reduce_fusion
  562.3 1.0 copy.37
  563.2 1.0 copy.38
  564.3 1.3 copy.39
  565.6 0.8 copy.40
  566.4 0.8 copy-done
  567.2 1.6 copy.41
  568.8 0.8 copy-done.2
  569.6 1.1 copy.42
  (25 shorter events, 0.7 us)
Async XLA Ops:
  0.6 8.3 %copy-start.9 = (bf16[128]{0:T(256)(128)(2,1)S(1)}, bf16[128]{0:T(256)(128)(2,1)}, u32[]{:S(2)}) copy-start(bf16[128]{0:T(256)(128)(2,1)} %param.16) | copy-start | bytes 772
  0.7 8.3 %copy-start.8 = (bf16[128]{0:T(256)(128)(2,1)S(1)}, bf16[128]{0:T(256)(128)(2,1)}, u32[]{:S(2)}) copy-start(bf16[128]{0:T(256)(128)(2,1)} %param.17) | copy-start | bytes 772
  0.7 8.3 %copy-start.7 = (bf16[128,16]{0,1:T(8,128)(2,1)S(1)}, bf16[128,16]{0,1:T(8,128)(2,1)}, u32[]{:S(2)}) copy-start(bf16[128,16]{0,1:T(8,128)(2,1)} %param.19) | copy-start | bytes 12292
  1.4 303.5 %collective-permute-start = (bf16[16,512]{1,0:T(8,128)(2,1)S(1)}, bf16[16,512]{1,0:T(8,128)(2,1)S(1)}, u32[]{:S(2)}, u32[]{:S(2)}) collective-permute-start(bf16[16,512]{1,0:T(8,128)(2,1)S(1)} %get-tuple-element.94), channel_id=1, source_target_pairs={{0,1},{1,0},{2,3},{3,2},{4,5},{5,4},{6,7},{7,6},{8,9},{9,8},{10,11... | collective-permute-start | bytes 49160 | tf_op jit(solution)/shard_map/ppermute | solution.py:1981
  254.7 50.2 %copy-start.6 = (bf16[16,1024]{1,0:T(8,128)(2,1)S(1)}, bf16[16,1024]{1,0:T(8,128)(2,1)}, u32[]{:S(2)}) copy-start(bf16[16,1024]{1,0:T(8,128)(2,1)} %param.20) | copy-start | bytes 98308
  437.1 125.1 %copy-start.3 = (bf16[2,128,2048]{2,1,0:T(8,128)(2,1)S(1)}, bf16[2,128,2048]{2,1,0:T(8,128)(2,1)}, u32[]{:S(2)}) copy-start(bf16[2,128,2048]{2,1,0:T(8,128)(2,1)} %get-tuple-element.74) | copy-start | bytes 3145732
  555.3 7.9 %copy-start.4 = (bf16[2,128,2048]{2,1,0:T(8,128)(2,1)S(1)}, bf16[2,128,2048]{2,1,0:T(8,128)(2,1)}, u32[]{:S(2)}) copy-start(bf16[2,128,2048]{2,1,0:T(8,128)(2,1)} %get-tuple-element.86) | copy-start | bytes 3145732
  562.3 2.0 copy-start.1
  564.3 1.4 copy-start.5
  564.3 2.9 copy-start
  567.2 2.4 copy-start.2
